TPU v7x, 128 devices: a whole 4x4x4 slice. The times are simulated.
128 devices in a mesh: dp: 4 (over z_lo, core), ctx: 32 (over y, z_hi, x).
Axes of the slice: x: 4, y: 4, z: 4 (z_hi: 2, z_lo: 2; z = z_hi * 2 + z_lo), core: 2. Of those that a mesh axis runs over, the one named last changes fastest.
Arguments:
- tokens: bfloat16 [4, 2048, 2, 1536], P('dp', 'ctx'), may hold values from -6 to 6
- cotangent: bfloat16 [4, 2048, 2, 1536], P('dp', 'ctx'), may hold values from -6 to 6
- w_qkv: bfloat16 [1536, 2048], P(('dp', 'ctx')), may hold values from -0.15625 to 0.15625
- b_qkv: bfloat16 [2048], replicated, may hold values from -3 to 3
- w_out: bfloat16 [1536, 1536], P(('dp', 'ctx')), may hold values from -0.625 to 0.625
- w_gu: bfloat16 [1536, 2, 8960], P(('dp', 'ctx')), may hold values from -0.15625 to 0.15625
- w_down: bfloat16 [8960, 1536], P(('dp', 'ctx')), may hold values from -0.0625 to 0.0625
- gain_attn: bfloat16 [1536], replicated, may hold values from 0.099609375 to 1.8984375
- gain_mlp: bfloat16 [1536], replicated, may hold values from 0.099609375 to 1.8984375
- adapt_in: bfloat16 [8, 6, 16, 1536], replicated, may hold values from -0.15625 to 0.15625
- adapt_in_ff: bfloat16 [8, 16, 8960], replicated, may hold values from -0.0625 to 0.0625
- adapt_out_qkv: bfloat16 [8, 16, 2048], replicated, may hold values from -0.75 to 0.75
- adapt_out_res: bfloat16 [8, 2, 16, 1536], replicated, may hold values from -0.75 to 0.75
- adapt_out_ff: bfloat16 [8, 2, 16, 8960], replicated, may hold values from -0.75 to 0.75
- doc_lengths: int32 [4, 8], P('dp'), may hold values from 1 to 2048, 4096 in all within a row
- adapter_index: int32 [4], P('dp'), may hold values from 0 to 7
- window: int32 [4], P('dp'), may hold values from 512 to 1024, as said below
Outputs:
- layer_out: bfloat16 [4, 2048, 2, 1536], P('dp', 'ctx')
- grad_tokens: bfloat16 [4, 2048, 2, 1536], P('dp', 'ctx')
- grad_adapt_in: float32 [8, 6, 16, 1536], replicated
- grad_adapt_in_ff: float32 [8, 16, 8960], replicated
- grad_adapt_out_qkv: float32 [8, 16, 2048], replicated
- grad_adapt_out_res: float32 [8, 2, 16, 1536], replicated
- grad_adapt_out_ff: float32 [8, 2, 16, 8960], replicated
Inputs may be any that keep to these rules, and one draw needn't show every extreme that they name: `doc_lengths`: a sequence's document lengths sum to 4096, and one document of every sequence has exactly 2048 tokens. Some sequence has a window of exactly 1024.
All inputs are finite; a program needn't handle non-finite values.
Results may differ from a plain program's by a relative error of at most 0.029.
Values may be sent and summed in bfloat16 or wider, within the bound.
A program may use at most 448 MiB of HBM per device.

v0:
```python
import jax
import jax.numpy as jnp
from jax import lax
from jax.sharding import PartitionSpec as P

D = 1536
QUERY_HEADS = 12
VALUE_HEADS = 2
HEAD_SIZE = 128
ADAPT = 8
WINDOW_LIMIT = 1024


rope_base = 1000000.0
norm_eps = 1e-06


def side_by_side(arrays, axis, dim, along):
    ends, at = ([], 0)
    for a in arrays[:-1]:
        at += a.shape[along]
        ends.append(at)
    both = jnp.concatenate(arrays, axis=along)
    return tuple(jnp.split(lax.all_gather(both, axis, axis=dim, tiled=True), ends, axis=along))


def rms_norm(values, scaling):
    return values * lax.rsqrt(jnp.mean(values * values, -1, keepdims=True) + norm_eps) * scaling


def rotary_embedding(values, token_position):
    frequency = rope_base ** (-(2.0 * jnp.arange(HEAD_SIZE // 2, dtype=jnp.float32)) / HEAD_SIZE)
    angles = token_position.astype(jnp.float32)[:, None] * frequency[None, :]
    cosine = jnp.concatenate([jnp.cos(angles), jnp.cos(angles)], -1)[:, None, :]
    sine_part = jnp.concatenate([jnp.sin(angles), jnp.sin(angles)], -1)[:, None, :]
    halfway = HEAD_SIZE // 2
    turned = jnp.concatenate([-values[..., halfway:], values[..., :halfway]], -1)
    return values * cosine + turned * sine_part


def precise(left_side, right_side):
    return jnp.dot(left_side, right_side, precision=lax.Precision.HIGHEST)


def swish_product(gate_up):
    return jax.nn.silu(gate_up[:, 0]) * gate_up[:, 1]


def natural_order(dealt_rows, count):
    first_half = dealt_rows[:, 0]
    second = (
        dealt_rows[:, 1].reshape((count, -1) + dealt_rows.shape[2:])[::-1].reshape(first_half.shape)
    )
    return jnp.concatenate([first_half, second], 0)


def dealt_order(natural, count):
    half_len = natural.shape[0] // 2
    first_half = natural[:half_len]
    second = (
        natural[half_len:].reshape((count, -1) + natural.shape[1:])[::-1].reshape(first_half.shape)
    )
    return jnp.stack([first_half, second], 1)


def local(
    tokens,
    cotangent,
    w_qkv,
    b_qkv,
    w_out,
    w_gu,
    w_down,
    gain_attn,
    gain_mlp,
    adapt_in,
    adapt_in_ff,
    adapt_out_qkv,
    adapt_out_res,
    adapt_out_ff,
    doc_lengths,
    adapter_index,
    window,
):
    n_ctx = lax.axis_size("ctx")
    member = lax.axis_index("ctx")
    block_length = tokens.shape[1]
    count_of_rows = 2 * block_length
    query_width = QUERY_HEADS * HEAD_SIZE
    key_value_width = VALUE_HEADS * HEAD_SIZE
    query_group_width = QUERY_HEADS // VALUE_HEADS
    key_range_length = WINDOW_LIMIT + block_length
    score_scale = HEAD_SIZE ** (-0.5)
    chosen = adapter_index[0]
    window_len = window[0]
    doc_ends = jnp.cumsum(doc_lengths[0])
    offsets = jnp.arange(block_length, dtype=jnp.int32)
    block_starts = jnp.stack([member * block_length, (2 * n_ctx - 1 - member) * block_length])
    query_pos = block_starts[:, None] + offsets[None, :]
    token_position = jnp.transpose(query_pos).reshape(count_of_rows)
    key_pos = (
        block_starts[:, None]
        - WINDOW_LIMIT
        + jnp.arange(key_range_length, dtype=jnp.int32)[None, :]
    )

    def doc_index(places):
        return jnp.sum((places[..., None] >= doc_ends).astype(jnp.int32), -1)

    distance = query_pos[:, :, None] - key_pos[:, None, :]
    allowed = (distance >= 0) & (distance < window_len) & (key_pos[:, None, :] >= 0)
    allowed = allowed & (doc_index(query_pos)[:, :, None] == doc_index(key_pos)[:, None, :])
    allowed = allowed[:, None, None]
    adapter_in = lax.dynamic_index_in_dim(adapt_in, chosen, 0, keepdims=False)
    adapter_ff_low = lax.dynamic_index_in_dim(adapt_in_ff, chosen, 0, keepdims=False)
    adapter_ff = adapter_ff_low.astype(jnp.float32)
    in_float = adapter_in.astype(jnp.float32)
    out_qkv_low = lax.dynamic_index_in_dim(adapt_out_qkv, chosen, 0, keepdims=False)
    out_res_low = lax.dynamic_index_in_dim(adapt_out_res, chosen, 0, keepdims=False)
    out_ff_low = lax.dynamic_index_in_dim(adapt_out_ff, chosen, 0, keepdims=False)
    out_qkv = out_qkv_low.astype(jnp.float32)
    out_res = out_res_low.astype(jnp.float32)
    out_ff = out_ff_low.astype(jnp.float32)
    inputs = tokens[0].reshape(count_of_rows, D).astype(jnp.float32)
    attn_full, out_full = side_by_side((w_qkv, w_out), ("dp", "ctx"), 0, 1)
    normed = rms_norm(inputs, gain_attn.astype(jnp.float32)).astype(jnp.bfloat16)
    low_rank = jnp.einsum("td,krd->tkr", normed, adapter_in[:3], preferred_element_type=jnp.float32)
    adapter_terms = jnp.concatenate(
        [
            precise(low_rank[:, 0], out_qkv[:, :query_width]),
            precise(low_rank[:, 1], out_qkv[:, query_width : query_width + key_value_width]),
            precise(low_rank[:, 2], out_qkv[:, query_width + key_value_width :]),
        ],
        1,
    )
    joined_heads = (
        jnp.dot(normed, attn_full, preferred_element_type=jnp.float32)
        + b_qkv.astype(jnp.float32)
        + adapter_terms
    )
    query_pre = joined_heads[:, :query_width].reshape(count_of_rows, QUERY_HEADS, HEAD_SIZE)
    unrotated_keys = joined_heads[:, query_width : query_width + key_value_width].reshape(
        count_of_rows, VALUE_HEADS, HEAD_SIZE
    )
    query_rows = rotary_embedding(query_pre, token_position).astype(jnp.bfloat16)
    rows_of_keys = (
        rotary_embedding(unrotated_keys, token_position)
        .astype(jnp.bfloat16)
        .reshape(count_of_rows, key_value_width)
    )
    rows_of_values = joined_heads[:, query_width + key_value_width :].astype(jnp.bfloat16)
    kv_local = jnp.concatenate([rows_of_keys, rows_of_values], 1).reshape(
        block_length, 2, 2 * key_value_width
    )
    kv_all = lax.all_gather(kv_local, "ctx", axis=0, tiled=True)
    natural = natural_order(kv_all, n_ctx)
    padded = jnp.concatenate(
        [jnp.zeros((WINDOW_LIMIT, 2 * key_value_width), jnp.bfloat16), natural], 0
    )
    neighbour_block = jnp.stack(
        [
            lax.dynamic_slice_in_dim(padded, block_starts[0], key_range_length, 0),
            lax.dynamic_slice_in_dim(padded, block_starts[1], key_range_length, 0),
        ],
        0,
    )
    key_near = neighbour_block[..., :key_value_width].reshape(
        2, key_range_length, VALUE_HEADS, HEAD_SIZE
    )
    value_near = neighbour_block[..., key_value_width:].reshape(
        2, key_range_length, VALUE_HEADS, HEAD_SIZE
    )
    blocks_of_queries = query_rows.reshape(
        block_length, 2, VALUE_HEADS, query_group_width, HEAD_SIZE
    )

    def score_rows(key_block):
        raw_scores = (
            jnp.einsum(
                "ihagd,hkad->hagik",
                blocks_of_queries,
                key_block,
                preferred_element_type=jnp.float32,
            )
            * score_scale
        )
        return jnp.where(allowed, raw_scores, -1e30)

    masked = score_rows(key_near)
    row_peak = jnp.max(masked, -1, keepdims=True)
    exponent = jnp.exp(masked - row_peak)
    row_total = jnp.sum(exponent, -1, keepdims=True)
    log_total = row_peak + jnp.log(row_total)
    attended = jnp.einsum(
        "hagik,hkad->ihagd",
        (exponent / row_total).astype(jnp.bfloat16),
        value_near,
        preferred_element_type=jnp.float32,
    )
    mixed_heads = attended.reshape(count_of_rows, query_width).astype(jnp.bfloat16)
    out_rank = jnp.einsum(
        "tq,rq->tr", mixed_heads, adapter_in[3], preferred_element_type=jnp.float32
    )
    branch = jnp.dot(mixed_heads, out_full, preferred_element_type=jnp.float32) + precise(
        out_rank, out_res[0]
    )
    hidden = inputs + branch
    mlp_full, down_full = (
        lax.all_gather(w_gu, ("dp", "ctx"), axis=0, tiled=True),
        lax.all_gather(w_down, ("dp", "ctx"), axis=0, tiled=True),
    )
    normed_mlp = rms_norm(hidden, gain_mlp.astype(jnp.float32)).astype(jnp.bfloat16)
    mlp_rank = jnp.einsum(
        "td,krd->tkr", normed_mlp, adapter_in[4:], preferred_element_type=jnp.float32
    )
    gate_up = jnp.einsum(
        "td,dsf->tsf", normed_mlp, mlp_full, preferred_element_type=jnp.float32
    ) + jnp.einsum("tkr,krf->tkf", mlp_rank, out_ff, precision=lax.Precision.HIGHEST)
    active, act_back = jax.vjp(swish_product, gate_up)
    active = active.astype(jnp.bfloat16)
    down_rank = jnp.einsum("tf,rf->tr", active, adapter_ff_low, preferred_element_type=jnp.float32)
    result = jnp.dot(active, down_full, preferred_element_type=jnp.float32) + precise(
        down_rank, out_res[1]
    )
    layer_out = hidden + result
    grad_low = cotangent[0].reshape(count_of_rows, D)
    grad_out = grad_low.astype(jnp.float32)
    mlp_back, down_back = (mlp_full, down_full)
    grad_down_rank = jnp.einsum(
        "td,rd->tr", grad_low, out_res_low[1], preferred_element_type=jnp.float32
    )
    grad_active = jnp.einsum(
        "td,fd->tf", grad_low, down_back, preferred_element_type=jnp.float32
    ) + precise(grad_down_rank, adapter_ff)
    grad_res_down = precise(down_rank.T, grad_out)
    grad_in_ff = precise(grad_down_rank.T, active.astype(jnp.float32))
    grad_gate_up = act_back(grad_active)[0].astype(jnp.bfloat16)
    grad_gu_float = grad_gate_up.astype(jnp.float32)
    grad_mlp_rank = jnp.einsum(
        "tsf,srf->tsr", grad_gate_up, out_ff_low, preferred_element_type=jnp.float32
    )
    grad_normed_mlp = jnp.einsum(
        "tsf,dsf->td", grad_gate_up, mlp_back, preferred_element_type=jnp.float32
    ) + jnp.einsum("tsr,srd->td", grad_mlp_rank, in_float[4:], precision=lax.Precision.HIGHEST)
    grad_out_ff = jnp.einsum(
        "tsr,tsf->srf", mlp_rank, grad_gu_float, precision=lax.Precision.HIGHEST
    )
    grad_in_gu = jnp.einsum(
        "tsr,td->srd",
        grad_mlp_rank,
        normed_mlp.astype(jnp.float32),
        precision=lax.Precision.HIGHEST,
    )
    _, norm_back_mlp = jax.vjp(rms_norm, hidden, gain_mlp.astype(jnp.float32))
    grad_hidden = grad_out + norm_back_mlp(grad_normed_mlp)[0]
    grad_low_hidden = grad_hidden.astype(jnp.bfloat16)
    grad_hidden_float = grad_low_hidden.astype(jnp.float32)
    attn_back, out_back = (attn_full, out_full)
    key_back, value_back = (key_near, value_near)
    grad_out_rank = jnp.einsum(
        "td,rd->tr", grad_low_hidden, out_res_low[0], preferred_element_type=jnp.float32
    )
    mixed_gradient = jnp.einsum(
        "td,qd->tq", grad_low_hidden, out_back, preferred_element_type=jnp.float32
    ) + precise(grad_out_rank, in_float[3])
    grad_res_out = precise(out_rank.T, grad_hidden_float)
    grad_in_out = precise(grad_out_rank.T, mixed_heads.astype(jnp.float32))
    head_gradient = mixed_gradient.astype(jnp.bfloat16).reshape(
        block_length, 2, VALUE_HEADS, query_group_width, HEAD_SIZE
    )
    masked_again = score_rows(key_back)
    probabilities = jnp.where(allowed, jnp.exp(masked_again - log_total), 0.0)
    grad_probs = jnp.einsum(
        "ihagd,hkad->hagik", head_gradient, value_back, preferred_element_type=jnp.float32
    )
    row_delta = jnp.sum(probabilities * grad_probs, -1, keepdims=True)
    grad_scores = (probabilities * (grad_probs - row_delta)).astype(jnp.bfloat16)
    grad_query = (
        jnp.einsum("hagik,hkad->ihagd", grad_scores, key_back, preferred_element_type=jnp.float32)
        * score_scale
    )
    grad_keys = (
        jnp.einsum(
            "hagik,ihagd->hkad", grad_scores, blocks_of_queries, preferred_element_type=jnp.float32
        )
        * score_scale
    )
    grad_values = jnp.einsum(
        "hagik,ihagd->hkad",
        probabilities.astype(jnp.bfloat16),
        head_gradient,
        preferred_element_type=jnp.float32,
    )
    near_grads = jnp.concatenate(
        [
            grad_keys.reshape(2, key_range_length, key_value_width),
            grad_values.reshape(2, key_range_length, key_value_width),
        ],
        -1,
    )
    seq_len = 2 * block_length * n_ctx
    buffer = jnp.zeros((WINDOW_LIMIT + seq_len, 2 * key_value_width), jnp.float32)
    for which_half in range(2):
        current = lax.dynamic_slice_in_dim(buffer, block_starts[which_half], key_range_length, 0)
        buffer = lax.dynamic_update_slice_in_dim(
            buffer, current + near_grads[which_half], block_starts[which_half], 0
        )
    local_gradients = (
        lax.psum_scatter(
            dealt_order(buffer[WINDOW_LIMIT:], n_ctx).astype(jnp.bfloat16),
            "ctx",
            scatter_dimension=0,
            tiled=True,
        )
        .astype(jnp.float32)
        .reshape(count_of_rows, 2 * key_value_width)
    )

    def turn_rows(values):
        return rotary_embedding(values, token_position)

    _, rope_back_query = jax.vjp(turn_rows, query_pre)
    _, rotary_key_backward = jax.vjp(turn_rows, unrotated_keys)
    grad_query_pre = rope_back_query(grad_query.reshape(count_of_rows, QUERY_HEADS, HEAD_SIZE))[
        0
    ].reshape(count_of_rows, query_width)
    unrotated_key_gradient = rotary_key_backward(
        local_gradients[:, :key_value_width].reshape(count_of_rows, VALUE_HEADS, HEAD_SIZE)
    )[0].reshape(count_of_rows, key_value_width)
    grad_joined = jnp.concatenate(
        [grad_query_pre, unrotated_key_gradient, local_gradients[:, key_value_width:]], 1
    ).astype(jnp.bfloat16)
    grad_joined_float = grad_joined.astype(jnp.float32)
    query_part = grad_joined_float[:, :query_width]
    key_part = grad_joined_float[:, query_width : query_width + key_value_width]
    value_part = grad_joined_float[:, query_width + key_value_width :]
    grad_rank = jnp.stack(
        [
            jnp.einsum(
                "tc,rc->tr",
                grad_joined[:, :query_width],
                out_qkv_low[:, :query_width],
                preferred_element_type=jnp.float32,
            ),
            jnp.einsum(
                "tc,rc->tr",
                grad_joined[:, query_width : query_width + key_value_width],
                out_qkv_low[:, query_width : query_width + key_value_width],
                preferred_element_type=jnp.float32,
            ),
            jnp.einsum(
                "tc,rc->tr",
                grad_joined[:, query_width + key_value_width :],
                out_qkv_low[:, query_width + key_value_width :],
                preferred_element_type=jnp.float32,
            ),
        ],
        1,
    )
    grad_normed = jnp.einsum(
        "tc,dc->td", grad_joined, attn_back, preferred_element_type=jnp.float32
    ) + jnp.einsum("tkr,krd->td", grad_rank, in_float[:3], precision=lax.Precision.HIGHEST)
    grad_out_qkv = jnp.concatenate(
        [
            precise(low_rank[:, 0].T, query_part),
            precise(low_rank[:, 1].T, key_part),
            precise(low_rank[:, 2].T, value_part),
        ],
        1,
    )
    grad_in_qkv = jnp.einsum(
        "tkr,td->krd", grad_rank, normed.astype(jnp.float32), precision=lax.Precision.HIGHEST
    )
    _, norm_back_attn = jax.vjp(rms_norm, inputs, gain_attn.astype(jnp.float32))
    grad_inputs = grad_hidden + norm_back_attn(grad_normed)[0]
    grad_in_all = jnp.concatenate([grad_in_qkv, grad_in_out[None], grad_in_gu], 0)
    grad_res_all = jnp.stack([grad_res_out, grad_res_down], 0)
    one_hot = (jnp.arange(ADAPT, dtype=jnp.int32) == chosen).astype(jnp.float32)

    def spread_slot(local_grad):
        return one_hot.reshape((ADAPT,) + (1,) * local_grad.ndim) * local_grad[None]

    summed = lax.psum(
        (
            spread_slot(grad_in_all),
            spread_slot(grad_in_ff),
            spread_slot(grad_out_qkv),
            spread_slot(grad_res_all),
            spread_slot(grad_out_ff),
        ),
        ("dp", "ctx"),
    )
    shape_out = (1, block_length, 2, D)
    return (
        layer_out.astype(jnp.bfloat16).reshape(shape_out),
        grad_inputs.astype(jnp.bfloat16).reshape(shape_out),
        summed[0],
        summed[1],
        summed[2],
        summed[3],
        summed[4],
    )


def solution(mesh):
    return jax.shard_map(
        local,
        mesh=mesh,
        in_specs=(
            P("dp", "ctx", None, None),
            P("dp", "ctx", None, None),
            P(("dp", "ctx"), None),
            P(),
            P(("dp", "ctx"), None),
            P(("dp", "ctx"), None, None),
            P(("dp", "ctx"), None),
            P(),
            P(),
            P(),
            P(),
            P(),
            P(),
            P(),
            P("dp", None),
            P("dp"),
            P("dp"),
        ),
        out_specs=(P("dp", "ctx", None, None), P("dp", "ctx", None, None), P(), P(), P(), P(), P()),
        check_vma=False,
    )
```

profile of v0, /device:TPU:1, one launch (start us, length us, event | category | flops | bytes accessed | tf_op | source)
XLA Modules:
  0.0 1792.2 jit_solution(13509283335603846816)
XLA Ops:
  25.4 312.9 %all-gather.11.cloned.1.call-done = bf16[128,12,3584]{2,1,0:T(8,128)(2,1)} async-done(((bf16[1,12,3584]{2,1,0:T(8,128)(2,1)}), bf16[128,12,3584]{2,1,0:T(8,128)(2,1)}) %all-gather.11.cloned.1.call-update) | async-done | bytes 11010064 | tf_op jit(solution)/shard_map/all_gather | solution.py:24
  338.2 17.1 reshape.394
  386.0 58.1 %all-gather.7.cloned.1.call-done = bf16[2048,2,512]{2,0,1:T(8,128)(2,1)} async-done(((bf16[64,2,512]{2,0,1:T(8,128)(2,1)}), bf16[2048,2,512]{2,0,1:T(8,128)(2,1)}) %all-gather.7.cloned.1.call-update) | async-done | bytes 4194320 | tf_op jit(solution)/shard_map/all_gather | solution.py:155
  451.7 5.2 pad_maximum_fusion
  480.4 306.5 %all-gather.13.cloned.1.call-done = bf16[128,70,1536]{2,1,0:T(8,128)(2,1)} async-done(((bf16[1,70,1536]{2,1,0:T(8,128)(2,1)}), bf16[128,70,1536]{2,1,0:T(8,128)(2,1)}) %all-gather.13.cloned.1.call-update) | async-done | bytes 27525136 | tf_op jit(solution)/shard_map/all_gather | solution.py:210
  786.9 34.0 %reshape.396 = bf16[8960,1536]{1,0:T(8,128)(2,1)} reshape(bf16[128,70,1536]{2,1,0:T(8,128)(2,1)} %all-gather.13.cloned.1.call-done) | data formatting | bytes 55050240
  820.9 16.5 fusion.149
  837.4 326.4 %all-gather.9.cloned.1.call-done = bf16[1536,2,8960]{2,1,0:T(2,128)(2,1)} async-done(((bf16[12,2,8960]{2,1,0:T(2,128)(2,1)}), bf16[1536,2,8960]{2,1,0:T(2,128)(2,1)}) %all-gather.9.cloned.1.call-update) | async-done | bytes 55050256 | tf_op jit(solution)/shard_map/all_gather | solution.py:209
  1163.7 32.1 %fusion.2 = f32[128,2,8960]{2,0,1:T(8,128)} fusion(bf16[128,1536,1]{1,0,2:T(8,128)(2,1)} %copy-done.21, bf16[1536,2,8960]{2,1,0:T(2,128)(2,1)} %all-gather.9.cloned.1.call-done), kind=kOutput, calls=%fused_computation.2 | convolution fusion | flops 7046430720 | bytes 64618496 | tf_op jit(solution)/shard_map/td,dsf->tsf/dot_general | solution.py:216
  1195.9 8.0 fusion.4
  1203.9 6.9 multiply_bitcast_fusion
  1216.8 26.6 %fusion.46 = f32[128,1536]{1,0:T(8,128)S(1)} fusion(bf16[1536,2,8960]{2,1,0:T(2,128)(2,1)} %all-gather.9.cloned.1.call-done, f32[128,1,8960]{2,0,1:T(8,128)} %copy-done.3, f32[128,1,8960]{2,0,1:T(8,128)} %copy-done.2), kind=kOutput, calls=%fused_computation.69 | convolution fusion | flops 7051018240 | bytes 65011712 | tf_op jit(solution)/shard_map/tsf,dsf->td/dot_general | solution.py:242
  1253.0 6.7 fusion.31
  1283.2 5.3 broadcast_in_dim.43
  1288.5 11.2 dynamic_update_slice.6
  1304.1 12.0 dynamic_update_slice.7
  1316.2 6.2 fusion.141
  1344.7 6.0 fusion.61
  1366.7 141.6 %reduce-scatter.2.cloned.1.call-done = bf16[64,2,512]{2,0,1:T(8,128)(2,1)} async-done(((bf16[2048,2,512]{2,0,1:T(8,128)(2,1)}), bf16[64,2,512]{2,0,1:T(8,128)(2,1)}) %reduce-scatter.2.cloned.1.call-update) | async-done | bytes 131088 | tf_op jit(solution)/shard_map/reduce_scatter | solution.py:309
  1523.1 11.6 fusion.148
  1540.9 5.4 multiply_reduce_fusion
  1547.5 221.4 %all-reduce.9.cloned.1.call-done = (f32[8,6,16,1536]{3,2,1,0:T(8,128)}, f32[8,16,8960]{2,1,0:T(8,128)}, f32[8,16,2048]{2,1,0:T(8,128)}, f32[8,2,16,1536]{3,2,1,0:T(8,128)}, f32[8,2,16,8960]{3,2,1,0:T(8,128)}) async-done(((f32[8,6,16,1536]{3,2,1,0:T(8,128)}, f32[8,16,8960]{2,1,0:T(8,128)}, f32[8,16,2048]{2,1,0:T(8,128)}, f32[8,2,16,1536]{3,2,1,0:T(8,128)}, f32[8,2,16,8960]{3,2,1,0:T(8,128)}), ...) | async-done | bytes 21102608 | tf_op jit(solution)/shard_map/psum | solution.py:383
  1768.9 5.5 copy.194
  1774.4 4.9 copy.195
  (316 shorter events, 187.3 us)
Async XLA Ops:
  7.2 15.9 copy-start
  7.2 331.0 %all-gather.11.cloned.1.call-start = ((), (), s32[]{:S(2)}) async-start(), calls=%async_computation.4 | async-start | bytes 14794752 | tf_op jit(solution)/shard_map/all_gather | solution.py:24
  8.9 435.2 %all-gather.7.cloned.1.call-start = ((), (), s32[]{:S(2)}) async-start(), calls=%async_computation.1 | async-start | bytes 4325376 | tf_op jit(solution)/shard_map/all_gather | solution.py:155
  10.3 345.0 %copy-start.48 = (f32[1536]{0:T(1024)}, f32[1536]{0:T(1024)S(1)}, u32[]{:S(2)}) copy-start(f32[1536]{0:T(1024)S(1)} %convert_element_type.136) | copy-start | bytes 18436
  14.6 340.8 %copy-start.7 = (f32[128,1536]{1,0:T(8,128)}, f32[128,1536]{1,0:T(8,128)S(1)}, u32[]{:S(2)}) copy-start(f32[128,1536]{1,0:T(8,128)S(1)} %reshape.390) | copy-start | bytes 2359300
  362.7 424.2 %all-gather.13.cloned.1.call-start = ((), (), s32[]{:S(2)}) async-start(), calls=%async_computation.5 | async-start | bytes 28532736 | tf_op jit(solution)/shard_map/all_gather | solution.py:210
  363.5 800.3 %all-gather.9.cloned.1.call-start = ((), (), s32[]{:S(2)}) async-start(), calls=%async_computation.2 | async-start | bytes 55480320 | tf_op jit(solution)/shard_map/all_gather | solution.py:209
  364.0 1144.3 %reduce-scatter.2.cloned.1.call-start = ((), (), s32[]{:S(2)}) async-start(), calls=%async_computation.3 | async-start | bytes 4325376 | tf_op jit(solution)/shard_map/reduce_scatter | solution.py:309
  386.0 77.4 %copy-start.23 = (bf16[64,2,2,6,128]{4,3,2,1,0:T(8,128)(2,1)}, bf16[64,2,2,6,128]{4,3,2,1,0:T(8,128)(2,1)S(1)}, u32[]{:S(2)}) copy-start(bf16[64,2,2,6,128]{4,3,2,1,0:T(8,128)(2,1)S(1)} %fusion.68) | copy-start | bytes 1179652
  480.4 715.5 %copy-start.40 = (f32[128,2,16]{0,2,1:T(8,128)}, f32[128,2,16]{0,2,1:T(8,128)S(1)}, u32[]{:S(2)}) copy-start(f32[128,2,16]{0,2,1:T(8,128)S(1)} %fusion.98) | copy-start | bytes 49156
  1216.8 26.7 %copy-start.50 = (f32[1536]{0:T(1024)S(1)}, f32[1536]{0:T(1024)}, u32[]{:S(2)}) copy-start(f32[1536]{0:T(1024)} %convert_element_type.151) | copy-start | bytes 18436
  1216.8 27.4 %copy-start.70 = (f32[128]{0:T(128)S(1)}, f32[128]{0:T(128)}, u32[]{:S(2)}) copy-start(f32[128]{0:T(128)} %copy-done.69) | copy-start | bytes 1540
  1216.8 27.4 %copy-start.64 = (f32[128]{0:T(128)S(1)}, f32[128]{0:T(128)}, u32[]{:S(2)}) copy-start(f32[128]{0:T(128)} %copy-done.63) | copy-start | bytes 1540
  1253.0 11.3 slice-start
  1338.0 431.0 %all-reduce.9.cloned.1.call-start = ((), (), s32[]{:S(2)}) async-start(), calls=%async_computation.6 | async-start | bytes 42205184 | tf_op jit(solution)/shard_map/psum | solution.py:383
  1342.6 12.6 slice-start.2
  1342.6 12.6 slice-start.4
  1362.1 150.4 %copy-start.29 = (f32[128,128]{1,0:T(8,128)S(1)}, f32[128,128]{1,0:T(8,128)}, u32[]{:S(2)}) copy-start(f32[128,128]{1,0:T(8,128)} %get-tuple-element.52) | copy-start | bytes 196612
  1362.1 150.7 %copy-start.33 = (f32[128,128]{1,0:T(8,128)S(1)}, f32[128,128]{1,0:T(8,128)}, u32[]{:S(2)}) copy-start(f32[128,128]{1,0:T(8,128)} %get-tuple-element.51) | copy-start | bytes 196612
  1362.1 155.5 %copy-start.45 = (f32[128,1,16]{0,2,1:T(8,128)S(1)}, f32[128,1,16]{0,2,1:T(8,128)}, u32[]{:S(2)}) copy-start(f32[128,1,16]{0,2,1:T(8,128)} %convolution_bitcast_fusion.10) | copy-start | bytes 24580
  1523.0 11.7 copy-start.56
  1523.1 17.8 copy-start.20
  1768.9 12.5 slice-start.6
  1768.9 12.5 slice-start.7
  (62 other events, 304.8 us)
Sparse Core Ops, SparseCore 0:
  10.3 327.8 all-gather.10
  362.8 81.1 all-gather.6
  445.8 341.0 all-gather.12
  788.5 375.2 all-gather.8
  1338.1 170.2 reduce-scatter.1
  1523.2 245.7 all-reduce.8
where the time goes:
time: 1800 us; the launch traced here: 1790 us
  waiting for transfers between devices  1370 us (76%)
  matrix products  174 us (10%)
  local copies, waits for them, and re-layouts  168 us (9%)
  other arithmetic  64.5 us (4%)
    all_gather x1, waiting for transfers between devices, local(): lax.all_gather(w_gu, ('dp', 'ctx'), axis=0, tiled=True)  326 us
    all_gather x1, waiting for transfers between devices, side_by_side(): lax.all_gather(both, axis, axis=dim, tiled=True)  313 us
    all_gather x1, waiting for transfers between devices, local(): lax.all_gather(w_down, ('dp', 'ctx'), axis=0, tiled=True)  307 us
    psum x1, waiting for transfers between devices, local(): lax.psum((spread_slot(grad_in_all), spread_slot(grad_in_ff), spread_slot(...  221 us
    reduce_scatter x1, waiting for transfers between devices, local(): lax.psum_scatter(dealt_order(buffer[WINDOW_LIMIT:], n_ctx).astype(jnp.bfl...  142 us
    unnamed x168, local copies, waits for them, and re-layouts  76.8 us
    all_gather x1, waiting for transfers between devices, local(): kv_all = lax.all_gather(kv_local, 'ctx', axis=0, tiled=True)  58.1 us
  transfers between devices with their start and end apart: 6, of which 6 were waited for; matrix products, arithmetic and copies ran while one was open for 10% of the time, Pallas kernels for 0%

commit v1 on v0

v1 whole, which is shorter than its diff:
```python
import functools

import jax
import jax.numpy as jnp
from jax import lax
from jax.experimental import pallas as pl
from jax.experimental.pallas import tpu as pltpu
from jax.sharding import PartitionSpec as P

D = 1536
HEADS = 12
KV_HEADS = 2
HS = 128
GROUP = HEADS // KV_HEADS
FF = 8960
R = 16
ADAPT = 8
BLK = 64
ROWS = 2 * BLK
N_CTX = 32
NBLK = 2 * N_CTX
WIN = 1024
NWB = WIN // BLK + 1
KEYS = NWB * BLK
EXT = 128
DX = D + EXT
FW = 1280
FV = FF // 8
QW = HEADS * HS
KW = KV_HEADS * HS
SCALE = HS**-0.5
EPS = 1e-6

MESH = pl.DeviceIdType.MESH
BF = jnp.bfloat16
F32 = jnp.float32
ANY = pl.BlockSpec(memory_space=pl.ANY)
VM = pl.BlockSpec(memory_space=pltpu.VMEM)
SM = pl.BlockSpec(memory_space=pltpu.SMEM)
DMA = pltpu.SemaphoreType.DMA
VMEM_LIMIT = 60 * 2**20


def sds(shape, dtype):
    return jax.ShapeDtypeStruct(shape, dtype)


def nt(a, b):
    return lax.dot_general(a, b, (((1,), (1,)), ((), ())), preferred_element_type=F32)


def tn(a, b):
    return lax.dot_general(a, b, (((0,), (0,)), ((), ())), preferred_element_type=F32)


def mm(a, b):
    return jnp.dot(a, b, preferred_element_type=F32)


def iota(shape, dim):
    return lax.broadcasted_iota(jnp.int32, shape, dim)


class Place:
    def __init__(self):
        dp, ctx = lax.axis_index("dp"), lax.axis_index("ctx")
        self.dp, self.ctx = dp, ctx
        self.zlo, self.core = lax.div(dp, 2), lax.rem(dp, 2)
        self.y, self.zhi, self.x = lax.div(ctx, 8), lax.rem(lax.div(ctx, 4), 2), lax.rem(ctx, 4)
        self.z = self.zhi * 2 + self.zlo
        self.slice = 2 * dp + self.zhi

    def at(self, x=None, y=None, z=None, core=None):
        x = self.x if x is None else x
        y = self.y if y is None else y
        z = self.z if z is None else z
        core = self.core if core is None else core
        return (lax.rem(z, 2) * 2 + core, y * 8 + lax.div(z, 2) * 4 + x)

    def step(self, axis, by):
        return lax.rem(getattr(self, axis) + by, 4)

    def ring(self, axis):
        return [self.at(**{axis: self.step(axis, k)}) for k in (1, 2, 3)]

    def sibling(self):
        return self.at(core=1 - self.core)


def window_tile(piece):
    return jnp.minimum(lax.div(35 * piece, 4), 60)


def remote(src, dst, send, recv, device):
    return pltpu.make_async_remote_copy(
        src_ref=src, dst_ref=dst, send_sem=send, recv_sem=recv, device_id=device, device_id_type=MESH
    )


def greet(peers):
    sem = pltpu.get_barrier_semaphore()
    for device in peers:
        pl.semaphore_signal(sem, inc=1, device_id=device, device_id_type=MESH)
    pl.semaphore_wait(sem, len(peers))


class Ring:
    def __init__(self, me, axis, own, view, send, recv):
        self.i = getattr(me, axis)
        self.r, self.o, self.l = (me.step(axis, k) for k in (1, 2, 3))
        self.right, self.left = me.at(**{axis: self.r}), me.at(**{axis: self.l})
        self.own, self.view, self.send, self.recv = own, view, send, recv

    def copy(self, k, src, dst, device):
        return remote(src, dst, self.send.at[k], self.recv.at[k], device)

    def first(self):
        place = self.view(self.i, None)
        self.out = [self.copy(0, self.own, place, self.right), self.copy(1, self.own, place, self.left)]
        for c in self.out:
            c.start()

    def second(self):
        v = self.view
        self.copy(0, v(self.l, None), v(self.l, None), self.right).wait_recv()
        c = self.copy(2, v(self.l, 0), v(self.l, 0), self.right)
        c.start()
        self.out.append(c)
        self.copy(1, v(self.r, None), v(self.r, None), self.left).wait_recv()
        c = self.copy(3, v(self.r, 1), v(self.r, 1), self.left)
        c.start()
        self.out.append(c)

    def last(self):
        v = self.view
        self.copy(2, v(self.o, 0), v(self.o, 0), self.right).wait_recv()
        self.copy(3, v(self.o, 1), v(self.o, 1), self.left).wait_recv()

    def sent(self):
        for c in self.out:
            c.wait_send()


class ZGather:
    def __init__(self, me, own, buf, send, recv, core_send, core_recv, half):
        self.me, self.own, self.buf = me, own, buf
        self.cs, self.cr = core_send, core_recv

        def view(j, h, core=me.core):
            ref = buf.at[lax.rem(j, 2), core, lax.div(j, 2)]
            return ref if h is None else ref.at[pl.ds(h * half, half)]

        self.view = view
        self.ring = Ring(me, "z", own, view, send, recv)
        self.out = []

    def swap(self, src, j):
        c = remote(src, self.view(j, None), self.cs.at[len(self.out)], self.cr.at[len(self.out)], self.me.sibling())
        c.start()
        self.out.append((c, j))

    def first(self):
        self.ring.first()
        self.swap(self.own, self.me.z)

    def second(self):
        self.ring.second()
        self.swap(self.view(self.ring.l, None), self.ring.l)
        self.swap(self.view(self.ring.r, None), self.ring.r)

    def last(self):
        self.ring.last()
        self.swap(self.view(self.ring.o, None), self.ring.o)

    def finish(self):
        self.ring.sent()
        for k, (c, j) in enumerate(self.out):
            c.wait_send()
            place = self.view(j, None, 1 - self.me.core)
            remote(place, place, self.cs.at[k], self.cr.at[k], self.me.sibling()).wait_recv()


def rms(z):
    return lax.rsqrt(jnp.mean(z * z, -1, keepdims=True) + EPS)


def prepare_kernel(idx, tok, cot, a_in, b_qkv_ad, b_res, gain, bias, x_o, n1_o, e_o, ub_o, a45_o, bd_o):
    s = lax.axis_index("dp")
    x = tok[...].astype(F32)
    x_o[...] = tok[...]
    n1 = (x * rms(x) * gain[...].astype(F32)).astype(BF)
    n1_o[...] = n1
    for m, (lo, hi) in enumerate(((0, QW), (QW, QW + KW), (QW + KW, QW + 2 * KW))):
        u = nt(n1, a_in[0, m]).astype(BF)
        ub_o[:, lo:hi] = mm(u, b_qkv_ad[0, :, lo:hi]) + bias[:, lo:hi].astype(F32)
    at = pl.multiple_of(s * R, R)
    a45_o[...] = jnp.zeros_like(a45_o)
    a45_o[pl.ds(at, R), :] = a_in[0, 4]
    a45_o[pl.ds(at + 64, R), :] = a_in[0, 5]
    bd_o[...] = jnp.zeros_like(bd_o)
    bd_o[pl.ds(at, R), :] = b_res[0, 1]
    e_o[:, :D] = cot[...]
    e_o[:, D:] = nt(cot[...], bd_o[...]).astype(BF)


def pick(shape):
    return pl.BlockSpec((1,) + shape[1:], lambda i, idx: (idx[0],) + (0,) * (len(shape) - 1))


def whole(shape):
    return pl.BlockSpec(shape, lambda i, idx: (0,) * len(shape))


def prepare(idx, tok, cot, a_in, b_qkv_ad, b_res, gain, bias):
    outs = (
        sds((ROWS, D), BF),
        sds((ROWS, D), BF),
        sds((ROWS, DX), BF),
        sds((ROWS, 2048), F32),
        sds((EXT, D), BF),
        sds((EXT, D), BF),
    )
    return pl.pallas_call(
        prepare_kernel,
        out_shape=outs,
        grid_spec=pltpu.PrefetchScalarGridSpec(
            num_scalar_prefetch=1,
            grid=(1,),
            in_specs=[
                whole((ROWS, D)),
                whole((ROWS, D)),
                pick(a_in.shape),
                pick(b_qkv_ad.shape),
                pick(b_res.shape),
                whole((1, D)),
                whole((1, 2048)),
            ],
            out_specs=[whole(o.shape) for o in outs],
        ),
        compiler_params=pltpu.CompilerParams(vmem_limit_bytes=VMEM_LIMIT),
    )(idx, tok, cot, a_in, b_qkv_ad, b_res, gain, bias)


def weights_kernel(
    idx, wq, wo, wg, wd, eext,
    oq, oo, og, od, oe, oi,
    rq, ro, rg, cq, co, cg,
    ss, rs, ls, s1, r1, s2, r2, sc, rc_, sd, rd, se, re_, ce, cre, si, ri,
):
    me = Place()
    sib = me.sibling()
    zpeers = [
        me.at(z=me.step("z", dz), core=lax.rem(me.core + dc, 2)) for dz in range(4) for dc in range(2) if dz or dc
    ]
    m = me.ctx
    bar = pltpu.get_barrier_semaphore()

    def hello(t, carry):
        @pl.when(t != m)
        def _():
            pl.semaphore_signal(bar, inc=1, device_id=(me.dp, t), device_id_type=MESH)

        return carry

    lax.fori_loop(0, N_CTX, hello, 0)
    others = [
        me.at(z=me.step("z", dz), core=lax.rem(me.core + dc, 2)) for dz in range(4) for dc in range(2) if dz % 2 or dc
    ]
    for d in others:
        pl.semaphore_signal(bar, inc=1, device_id=d, device_id_type=MESH)
    pl.semaphore_wait(bar, N_CTX - 1 + len(others))

    first = []
    for k in (1, 2, 3):
        t = me.step("x", k)
        d = me.at(x=t)
        for n, (src, dst) in enumerate(((wq, rq.at[me.x]), (wo, ro.at[me.x]))):
            first.append(remote(src, dst, s1.at[k - 1, n], r1.at[k - 1, n], d))
        for g in range(8):
            tile = 60 if g == 7 else 35 * g // 4
            col = pl.multiple_of(tile * 128 + lax.rem(t, 2) * 640, 128)
            src = wg.at[lax.div(t, 2), :, pl.ds(col, 640)]
            first.append(remote(src, rg.at[me.x, g], s1.at[k - 1, 2 + g], r1.at[k - 1, 2 + g], d))
    for c in first:
        c.start()
    mine = [
        pltpu.make_async_copy(wq, rq.at[me.x], ls.at[0]),
        pltpu.make_async_copy(wo, ro.at[me.x], ls.at[1]),
    ]
    for g in range(8):
        tile = 60 if g == 7 else 35 * g // 4
        col = pl.multiple_of(tile * 128 + lax.rem(me.x, 2) * 640, 128)
        mine.append(
            pltpu.make_async_copy(wg.at[lax.div(me.x, 2), :, pl.ds(col, 640)], rg.at[me.x, g], ls.at[2 + g])
        )
    for c in mine:
        c.start()
    ez = ZGather(me, eext, oe, se, re_, ce, cre, BLK)
    ez.first()
    own_e = pltpu.make_async_copy(eext, oe.at[me.zlo, me.core, me.zhi], ls.at[10])
    own_e.start()
    own_i = pltpu.make_async_copy(idx, oi.at[me.dp, me.zhi], ls.at[11])
    own_i.start()
    ic = []
    for n, d in enumerate(zpeers):
        c = remote(idx, oi.at[me.dp, me.zhi], si.at[n], ri.at[n], d)
        c.start()
        ic.append(c)

    for c in mine:
        c.wait()
    for k in (1, 2, 3):
        f = me.step("x", 4 - k)
        d = me.at(x=f)
        for n, ref in enumerate((rq.at[f], ro.at[f])):
            remote(ref, ref, s1.at[k - 1, n], r1.at[k - 1, n], d).wait_recv()
        for g in range(8):
            ref = rg.at[f, g]
            remote(ref, ref, s1.at[k - 1, 2 + g], r1.at[k - 1, 2 + g], d).wait_recv()
    row, col = iota((48, 64), 0), iota((48, 64), 1)
    put = jnp.where(
        (lax.rem(col, 16) < 12) & (lax.div(col, 16) * 12 + lax.rem(col, 16) == row), 1.0, 0.0
    ).astype(BF)
    cq[...] = mm(put, rq[...].reshape(64, 2048)).astype(BF)
    co[...] = mm(put, ro[...].reshape(64, D)).astype(BF)

    def vy0(j, h):
        ref = oq.at[me.zlo, me.core, j, me.zhi]
        return ref if h is None else ref.at[:, pl.ds(1024 * h, 1024)]

    def vz0(j, h, core=me.core):
        zl, zh = lax.rem(j, 2), lax.div(j, 2)
        return oq.at[zl, core, :, zh] if h is None else oq.at[zl, core, pl.ds(2 * h, 2), zh]

    def vz1(j, h):
        ref = oo.at[lax.rem(j, 2), me.core, me.y, lax.div(j, 2)]
        return ref if h is None else ref.at[:, pl.ds(768 * h, 768)]

    def vy1(j, h, core=me.core):
        return oo.at[:, core, j] if h is None else oo.at[h, core, j]

    ra = Ring(me, "y", cq, vy0, ss.at[0], rs.at[0])
    rb = Ring(me, "z", co, vz1, ss.at[1], rs.at[1])
    ra.first()
    rb.first()
    own = [
        pltpu.make_async_copy(cq, oq.at[me.zlo, me.core, me.y, me.zhi], ls.at[12]),
        pltpu.make_async_copy(co, oo.at[me.zlo, me.core, me.y, me.zhi], ls.at[13]),
    ]
    for c in own:
        c.start()
    for g in range(8):
        cg[g] = mm(put, rg[:, g].reshape(64, 640)).astype(BF)
    own_g = pltpu.make_async_copy(
        cg.at[me.slice], og.at[me.x, me.zlo, me.core, me.y, me.zhi], ls.at[14]
    )
    own_g.start()
    zc = []
    zk = [(dz, dc) for dz in range(4) for dc in range(2) if dz or dc]
    for n, (dz, dc) in enumerate(zk):
        z, core = me.step("z", dz), lax.rem(me.core + dc, 2)
        piece = 2 * (2 * lax.rem(z, 2) + core) + lax.div(z, 2)
        c = remote(
            cg.at[piece], og.at[me.x, me.zlo, me.core, me.y, me.zhi], s2.at[n], r2.at[n], me.at(z=z, core=core)
        )
        c.start()
        zc.append(c)
    zr = lax.div(me.y, 2)
    slot = lax.rem(me.y, 2) * 8 + me.zhi * 4 + me.x

    def down(k, wait):
        t = lax.rem(m + k, N_CTX)

        @pl.when(lax.rem(lax.div(t, 4), 2) == zr)
        def _():
            c = remote(wd, od.at[slot], sd.at[k], rd.at[slot], (me.dp, t))
            if wait:
                c.wait_send()
            else:
                c.start()

    def down_send(k, carry):
        down(k, False)
        return carry

    def down_sent(k, carry):
        down(k, True)
        return carry

    lax.fori_loop(1, N_CTX, down_send, 0)

    @pl.when(me.zhi == zr)
    def _():
        c = pltpu.make_async_copy(wd, od.at[slot], ls.at[15])
        c.start()
        c.wait()

    ra.second()
    rb.second()
    ez.second()
    ra.last()
    rb.last()
    for c in own:
        c.wait()
    ra2 = Ring(me, "z", vz0(me.z, None), vz0, ss.at[2], rs.at[2])
    rb2 = Ring(me, "y", vy1(me.y, None), vy1, ss.at[3], rs.at[3])
    ra2.first()
    rb2.first()
    swaps = []

    def swap(view, j):
        n = len(swaps)
        c = remote(view(j, None), view(j, None), sc.at[n], rc_.at[n], sib)
        c.start()
        swaps.append((c, view, j))

    swap(vz0, me.z)
    swap(vy1, me.y)

    own_g.wait()
    for n, (dz, dc) in enumerate(zk):
        z, core = me.step("z", 4 - dz if dz else 0), lax.rem(me.core + dc, 2)
        ref = og.at[me.x, lax.rem(z, 2), core, me.y, lax.div(z, 2)]
        remote(ref, ref, s2.at[n], r2.at[n], me.at(z=z, core=core)).wait_recv()

    def g0a(j, h):
        return og.at[me.x, 0, :, j] if h is None else og.at[me.x, 0, h, j]

    def g0b(j, h):
        return og.at[j, 0] if h is None else og.at[j, 0, h]

    def g1a(j, h):
        return og.at[j, 1, :, me.y] if h is None else og.at[j, 1, h, me.y]

    def g1b(j, h):
        return og.at[:, 1, :, j] if h is None else og.at[:, 1, h, j]

    ga = Ring(me, "y", g0a(me.y, None), g0a, ss.at[4], rs.at[4])
    gb = Ring(me, "x", g1a(me.x, None), g1a, ss.at[5], rs.at[5])
    ga.first()
    gb.first()
    ra2.second()
    rb2.second()
    swap(vz0, ra2.l)
    swap(vy1, rb2.l)
    swap(vz0, ra2.r)
    swap(vy1, rb2.r)
    ga.second()
    gb.second()
    ga.last()
    gb.last()
    ga2 = Ring(me, "x", g0b(me.x, None), g0b, ss.at[6], rs.at[6])
    gb2 = Ring(me, "y", g1b(me.y, None), g1b, ss.at[7], rs.at[7])
    ga2.first()
    gb2.first()
    ra2.last()
    rb2.last()
    swap(vz0, ra2.o)
    swap(vy1, rb2.o)
    ez.last()
    ga2.second()
    gb2.second()
    ga2.last()
    gb2.last()

    for r in (ra, rb, ra2, rb2, ga, gb, ga2, gb2):
        r.sent()
    for c in first:
        c.wait_send()
    for c in zc:
        c.wait_send()
    for n, (c, view, j) in enumerate(swaps):
        c.wait_send()
        ref = view(j, None, 1 - me.core)
        remote(ref, ref, sc.at[n], rc_.at[n], sib).wait_recv()
    ez.finish()
    own_e.wait()
    own_i.wait()
    for n, (dz, dc) in enumerate(zk):
        z, core = me.step("z", 4 - dz if dz else 0), lax.rem(me.core + dc, 2)
        ic[n].wait_send()
        ref = oi.at[2 * lax.rem(z, 2) + core, lax.div(z, 2)]
        remote(ref, ref, si.at[n], ri.at[n], me.at(z=z, core=core)).wait_recv()
    lax.fori_loop(1, N_CTX, down_sent, 0)

    def down_got(n, carry):
        src = (2 * me.zhi + lax.div(n, 8)) * 8 + lax.rem(n, 8)

        @pl.when(src != m)
        def _():
            remote(wd, od.at[n], sd.at[0], rd.at[n], (me.dp, src)).wait_recv()

        return carry

    lax.fori_loop(0, 16, down_got, 0)


def weights(idx, wq, wo, wg, wd, eext):
    outs = (
        sds((2, 2, 4, 2, 48, 2048), BF),
        sds((2, 2, 4, 2, 48, D), BF),
        sds((4, 2, 2, 4, 2, 48, 640), BF),
        sds((16, 80, D), BF),
        sds((2, 2, 2, ROWS, DX), BF),
        sds((4, 2, 8, 128), jnp.int32),
    )
    scratch = [
        pltpu.VMEM((4, 16, 2048), BF),
        pltpu.VMEM((4, 16, D), BF),
        pltpu.VMEM((4, 8, 16, 640), BF),
        pltpu.VMEM((48, 2048), BF),
        pltpu.VMEM((48, D), BF),
        pltpu.VMEM((8, 48, 640), BF),
        DMA((8, 4)),
        DMA((8, 4)),
        DMA((16,)),
        DMA((3, 10)),
        DMA((3, 10)),
        DMA((7,)),
        DMA((7,)),
        DMA((8,)),
        DMA((8,)),
        DMA((N_CTX,)),
        DMA((16,)),
        DMA((4,)),
        DMA((4,)),
        DMA((4,)),
        DMA((4,)),
        DMA((7,)),
        DMA((7,)),
    ]
    return pl.pallas_call(
        weights_kernel,
        out_shape=outs,
        in_specs=[ANY] * 6,
        out_specs=[ANY] * 6,
        scratch_shapes=scratch,
        compiler_params=pltpu.CompilerParams(collective_id=1, has_side_effects=True, vmem_limit_bytes=VMEM_LIMIT),
    )(idx, wq, wo, wg, wd, eext)


def turn(v, cos, sin):
    return v * cos + pltpu.roll(v, 64, 1) * sin


def turn_back(v, cos, sin):
    return v * cos - pltpu.roll(v, 64, 1) * sin


def qkv_kernel(n1, w, ub, cos, sin, q_o, kv_o):
    c, s = cos[...], sin[...]
    for h in range(HEADS + 2 * KV_HEADS):
        cols = slice(h * HS, (h + 1) * HS)
        if h % 2 == 0:
            pair = slice(h * HS, (h + 2) * HS)
            j = mm(n1[...], w[:, pair]) + ub[:, pair]
        v = j[:, (h % 2) * HS : (h % 2 + 1) * HS]
        if h < HEADS + KV_HEADS:
            v = turn(v, c, s)
        v = v.astype(BF)
        if h < HEADS:
            q_o[:, cols] = v
        else:
            at = slice((h - HEADS) * HS, (h - HEADS + 1) * HS)
            kv_o[0, :, at] = v[:BLK]
            kv_o[1, :, at] = v[BLK:]


def qkv(n1, w, ub, cos, sin):
    return pl.pallas_call(
        qkv_kernel,
        out_shape=(sds((ROWS, D), BF), sds((2, BLK, 2 * KW), BF)),
        in_specs=[VM] * 5,
        out_specs=[VM] * 2,
        compiler_params=pltpu.CompilerParams(vmem_limit_bytes=VMEM_LIMIT),
    )(n1, w, ub, cos, sin)


def reads(t, block):
    a, b = t - block, NBLK - 1 - t - block
    return ((a >= 0) & (a < NWB)) | ((b >= 0) & (b < NWB))


def halo_kernel(own, out, zero, ss, rs, ls):
    me = Place()
    m = me.ctx
    bar = pltpu.get_barrier_semaphore()

    def hello(t, carry):
        @pl.when(t != m)
        def _():
            pl.semaphore_signal(bar, inc=1, device_id=(me.dp, t), device_id_type=MESH)

        return carry

    lax.fori_loop(0, N_CTX, hello, 0)
    zero[...] = jnp.zeros_like(zero)
    local = [
        pltpu.make_async_copy(own.at[0], out.at[16 + m], ls.at[0]),
        pltpu.make_async_copy(own.at[1], out.at[16 + NBLK - 1 - m], ls.at[1]),
        pltpu.make_async_copy(zero, out.at[pl.ds(0, 16)], ls.at[2]),
    ]
    for c in local:
        c.start()
    pl.semaphore_wait(bar, N_CTX - 1)

    def send(k, carry):
        t = lax.rem(m + k, N_CTX)
        for h in range(2):
            block = m if h == 0 else NBLK - 1 - m

            @pl.when(reads(t, block))
            def _():
                remote(own.at[h], out.at[16 + block], ss.at[h, k], rs.at[block], (me.dp, t)).start()

        return carry

    lax.fori_loop(1, N_CTX, send, 0)

    def wait(k, carry):
        t = lax.rem(m + k, N_CTX)
        for h in range(2):
            block = m if h == 0 else NBLK - 1 - m

            @pl.when(reads(t, block))
            def _():
                remote(own.at[h], out.at[16 + block], ss.at[h, k], rs.at[block], (me.dp, t)).wait_send()

            theirs = t if h == 0 else NBLK - 1 - t

            @pl.when(reads(m, theirs))
            def _():
                remote(own.at[h], out.at[16 + theirs], ss.at[h, k], rs.at[theirs], (me.dp, t)).wait_recv()

        return carry

    lax.fori_loop(1, N_CTX, wait, 0)
    for c in local:
        c.wait()


def halo(kv):
    return pl.pallas_call(
        halo_kernel,
        out_shape=sds((16 + NBLK, BLK, 2 * KW), BF),
        in_specs=[ANY],
        out_specs=ANY,
        scratch_shapes=[pltpu.VMEM((16, BLK, 2 * KW), BF), DMA((2, N_CTX)), DMA((NBLK,)), DMA((3,))],
        compiler_params=pltpu.CompilerParams(collective_id=2, has_side_effects=True, vmem_limit_bytes=VMEM_LIMIT),
    )(kv)


def load_windows(kv, win, sem):
    m = lax.axis_index("ctx")
    copies = [
        pltpu.make_async_copy(kv.at[pl.ds(m, NWB)], win.at[0], sem.at[0]),
        pltpu.make_async_copy(kv.at[pl.ds(NBLK - 1 - m, NWB)], win.at[1], sem.at[1]),
    ]
    for c in copies:
        c.start()
    return copies


def stack_heads(ref, h, a):
    rows = slice(h * BLK, (h + 1) * BLK)
    return jnp.concatenate(
        [ref[rows, (a * GROUP + g) * HS : (a * GROUP + g + 1) * HS] for g in range(GROUP)], 0
    )


def attend_kernel(idx, low, q, kv, x, w_out, a_in, b_res, gain, a45, p_o, o_o, h_o, n2_o, win, sem):
    m = lax.axis_index("ctx")
    copies = load_windows(kv, win, sem)
    for h in range(2):
        copies[h].wait()
        base = (m if h == 0 else NBLK - 1 - m) * BLK
        kpos = base - WIN + iota((BLK, KEYS), 1)
        qpos = base + iota((BLK, KEYS), 0)
        keep = (kpos <= qpos) & (kpos >= low[h * BLK : (h + 1) * BLK, :1])
        for a in range(KV_HEADS):
            qs = stack_heads(q, h, a)
            k = win[h, :, :, a * HS : (a + 1) * HS].reshape(KEYS, HS)
            v = win[h, :, :, KW + a * HS : KW + (a + 1) * HS].reshape(KEYS, HS)
            sc = nt(qs, k) * SCALE
            sc = jnp.where(keep[None], sc.reshape(GROUP, BLK, KEYS), -1e30)
            e = jnp.exp(sc - jnp.max(sc, -1, keepdims=True))
            p = (e / jnp.sum(e, -1, keepdims=True)).astype(BF).reshape(GROUP * BLK, KEYS)
            p_o[2 * h + a] = p
            o = mm(p, v).astype(BF)
            for g in range(GROUP):
                o_o[h * BLK : (h + 1) * BLK, (a * GROUP + g) * HS : (a * GROUP + g + 1) * HS] = o[
                    g * BLK : (g + 1) * BLK
                ]
    o = o_o[...]
    u3 = nt(o, a_in[0, 3]).astype(BF)
    hid = x[...].astype(F32) + mm(o, w_out[...]) + mm(u3, b_res[0, 0])
    h_o[...] = hid
    n2 = (hid * rms(hid) * gain[...].astype(F32)).astype(BF)
    n2_o[:, :D] = n2
    n2_o[:, D:] = nt(n2, a45[...]).astype(BF)


def attend(idx, low, q, kv, x, w_out, a_in, b_res, gain, a45):
    outs = (
        sds((4, GROUP * BLK, KEYS), BF),
        sds((ROWS, D), BF),
        sds((ROWS, D), F32),
        sds((ROWS, DX), BF),
    )
    return pl.pallas_call(
        attend_kernel,
        out_shape=outs,
        grid_spec=pltpu.PrefetchScalarGridSpec(
            num_scalar_prefetch=1,
            grid=(1,),
            in_specs=[
                whole(low.shape),
                whole(q.shape),
                ANY,
                whole(x.shape),
                whole(w_out.shape),
                pick(a_in.shape),
                pick(b_res.shape),
                whole((1, D)),
                whole(a45.shape),
            ],
            out_specs=[whole(o.shape) for o in outs],
            scratch_shapes=[pltpu.VMEM((2, NWB, BLK, 2 * KW), BF), DMA((2,))],
        ),
        compiler_params=pltpu.CompilerParams(vmem_limit_bytes=VMEM_LIMIT),
    )(idx, low, q, kv, x, w_out, a_in, b_res, gain, a45)


def gather_kernel(own, out, ss, rs, cs, cr, ls):
    me = Place()
    greet(me.ring("z") + [me.sibling()])
    c = pltpu.make_async_copy(own, out.at[me.zlo, me.core, me.zhi], ls.at[0])
    c.start()
    z = ZGather(me, own, out, ss, rs, cs, cr, BLK)
    z.first()
    z.second()
    z.last()
    z.finish()
    c.wait()


def gather(own):
    return pl.pallas_call(
        gather_kernel,
        out_shape=sds((2, 2, 2, ROWS, DX), BF),
        in_specs=[ANY],
        out_specs=ANY,
        scratch_shapes=[DMA((4,))] * 4 + [DMA((1,))],
        compiler_params=pltpu.CompilerParams(collective_id=3, has_side_effects=True, vmem_limit_bytes=VMEM_LIMIT),
    )(own)


def compact_kernel(wd, out):
    piece = 2 * lax.axis_index("dp") + lax.rem(lax.div(lax.axis_index("ctx"), 4), 2)
    o = FV * piece - 128 * window_tile(piece)
    for r in range(5):
        row = iota((256, 1280), 0) + 256 * r - o
        col = iota((256, 1280), 1)
        i, k = lax.div(col, 80), lax.rem(col, 80)
        put = jnp.where((k < 70) & (i * 70 + k == row), 1.0, 0.0).astype(BF)
        out[256 * r : 256 * (r + 1)] = mm(put, wd[...].reshape(1280, D)).astype(BF)


def compact(wd):
    return pl.pallas_call(
        compact_kernel,
        out_shape=sds((FW, D), BF),
        in_specs=[VM],
        out_specs=VM,
        compiler_params=pltpu.CompilerParams(vmem_limit_bytes=VMEM_LIMIT),
    )(wd)


FSTEPS = 4
FROWS = 8 * ROWS // FSTEPS


def feed_kernel(idx, x, e, og, wd, ad_all, b_all, y_o, g_o, tiles_o, wg, wu, ad, bg, bu, acc, sem):
    piece = 2 * lax.axis_index("dp") + lax.rem(lax.div(lax.axis_index("ctx"), 4), 2)
    tile = window_tile(piece)
    o = FV * piece - 128 * tile
    step = pl.program_id(0)

    @pl.when(step == 0)
    def _():
        cols = pl.ds(pl.multiple_of(tile * 128, 128), FW)
        copies = []
        for q in range(4):
            w = wg if q < 2 else wu
            copies.append(pltpu.make_async_copy(og.at[q], w.at[:, pl.ds(640 * (q % 2), 640)], sem.at[q]))
        for s in range(4):
            rows, rows2 = pl.ds(R * s, R), pl.ds(64 + R * s, R)
            copies.append(pltpu.make_async_copy(ad_all.at[idx[s], :, cols], ad.at[rows], sem.at[4 + s]))
            copies.append(pltpu.make_async_copy(b_all.at[idx[s], 0, :, cols], bg.at[rows], sem.at[8 + s]))
            copies.append(pltpu.make_async_copy(b_all.at[idx[s], 1, :, cols], bu.at[rows2], sem.at[12 + s]))
        for c in copies:
            c.start()
        ad[64:] = jnp.zeros((64, FW), BF)
        bg[64:] = jnp.zeros((64, FW), BF)
        bu[:64] = jnp.zeros((64, FW), BF)
        acc[...] = jnp.zeros_like(acc)
        for c in copies:
            c.wait()
        col = iota((64, FW), 1)
        ad[:64] = jnp.where((col >= o) & (col < o + FV), ad[:64], jnp.zeros((), BF))

    n2, u = x[:, :D], x[:, D:]
    eo, gud = e[:, :D], e[:, D:]
    gate = mm(n2, wg[...]) + mm(u, bg[...])
    up = mm(n2, wu[...]) + mm(u, bu[...])
    gm = nt(eo, wd[...]) + mm(gud, ad[...])
    sig = 1.0 / (1.0 + jnp.exp(-gate))
    sl = gate * sig
    act = (sl * up).astype(BF)
    gg = (gm * up * (sig * (1.0 + gate * (1.0 - sig)))).astype(BF)
    gu = (gm * sl).astype(BF)
    y_o[:, :D] = mm(act, wd[...]).astype(BF)
    y_o[:, D:] = nt(act, ad[...]).astype(BF)
    g_o[:, :D] = (nt(gg, wg[...]) + nt(gu, wu[...])).astype(BF)
    g_o[:, D:] = (nt(gg, bg[...]) + nt(gu, bu[...])).astype(BF)
    acc[0] += tn(gud, act)[:64]
    acc[1] += tn(u, gg)[:64]
    acc[2] += tn(u, gu)[64:]

    @pl.when(step == FSTEPS - 1)
    def _():
        col = iota((64, FW), 1)
        valid = (col >= o) & (col < o + FV)
        for k in range(3):
            v = jnp.where(valid, acc[k], 0.0).astype(BF)
            for s in range(4):
                for t in range(10):
                    tiles_o[s * 30 + k * 10 + t] = v[R * s : R * (s + 1), 128 * t : 128 * (t + 1)]
        for t in range(120, 128):
            tiles_o[t] = jnp.zeros((R, 128), BF)


def feed(idx, x, e, og, wd, ad_all, b_all):
    outs = (sds((8 * ROWS, DX), BF), sds((8 * ROWS, DX), BF), sds((128, R, 128), BF))
    rows = pl.BlockSpec((FROWS, DX), lambda i, idx: (i, 0))
    return pl.pallas_call(
        feed_kernel,
        out_shape=outs,
        grid_spec=pltpu.PrefetchScalarGridSpec(
            num_scalar_prefetch=1,
            grid=(FSTEPS,),
            in_specs=[rows, rows, ANY, whole((FW, D)), ANY, ANY],
            out_specs=[rows, rows, whole((128, R, 128))],
            scratch_shapes=[
                pltpu.VMEM((D, FW), BF),
                pltpu.VMEM((D, FW), BF),
                pltpu.VMEM((EXT, FW), BF),
                pltpu.VMEM((EXT, FW), BF),
                pltpu.VMEM((EXT, FW), BF),
                pltpu.VMEM((3, 64, FW), F32),
                DMA((16,)),
            ],
        ),
        compiler_params=pltpu.CompilerParams(vmem_limit_bytes=VMEM_LIMIT),
    )(idx, x, e, og, wd, ad_all, b_all)


def scatter_kernel(part, out, own, got, got2, red, ls, cs, cr, ss, rs):
    me = Place()
    sib = me.sibling()
    greet(me.ring("z") + [sib])
    sends, mine = [], []
    for j in range(4):
        z = me.step("z", j)
        zl, zh = lax.rem(z, 2), lax.div(z, 2)
        c = remote(part.at[zl, 1 - me.core, zh], got.at[j], cs.at[j], cr.at[j], sib)
        c.start()
        sends.append(c)
        c = pltpu.make_async_copy(part.at[zl, me.core, zh], own.at[j], ls.at[j])
        c.start()
        mine.append(c)
    outs = []
    for j in (2, 1, 3, 0):
        sends[j].wait_recv()
        mine[j].wait()
        total = own[j].astype(F32) + got[j].astype(F32)
        if j == 0:
            out[...] = total
        else:
            red[j - 1] = total.astype(BF)
            c = remote(red.at[j - 1], got2.at[j - 1], ss.at[j - 1], rs.at[j - 1], me.at(z=me.step("z", j)))
            c.start()
            outs.append(c)
    for c in sends:
        c.wait_send()
    for j in (1, 3, 2):
        f = me.at(z=me.step("z", 4 - j))
        remote(red.at[j - 1], got2.at[j - 1], ss.at[j - 1], rs.at[j - 1], f).wait_recv()
        out[...] += got2[j - 1].astype(F32)
    for c in outs:
        c.wait_send()


def scatter(part, cid):
    return pl.pallas_call(
        scatter_kernel,
        out_shape=sds((ROWS, DX), F32),
        in_specs=[ANY],
        out_specs=VM,
        scratch_shapes=[
            pltpu.VMEM((4, ROWS, DX), BF),
            pltpu.VMEM((4, ROWS, DX), BF),
            pltpu.VMEM((3, ROWS, DX), BF),
            pltpu.VMEM((3, ROWS, DX), BF),
            DMA((4,)),
            DMA((4,)),
            DMA((4,)),
            DMA((3,)),
            DMA((3,)),
        ],
        compiler_params=pltpu.CompilerParams(collective_id=cid, has_side_effects=True, vmem_limit_bytes=VMEM_LIMIT),
    )(part)


def norm_back(z, gain, grad):
    r = rms(z)
    t = gain * grad
    return r * t - z * (r * r * r) * jnp.mean(t * z, -1, keepdims=True)


def back_kernel(
    idx, gn2, e, hid, n2, q, o, p, kv, w_out, a_in, b_res, gain, a45,
    gh_o, gq_o, win_o, g45_o, gbo_o, ga3_o, go, win, sem,
):
    copies = load_windows(kv, win, sem)
    s = lax.axis_index("dp")
    gue = gn2[:, D:].astype(BF)
    gn = gn2[:, :D] + mm(gue, a45[...])
    gh = e[:, :D].astype(F32) + norm_back(hid[...], gain[...].astype(F32), gn)
    gh_o[...] = gh
    ghb = gh.astype(BF)
    ob = o[...]
    gu3 = nt(ghb, b_res[0, 0]).astype(BF)
    go[...] = (nt(ghb, w_out[...]) + mm(gu3, a_in[0, 3])).astype(BF)
    u3 = nt(ob, a_in[0, 3]).astype(BF)
    gbo_o[...] = tn(u3, ghb)
    ga3_o[...] = tn(gu3, ob)
    g45_o[...] = tn(gue, n2[:, :D])
    for h in range(2):
        copies[h].wait()
        for a in range(KV_HEADS):
            qs, gs, os = stack_heads(q, h, a), stack_heads(go, h, a), stack_heads(o, h, a)
            k = win[h, :, :, a * HS : (a + 1) * HS].reshape(KEYS, HS)
            v = win[h, :, :, KW + a * HS : KW + (a + 1) * HS].reshape(KEYS, HS)
            pr = p[2 * h + a]
            delta = jnp.sum(gs.astype(F32) * os.astype(F32), -1, keepdims=True)
            ds = (pr.astype(F32) * (nt(gs, v) - delta)).astype(BF)
            gq = mm(ds, k) * SCALE
            for g in range(GROUP):
                gq_o[h * BLK : (h + 1) * BLK, (a * GROUP + g) * HS : (a * GROUP + g + 1) * HS] = gq[
                    g * BLK : (g + 1) * BLK
                ]
            win_o[h, :, :, a * HS : (a + 1) * HS] = (tn(ds, qs) * SCALE).astype(BF).reshape(NWB, BLK, HS)
            win_o[h, :, :, KW + a * HS : KW + (a + 1) * HS] = tn(pr, gs).astype(BF).reshape(NWB, BLK, HS)


def back(idx, gn2, e, hid, n2, q, o, p, kv, w_out, a_in, b_res, gain, a45):
    outs = (
        sds((ROWS, D), F32),
        sds((ROWS, D), F32),
        sds((2, NWB, BLK, 2 * KW), BF),
        sds((EXT, D), F32),
        sds((R, D), F32),
        sds((R, D), F32),
    )
    return pl.pallas_call(
        back_kernel,
        out_shape=outs,
        grid_spec=pltpu.PrefetchScalarGridSpec(
            num_scalar_prefetch=1,
            grid=(1,),
            in_specs=[
                whole(gn2.shape),
                whole(e.shape),
                whole(hid.shape),
                whole(n2.shape),
                whole(q.shape),
                whole(o.shape),
                whole(p.shape),
                ANY,
                whole(w_out.shape),
                pick(a_in.shape),
                pick(b_res.shape),
                whole((1, D)),
                whole(a45.shape),
            ],
            out_specs=[whole(x.shape) for x in outs],
            scratch_shapes=[
                pltpu.VMEM((ROWS, D), BF),
                pltpu.VMEM((2, NWB, BLK, 2 * KW), BF),
                DMA((2,)),
            ],
        ),
        compiler_params=pltpu.CompilerParams(vmem_limit_bytes=VMEM_LIMIT),
    )(idx, gn2, e, hid, n2, q, o, p, kv, w_out, a_in, b_res, gain, a45)


def return_kernel(win, out, got, ss, rs, ls):
    me = Place()
    m = me.ctx
    bar = pltpu.get_barrier_semaphore()

    def hello(t, carry):
        @pl.when(t != m)
        def _():
            pl.semaphore_signal(bar, inc=1, device_id=(me.dp, t), device_id_type=MESH)

        return carry

    lax.fori_loop(0, N_CTX, hello, 0)
    pl.semaphore_wait(bar, N_CTX - 1)

    def covers(t, w, owner, h):
        block = owner if h == 0 else NBLK - 1 - owner
        j = block - ((t if w == 0 else NBLK - 1 - t) - (NWB - 1))
        return j, (j >= 0) & (j < NWB)

    def send(k, carry):
        t = lax.rem(m + k, N_CTX)
        for w in range(2):
            for h in range(2):
                j, ok = covers(m, w, t, h)

                @pl.when(ok)
                def _():
                    remote(win.at[w, j], got.at[h, w, m], ss.at[h, w, t], rs.at[h, w, m], (me.dp, t)).start()

        return carry

    lax.fori_loop(1, N_CTX, send, 0)
    for w in range(2):
        for h in range(2):
            j, ok = covers(m, w, m, h)

            @pl.when(ok)
            def _():
                c = pltpu.make_async_copy(win.at[w, j], got.at[h, w, m], ls.at[h, w])
                c.start()
                c.wait()

    out[...] = jnp.zeros_like(out)

    def take(k, carry):
        t = lax.rem(m + N_CTX - k, N_CTX)
        for w in range(2):
            for h in range(2):
                _, ok = covers(t, w, m, h)

                @pl.when(ok & (k > 0))
                def _():
                    remote(got.at[h, w, t], got.at[h, w, t], ss.at[h, w, t], rs.at[h, w, t], (me.dp, t)).wait_recv()

                @pl.when(ok)
                def _():
                    out[h] += got[h, w, t].astype(F32)

        return carry

    lax.fori_loop(0, N_CTX, take, 0)

    def sent(k, carry):
        t = lax.rem(m + k, N_CTX)
        for w in range(2):
            for h in range(2):
                j, ok = covers(m, w, t, h)

                @pl.when(ok)
                def _():
                    remote(win.at[w, j], got.at[h, w, m], ss.at[h, w, t], rs.at[h, w, m], (me.dp, t)).wait_send()

        return carry

    lax.fori_loop(1, N_CTX, sent, 0)


def give_back(win):
    return pl.pallas_call(
        return_kernel,
        out_shape=sds((2, BLK, 2 * KW), F32),
        in_specs=[ANY],
        out_specs=VM,
        scratch_shapes=[
            pltpu.VMEM((2, 2, N_CTX, BLK, 2 * KW), BF),
            DMA((2, 2, N_CTX)),
            DMA((2, 2, N_CTX)),
            DMA((2, 2)),
        ],
        compiler_params=pltpu.CompilerParams(collective_id=5, has_side_effects=True, vmem_limit_bytes=VMEM_LIMIT),
    )(win)


def final_kernel(
    idx, gkv, gq, x, n1, gh, hid, y, e, w_qkv, a_in, b_qkv_ad, bd, gain, cos, sin, g45, gbo, ga3,
    out_o, gt_o, tiles_o, gj,
):
    s = lax.axis_index("dp")
    c, sn = cos[...], sin[...]
    for h in range(HEADS):
        cols = slice(h * HS, (h + 1) * HS)
        gj[:, cols] = turn_back(gq[:, cols], c, sn).astype(BF)
    for a in range(KV_HEADS):
        v = jnp.concatenate([gkv[0, :, a * HS : (a + 1) * HS], gkv[1, :, a * HS : (a + 1) * HS]], 0)
        gj[:, QW + a * HS : QW + (a + 1) * HS] = turn_back(v, c, sn).astype(BF)
    gj[:, QW + KW :] = jnp.concatenate([gkv[0, :, KW:], gkv[1, :, KW:]], 0).astype(BF)
    n1b = n1[...]
    gn = nt(gj[...], w_qkv[...])

    def put(at, v):
        for t in range(v.shape[1] // 128):
            tiles_o[at + t] = v[:, 128 * t : 128 * (t + 1)].astype(BF)

    at_qkv = 8 * 12
    for m, (lo, hi) in enumerate(((0, QW), (QW, QW + KW), (QW + KW, QW + 2 * KW))):
        am = a_in[0, m]
        u = nt(n1b, am).astype(BF)
        gjm = gj[:, lo:hi]
        gum = nt(gjm, b_qkv_ad[0, :, lo:hi]).astype(BF)
        gn += mm(gum, am)
        put(at_qkv + lo // 128, tn(u, gjm))
        put(12 * m, tn(gum, n1b))
    put(12 * 3, ga3[...])
    own = pl.multiple_of(s * R, R)
    put(12 * 4, g45[pl.ds(own, R), :])
    put(12 * 5, g45[pl.ds(own + 64, R), :])
    put(12 * 6, gbo[...])
    ud = y[:, D:].astype(BF)
    gbd = tn(ud, e[:, :D])
    own_bd = jnp.where((iota((R, EXT), 1) == iota((R, EXT), 0) + s * R), 1.0, 0.0)
    put(12 * 7, jnp.dot(own_bd, gbd, preferred_element_type=F32))
    for t in range(112, 128):
        tiles_o[t] = jnp.zeros((R, 128), BF)
    gt_o[...] = (gh[...] + norm_back(x[...].astype(F32), gain[...].astype(F32), gn)).astype(BF)
    out_o[...] = (hid[...] + y[:, :D] + mm(ud, bd[...])).astype(BF)


def final(idx, gkv, gq, x, n1, gh, hid, y, e, w_qkv, a_in, b_qkv_ad, bd, gain, cos, sin, g45, gbo, ga3):
    outs = (sds((ROWS, D), BF), sds((ROWS, D), BF), sds((128, R, 128), BF))
    args = (gkv, gq, x, n1, gh, hid, y, e, w_qkv, a_in, b_qkv_ad, bd, gain, cos, sin, g45, gbo, ga3)
    return pl.pallas_call(
        final_kernel,
        out_shape=outs,
        grid_spec=pltpu.PrefetchScalarGridSpec(
            num_scalar_prefetch=1,
            grid=(1,),
            in_specs=[pick(v.shape) if i in (9, 10) else whole(v.shape) for i, v in enumerate(args)],
            out_specs=[whole(x.shape) for x in outs],
            scratch_shapes=[pltpu.VMEM((ROWS, 2048), BF)],
        ),
        compiler_params=pltpu.CompilerParams(vmem_limit_bytes=VMEM_LIMIT),
    )(idx, *args)


def total_kernel(lt, ft, out, gl, gf, red, ls, s1, r1, s2, r2, ss, rs, cs, cr, s3, r3):
    me = Place()
    sib = me.sibling()
    m = me.ctx
    bar = pltpu.get_barrier_semaphore()

    def hello(t, carry):
        @pl.when(t != m)
        def _():
            pl.semaphore_signal(bar, inc=1, device_id=(me.dp, t), device_id_type=MESH)

        return carry

    lax.fori_loop(0, N_CTX, hello, 0)
    others = [me.at(z=me.step("z", 1)), me.at(z=me.step("z", 3)), sib]
    for d in others:
        pl.semaphore_signal(bar, inc=1, device_id=d, device_id_type=MESH)
    pl.semaphore_wait(bar, N_CTX - 1 + len(others))

    xy = me.y * 4 + me.x

    def plane(k):
        return me.at(x=lax.rem(k, 4), y=lax.div(k, 4))

    def send_l(k, carry):
        t = lax.rem(m + k, N_CTX)
        remote(lt.at[pl.ds(4 * t, 4)], gl.at[m], s1.at[t], r1.at[m], (me.dp, t)).start()
        return carry

    def send_f(k, carry):
        t = lax.rem(xy + k, 16)
        remote(ft.at[pl.ds(8 * t, 8)], gf.at[xy], s2.at[t], r2.at[xy], plane(t)).start()
        return carry

    lax.fori_loop(1, 16, send_f, 0)
    lax.fori_loop(1, N_CTX, send_l, 0)
    own = [
        pltpu.make_async_copy(lt.at[pl.ds(4 * m, 4)], gl.at[m], ls.at[0]),
        pltpu.make_async_copy(ft.at[pl.ds(8 * xy, 8)], gf.at[xy], ls.at[1]),
    ]
    for c in own:
        c.start()
    for c in own:
        c.wait()

    def got_f(k, carry):
        t = lax.rem(xy + k, 16)
        remote(gf.at[t], gf.at[t], s2.at[t], r2.at[t], plane(t)).wait_recv()
        return carry + gf[t].astype(F32)

    red[4:] = lax.fori_loop(1, 16, got_f, gf[xy].astype(F32)).astype(BF)

    def got_l(k, carry):
        t = lax.rem(m + k, N_CTX)
        remote(gl.at[t], gl.at[t], s1.at[t], r1.at[t], (me.dp, t)).wait_recv()
        return carry + gl[t].astype(F32)

    red[:4] = lax.fori_loop(1, N_CTX, got_l, gl[m].astype(F32)).astype(BF)

    def vz(j, h):
        ref = out.at[me.y, me.x, lax.rem(j, 2), me.core, lax.div(j, 2)]
        return ref if h is None else ref.at[pl.ds(6 * h, 6)]

    c = pltpu.make_async_copy(red, vz(me.z, None), ls.at[2])
    c.start()
    rz = Ring(me, "z", red, vz, ss.at[0], rs.at[0])
    rz.first()
    rz.second()
    rz.last()
    c.wait()

    def x0(j, h):
        ref = out.at[me.y, j, :, me.core, :, pl.ds(0, 6)]
        return ref if h is None else out.at[me.y, j, h, me.core, :, pl.ds(0, 6)]

    def y0(j, h):
        ref = out.at[j, :, :, me.core, :, pl.ds(0, 6)]
        return ref if h is None else out.at[j, pl.ds(2 * h, 2), :, me.core, :, pl.ds(0, 6)]

    def y1(j, h):
        ref = out.at[j, me.x, :, me.core, :, pl.ds(6, 6)]
        return ref if h is None else out.at[j, me.x, h, me.core, :, pl.ds(6, 6)]

    def x1(j, h):
        ref = out.at[:, j, :, me.core, :, pl.ds(6, 6)]
        return ref if h is None else out.at[pl.ds(2 * h, 2), j, :, me.core, :, pl.ds(6, 6)]

    ra = Ring(me, "x", x0(me.x, None), x0, ss.at[1], rs.at[1])
    rb = Ring(me, "y", y1(me.y, None), y1, ss.at[2], rs.at[2])
    for f in ("first", "second", "last"):
        getattr(ra, f)()
        getattr(rb, f)()
    rc = Ring(me, "y", y0(me.y, None), y0, ss.at[3], rs.at[3])
    rd = Ring(me, "x", x1(me.x, None), x1, ss.at[4], rs.at[4])
    for f in ("first", "second", "last"):
        getattr(rc, f)()
        getattr(rd, f)()
    swaps = []
    for y in range(4):
        ref = out.at[y, :, :, me.core]
        k = remote(ref, ref, cs.at[y], cr.at[y], sib)
        k.start()
        swaps.append(k)
    for r in (rz, ra, rb, rc, rd):
        r.sent()

    def sent_l(k, carry):
        t = lax.rem(m + k, N_CTX)
        remote(lt.at[pl.ds(4 * t, 4)], gl.at[m], s1.at[t], r1.at[m], (me.dp, t)).wait_send()
        return carry

    def sent_f(k, carry):
        t = lax.rem(xy + k, 16)
        remote(ft.at[pl.ds(8 * t, 8)], gf.at[xy], s2.at[t], r2.at[xy], plane(t)).wait_send()
        return carry

    lax.fori_loop(1, 16, sent_f, 0)
    lax.fori_loop(1, N_CTX, sent_l, 0)
    for y in range(4):
        swaps[y].wait_send()
        ref = out.at[y, :, :, 1 - me.core]
        remote(ref, ref, cs.at[y], cr.at[y], sib).wait_recv()


def total(lt, ft):
    return pl.pallas_call(
        total_kernel,
        out_shape=sds((4, 4, 2, 2, 2, 12, R, 128), BF),
        in_specs=[ANY] * 2,
        out_specs=ANY,
        scratch_shapes=[
            pltpu.VMEM((N_CTX, 4, R, 128), BF),
            pltpu.VMEM((16, 8, R, 128), BF),
            pltpu.VMEM((12, R, 128), BF),
            DMA((3,)),
            DMA((N_CTX,)),
            DMA((N_CTX,)),
            DMA((16,)),
            DMA((16,)),
            DMA((5, 4)),
            DMA((5, 4)),
            DMA((4,)),
            DMA((4,)),
            DMA((1,)),
            DMA((1,)),
        ],
        compiler_params=pltpu.CompilerParams(collective_id=6, has_side_effects=True, vmem_limit_bytes=VMEM_LIMIT),
    )(lt, ft)


def spread_kernel(idx, t, ain_o, aff_o, bqkv_o, bres_o, bff_o):
    e = pl.program_id(0)
    for ref in (ain_o, aff_o, bqkv_o, bres_o, bff_o):
        ref[...] = jnp.zeros_like(ref)

    def local_tile(s, n):
        k, j = n // 4, n % 4
        y, zh, x = k // 8, (k // 4) % 2, k % 4
        return t[y, x, s // 2, s % 2, zh, j].astype(F32)

    def ff_tile(piece, n):
        k, j = n // 8, n % 8
        return t[k // 4, k % 4, piece // 4, (piece // 2) % 2, piece % 2, 4 + j].astype(F32)

    for s in range(4):

        @pl.when(idx[s] == e)
        def _():
            for m in range(6):
                for c in range(12):
                    ain_o[0, m, :, 128 * c : 128 * (c + 1)] += local_tile(s, 12 * m + c)
            for m in range(2):
                for c in range(12):
                    bres_o[0, m, :, 128 * c : 128 * (c + 1)] += local_tile(s, 12 * (6 + m) + c)
            for c in range(16):
                bqkv_o[0, :, 128 * c : 128 * (c + 1)] += local_tile(s, 96 + c)
            for piece in range(8):
                tile = 60 if piece == 7 else 35 * piece // 4
                for k in range(3):
                    for c in range(10):
                        cols = slice(128 * (tile + c), 128 * (tile + c + 1))
                        v = ff_tile(piece, s * 30 + k * 10 + c)
                        if k == 0:
                            aff_o[0, :, cols] += v
                        else:
                            bff_o[0, k - 1, :, cols] += v


def spread(idx, t):
    outs = (
        sds((ADAPT, 6, R, D), F32),
        sds((ADAPT, R, FF), F32),
        sds((ADAPT, R, 2048), F32),
        sds((ADAPT, 2, R, D), F32),
        sds((ADAPT, 2, R, FF), F32),
    )

    def one(shape):
        return pl.BlockSpec((1,) + shape[1:], lambda i, idx: (i,) + (0,) * (len(shape) - 1))

    return pl.pallas_call(
        spread_kernel,
        out_shape=outs,
        grid_spec=pltpu.PrefetchScalarGridSpec(
            num_scalar_prefetch=1,
            grid=(ADAPT,),
            in_specs=[whole(t.shape)],
            out_specs=[one(o.shape) for o in outs],
        ),
        compiler_params=pltpu.CompilerParams(vmem_limit_bytes=VMEM_LIMIT),
    )(idx, t)


def local(
    tokens,
    cotangent,
    w_qkv,
    b_qkv,
    w_out,
    w_gu,
    w_down,
    gain_attn,
    gain_mlp,
    adapt_in,
    adapt_in_ff,
    adapt_out_qkv,
    adapt_out_res,
    adapt_out_ff,
    doc_lengths,
    adapter_index,
    window,
):
    member = lax.axis_index("ctx")
    starts = jnp.stack([member * BLK, (NBLK - 1 - member) * BLK])
    pos = (starts[:, None] + jnp.arange(BLK, dtype=jnp.int32)[None]).reshape(ROWS)
    ends = jnp.cumsum(doc_lengths[0])
    begin = jnp.max(jnp.where(ends[None] <= pos[:, None], ends[None], 0), -1)
    low = jnp.maximum(begin, pos - window[0] + 1)
    low = jnp.broadcast_to(low[:, None], (ROWS, 128)).astype(jnp.int32)
    freq = 1000000.0 ** (-(2.0 * jnp.arange(HS // 2, dtype=F32)) / HS)
    ang = pos.astype(F32)[:, None] * freq[None]
    c, sn = jnp.cos(ang), jnp.sin(ang)
    cos = jnp.concatenate([c, c], -1)
    sin = jnp.concatenate([-sn, sn], -1)

    tok = jnp.transpose(tokens[0], (1, 0, 2)).reshape(ROWS, D)
    cot = jnp.transpose(cotangent[0], (1, 0, 2)).reshape(ROWS, D)
    gain1, gain2 = gain_attn[None], gain_mlp[None]
    wq = jnp.pad(w_qkv, ((0, 4), (0, 0)))
    wo = jnp.pad(w_out, ((0, 4), (0, 0)))
    wg = jnp.pad(jnp.transpose(w_gu, (1, 0, 2)), ((0, 0), (0, 4), (0, 0)))
    wd = jnp.pad(w_down, ((0, 10), (0, 0)))
    idx_row = jnp.broadcast_to(adapter_index[:, None], (8, 128)).astype(jnp.int32)

    x, n1, eext, ub, a45, bd = prepare(
        adapter_index, tok, cot, adapt_in, adapt_out_qkv, adapt_out_res, gain1, b_qkv[None]
    )
    oq, oo, og, od, oe, oi = weights(idx_row, wq, wo, wg, wd, eext)
    oq = oq.reshape(D, 2048)
    oo = oo.reshape(D, D)
    og = og.reshape(4, D, 640)
    idx4 = oi[:, 0, 0, 0]
    q, kv = qkv(n1, oq, ub, cos, sin)
    kv_all = halo(kv)
    p, o, hid, n2 = attend(adapter_index, low, q, kv_all, x, oo, adapt_in, adapt_out_res, gain2, a45)
    xg = gather(n2).reshape(8 * ROWS, DX)
    down = compact(od)
    yp, gp, ft = feed(idx4, xg, oe.reshape(8 * ROWS, DX), og, down, adapt_in_ff, adapt_out_ff)
    gn2 = scatter(gp.reshape(2, 2, 2, ROWS, DX), 4)
    gh, gq, win, g45, gbo, ga3 = back(
        adapter_index, gn2, eext, hid, n2, q, o, p, kv_all, oo, adapt_in, adapt_out_res, gain2, a45
    )
    y = scatter(yp.reshape(2, 2, 2, ROWS, DX), 4)
    gkv = give_back(win)
    out, gt, lt = final(
        adapter_index, gkv, gq, x, n1, gh, hid, y, eext, oq, adapt_in, adapt_out_qkv, bd, gain1, cos, sin, g45, gbo, ga3
    )
    tiles = total(lt, ft)
    grads = spread(idx4, tiles)

    def deal(v):
        return jnp.transpose(v.reshape(2, BLK, D), (1, 0, 2))[None]

    return (deal(out), deal(gt)) + tuple(grads)


def solution(mesh):
    return jax.shard_map(
        local,
        mesh=mesh,
        in_specs=(
            P("dp", "ctx", None, None),
            P("dp", "ctx", None, None),
            P(("dp", "ctx"), None),
            P(),
            P(("dp", "ctx"), None),
            P(("dp", "ctx"), None, None),
            P(("dp", "ctx"), None),
            P(),
            P(),
            P(),
            P(),
            P(),
            P(),
            P(),
            P("dp", None),
            P("dp"),
            P("dp"),
        ),
        out_specs=(P("dp", "ctx", None, None), P("dp", "ctx", None, None), P(), P(), P(), P(), P()),
        check_vma=False,
    )
```

time: 1800 us -> 511 us (0.28)
  waiting for transfers between devices: 1370 us -> 0 us
  Pallas kernels: 0 us -> 478 us
  matrix products: 174 us -> 0 us
  local copies, waits for them, and re-layouts: 168 us -> 21 us
  other arithmetic: 64.5 us -> 2.15 us
    all_gather x4 -> x0, waiting for transfers between devices: 1000 us -> none  [the longest x1 326 us: local(): lax.all_gather(w_gu, ('dp', 'ctx'), axis=0, tiled=True)]
    pallas_call x0 -> x15, Pallas kernels: none -> 478 us  [the longest x1 154 us: weights(): pl.pallas_call(weights_kernel, out_shape=outs, in_specs=[ANY] * 6, out_sp...]
    psum x1 -> x0, waiting for transfers between devices: 221 us -> none  [local(): lax.psum((spread_slot(grad_in_all), spread_slot(grad_in_ff), spread_slot(...]
    dot_general x44 -> x0, matrix products: 174 us -> none  [the longest x1 32.1 us: local(): jnp.einsum('td,dsf->tsf', normed_mlp, mlp_full, preferred_element_type=jn...]
    reduce_scatter x1 -> x0, waiting for transfers between devices: 142 us -> none  [local(): lax.psum_scatter(dealt_order(buffer[WINDOW_LIMIT:], n_ctx).astype(jnp.bfl...]
    unnamed x168 -> x1, local copies, waits for them, and re-layouts: 76.8 us -> 1.07 us
    dynamic_update_slice x2 -> x0, local copies, waits for them, and re-layouts: 23.2 us -> none  [local(): lax.dynamic_update_slice_in_dim(buffer, current + near_grads[which_half],...]
    slice x10 -> x1, local copies, waits for them, and re-layouts: 22.5 us -> 1.46 us  [local(): idx4 = oi[:, 0, 0, 0]]
  transfers between devices with their start and end apart: 6 -> 0, of which waited for: 6 -> 0; matrix products, arithmetic and copies ran while one was open for 10% -> 0% of each run, Pallas kernels for 0% -> 0%
where the time goes in v1:
time: 511 us; the launch traced here: 504 us
  Pallas kernels  478 us (94%)
  local copies, waits for them, and re-layouts  21 us (4%)
    pallas_call x1, Pallas kernels, weights(): pl.pallas_call(weights_kernel, out_shape=outs, in_specs=[ANY] * 6, out_sp...  154 us
    pallas_call x1, Pallas kernels, total(): pl.pallas_call(total_kernel, out_shape=sds((4, 4, 2, 2, 2, 12, R, 128), B...  66.6 us
    pallas_call x2, Pallas kernels, scatter(): pl.pallas_call(scatter_kernel, out_shape=sds((ROWS, DX), F32), in_specs=[...  59.9 us
    pallas_call x1, Pallas kernels, give_back(): pl.pallas_call(return_kernel, out_shape=sds((2, BLK, 2 * KW), F32), in_sp...  40.2 us
    pallas_call x1, Pallas kernels, feed(): pl.pallas_call(feed_kernel, out_shape=outs, grid_spec=pltpu.PrefetchScala...  39.1 us
    pallas_call x1, Pallas kernels, halo(): pl.pallas_call(halo_kernel, out_shape=sds((16 + NBLK, BLK, 2 * KW), BF),...  27.3 us
    pallas_call x1, Pallas kernels, gather(): pl.pallas_call(gather_kernel, out_shape=sds((2, 2, 2, ROWS, DX), BF), in_...  25.9 us
    pallas_call x1, Pallas kernels, back(): pl.pallas_call(back_kernel, out_shape=outs, grid_spec=pltpu.PrefetchScala...  14.4 us

profile of v1, /device:TPU:1, one launch (start us, length us, event | category | flops | bytes accessed | tf_op | source)
XLA Modules:
  0.0 503.5 jit_solution(12854522228242690852)
XLA Ops:
  6.3 1.3 broadcast_in_dim.48.bias
  7.5 1.4 pad.17.wo
  9.7 1.5 pad.16.wq
  12.2 1.6 pad.19.wd
  13.9 1.8 copy.35
  15.7 1.8 copy.36
  19.4 3.9 shard_map.216
  23.3 154.1 %shard_map.217 = (bf16[2,2,4,2,48,2048]{5,4,3,2,1,0:T(8,128)(2,1)}, bf16[2,2,4,2,48,1536]{5,4,3,2,1,0:T(8,128)(2,1)}, bf16[4,2,2,4,2,48,640]{6,5,4,3,2,1,0:T(8,1...) custom-call(s32[8,128]{1,0:T(8,128)} %broadcast_in_dim.46.idx, ...), custom_call_target="tpu_custom_call" | custom-call | tf_op jit(solution)/shard_map/pallas_call | solution.py:532
  177.4 1.5 slice_reduce_fusion.idx
  178.9 4.9 shard_map.218
  183.8 9.3 %shard_map.222.wd = bf16[1280,1536]{1,0:T(8,128)(2,1)} custom-call(bf16[16,80,1536]{2,1,0:T(8,128)(2,1)} %get-tuple-element.55.wd), custom_call_target="tpu_custom_call" | custom-call | tf_op jit(solution)/shard_map/pallas_call | solution.py:770
  193.1 27.3 %shard_map.219.kv = bf16[80,64,512]{2,1,0:T(8,128)(2,1)} custom-call(bf16[2,64,512]{2,1,0:T(8,128)(2,1)} %get-tuple-element.48.own), custom_call_target="tpu_custom_call" | custom-call | tf_op jit(solution)/shard_map/pallas_call | solution.py:643
  220.4 10.9 %shard_map.220 = (bf16[4,384,1088]{2,1,0:T(8,128)(2,1)}, bf16[128,1536]{1,0:T(8,128)(2,1)}, f32[128,1536]{1,0:T(8,128)}, bf16[128,1664]{1,0:T(8,128)(2,1)}) custom-call(s32[1]{0:T(128)} %copy.45.idx, s32[128,128]{1,0:T(8,128)} %broadcast_in_dim.50.low, bf16[128,1536]{1,0:T(8,128)(2,1)} %get-tuple-element.47.q, bf16[80,64,512]{2,1,0:T(8,128)(2,1)} %shard_map.219.kv, ...), custom_call_target="tpu_custom_call" | custom-call | tf_op jit(solution)/shard_map/pallas_call | solution.py:710
  231.3 25.9 %shard_map.221 = bf16[2,2,2,128,1664]{4,3,2,1,0:T(8,128)(2,1)} custom-call(bf16[128,1664]{1,0:T(8,128)(2,1)} %get-tuple-element.52.own.n2), custom_call_target="tpu_custom_call" | custom-call | tf_op jit(solution)/shard_map/pallas_call | solution.py:748
  257.2 39.1 %shard_map.223 = (bf16[1024,1664]{1,0:T(8,128)(2,1)}, bf16[1024,1664]{1,0:T(8,128)(2,1)}, bf16[128,16,128]{2,1,0:T(8,128)(2,1)}) custom-call(s32[4]{0:T(128)} %slice_reduce_fusion.idx, bf16[1024,1664]{1,0:T(8,128)(2,1)} %bitcast.42, bf16[1024,1664]{1,0:T(8,128)(2,1)} %bitcast.46, bf16[4,1536,640]{2,1,0:T(8,128)(2,1)} %bitcast.43, ...), custom_call_target="tpu_custom_call" | custom-call | tf_op jit(solution)/shard_map/pallas_call | solution.py:846
  296.3 29.9 %shard_map.224.gn2 = f32[128,1664]{1,0:T(8,128)} custom-call(bf16[2,2,2,128,1664]{4,3,2,1,0:T(8,128)(2,1)} %bitcast.45), custom_call_target="tpu_custom_call" | custom-call | tf_op jit(solution)/shard_map/pallas_call | solution.py:905
  326.2 14.4 %shard_map.225 = (f32[128,1536]{1,0:T(8,128)}, f32[128,1536]{1,0:T(8,128)}, bf16[2,17,64,512]{3,2,1,0:T(8,128)(2,1)}, f32[128,1536]{1,0:T(8,128)}, f32[16,1536]{1,0:T(8,128)}, /*index=5*/f32[16,1536]{1,0:T(8,128)}) custom-call(s32[1]{0:T(128)} %copy.45.idx, f32[128,1664]{1,0:T(8,128)} %shard_map.224.gn2, bf16[128,1664]{1,0:T(8,128)(2,1)} %get-tuple-element.42.eext.e, ...), custom_call_target="tpu_custom_call" | custom-call | tf_op jit(solution)/shard_map/pallas_call | solution.py:976
  340.5 40.2 %shard_map.226.gkv = f32[2,64,512]{2,1,0:T(8,128)} custom-call(bf16[2,17,64,512]{3,2,1,0:T(8,128)(2,1)} %get-tuple-element.60.win), custom_call_target="tpu_custom_call" | custom-call | tf_op jit(solution)/shard_map/pallas_call | solution.py:1087
  380.7 30.0 %shard_map.227.y = f32[128,1664]{1,0:T(8,128)} custom-call(bf16[2,2,2,128,1664]{4,3,2,1,0:T(8,128)(2,1)} %bitcast.44), custom_call_target="tpu_custom_call" | custom-call | tf_op jit(solution)/shard_map/pallas_call | solution.py:905
  410.8 9.8 %shard_map.228 = (bf16[128,1536]{1,0:T(8,128)(2,1)}, bf16[128,1536]{1,0:T(8,128)(2,1)}, bf16[128,16,128]{2,1,0:T(8,128)(2,1)}) custom-call(s32[1]{0:T(128)} %copy.45.idx, f32[2,64,512]{2,1,0:T(8,128)} %shard_map.226.gkv, f32[128,1536]{1,0:T(8,128)} %get-tuple-element.61.gq, bf16[128,1536]{1,0:T(8,128)(2,1)} %get-tuple-element.49.x, ...), custom_call_target="tpu_custom_call" | custom-call | tf_op jit(solution)/shard_map/pallas_call | solution.py:1149
  420.6 2.1 copy.44
  422.7 2.1 copy.43
  424.8 66.6 %shard_map.229.t = bf16[4,4,2,2,2,12,16,128]{7,6,5,4,3,2,1,0:T(8,128)(2,1)} custom-call(bf16[128,16,128]{2,1,0:T(8,128)(2,1)} %get-tuple-element.70.lt, bf16[128,16,128]{2,1,0:T(8,128)(2,1)} %get-tuple-element.71.ft), custom_call_target="tpu_custom_call" | custom-call | tf_op jit(solution)/shard_map/pallas_call | solution.py:1288
  491.4 11.8 %shard_map.230 = (f32[8,6,16,1536]{3,2,1,0:T(8,128)}, f32[8,16,8960]{2,1,0:T(8,128)}, f32[8,16,2048]{2,1,0:T(8,128)}, f32[8,2,16,1536]{3,2,1,0:T(8,128)}, f32[8,2,16,8960]{3,2,1,0:T(8,128)}) custom-call(s32[4]{0:T(128)} %slice_reduce_fusion.idx, bf16[4,4,2,2,2,12,16,128]{7,6,5,4,3,2,1,0:T(8,128)(2,1)} %shard_map.229.t), custom_call_target="tpu_custom_call" | custom-call | tf_op jit(solution)/shard_map/pallas_call | solution.py:1363
  (15 shorter events, 8.0 us)

commit v2 on v1

--- a/solution.py
+++ b/solution.py
@@ -184,23 +184,27 @@
     return lax.rsqrt(jnp.mean(z * z, -1, keepdims=True) + EPS)
 
 
-def prepare_kernel(idx, tok, cot, a_in, b_qkv_ad, b_res, gain, bias, x_o, n1_o, e_o, ub_o, a45_o, bd_o):
+def prepare_kernel(idx, tok, cot, a_in, b_qkv_ad, b_res, gain, bias, x_o, n1_o, e_o, ub_o, a45_o, bd_o, a3_o, bo_o):
     s = lax.axis_index("dp")
-    x = tok[...].astype(F32)
-    x_o[...] = tok[...]
+    for h in range(2):
+        rows = slice(h * BLK, (h + 1) * BLK)
+        x_o[rows] = tok[:, h, :]
+        e_o[rows, :D] = cot[:, h, :]
+    x = x_o[...].astype(F32)
     n1 = (x * rms(x) * gain[...].astype(F32)).astype(BF)
     n1_o[...] = n1
     for m, (lo, hi) in enumerate(((0, QW), (QW, QW + KW), (QW + KW, QW + 2 * KW))):
         u = nt(n1, a_in[0, m]).astype(BF)
-        ub_o[:, lo:hi] = mm(u, b_qkv_ad[0, :, lo:hi]) + bias[:, lo:hi].astype(F32)
+        ub_o[:, lo:hi] = mm(u, b_qkv_ad[0, :, lo:hi]) + bias[lo:hi].astype(F32)
     at = pl.multiple_of(s * R, R)
     a45_o[...] = jnp.zeros_like(a45_o)
     a45_o[pl.ds(at, R), :] = a_in[0, 4]
     a45_o[pl.ds(at + 64, R), :] = a_in[0, 5]
     bd_o[...] = jnp.zeros_like(bd_o)
     bd_o[pl.ds(at, R), :] = b_res[0, 1]
-    e_o[:, :D] = cot[...]
-    e_o[:, D:] = nt(cot[...], bd_o[...]).astype(BF)
+    a3_o[...] = a_in[0, 3]
+    bo_o[...] = b_res[0, 0]
+    e_o[:, D:] = nt(e_o[:, :D], bd_o[...]).astype(BF)
 
 
 def pick(shape):
@@ -219,6 +223,8 @@
         sds((ROWS, 2048), F32),
         sds((EXT, D), BF),
         sds((EXT, D), BF),
+        sds((R, D), BF),
+        sds((R, D), BF),
     )
     return pl.pallas_call(
         prepare_kernel,
@@ -227,13 +233,13 @@
             num_scalar_prefetch=1,
             grid=(1,),
             in_specs=[
-                whole((ROWS, D)),
-                whole((ROWS, D)),
+                whole((BLK, 2, D)),
+                whole((BLK, 2, D)),
                 pick(a_in.shape),
                 pick(b_qkv_ad.shape),
                 pick(b_res.shape),
-                whole((1, D)),
-                whole((1, 2048)),
+                whole((D,)),
+                whole((2048,)),
             ],
             out_specs=[whole(o.shape) for o in outs],
         ),
@@ -241,17 +247,37 @@
     )(idx, tok, cot, a_in, b_qkv_ad, b_res, gain, bias)
 
 
-def weights_kernel(
-    idx, wq, wo, wg, wd, eext,
-    oq, oo, og, od, oe, oi,
-    rq, ro, rg, cq, co, cg,
-    ss, rs, ls, s1, r1, s2, r2, sc, rc_, sd, rd, se, re_, ce, cre, si, ri,
+def turn(v, cos, sin):
+    return v * cos + pltpu.roll(v, 64, 1) * sin
+
+
+def turn_back(v, cos, sin):
+    return v * cos - pltpu.roll(v, 64, 1) * sin
+
+
+def stack_heads(ref, h, a):
+    rows = slice(h * BLK, (h + 1) * BLK)
+    return jnp.concatenate(
+        [ref[rows, (a * GROUP + g) * HS : (a * GROUP + g + 1) * HS] for g in range(GROUP)], 0
+    )
+
+
+def reads(t, block):
+    a, b = t - block, NBLK - 1 - t - block
+    return ((a >= 0) & (a < NWB)) | ((b >= 0) & (b < NWB))
+
+
+ZK = [(dz, dc) for dz in range(4) for dc in range(2) if dz or dc]
+
+
+def front_kernel(
+    idx, wq_i, wo_i, wg, wd_i, eext, n1, ub, cos, sin, low, x, gain, a45, a3, bo,
+    oq_o, oo_o, og, od_o, oe, oi, win_o, p_o, xg, q, o_o, hid_o, n2,
+    rq, ro, rg, wdp, rd, cq, co, cg, oq, oo, od, kv_own, kv, p, down,
+    ss, rs, ls, s1, r1, s2, r2, sc, rc, sd, rdn, sk, rk, ez_sems, si, ri, nz_sems,
 ):
     me = Place()
     sib = me.sibling()
-    zpeers = [
-        me.at(z=me.step("z", dz), core=lax.rem(me.core + dc, 2)) for dz in range(4) for dc in range(2) if dz or dc
-    ]
     m = me.ctx
     bar = pltpu.get_barrier_semaphore()
 
@@ -263,162 +289,167 @@
         return carry
 
     lax.fori_loop(0, N_CTX, hello, 0)
-    others = [
-        me.at(z=me.step("z", dz), core=lax.rem(me.core + dc, 2)) for dz in range(4) for dc in range(2) if dz % 2 or dc
-    ]
+    others = [me.at(z=me.step("z", dz), core=lax.rem(me.core + dc, 2)) for dz, dc in ZK if dz % 2 or dc]
     for d in others:
         pl.semaphore_signal(bar, inc=1, device_id=d, device_id_type=MESH)
+
+    rq[me.x, :12] = wq_i[...]
+    rq[me.x, 12:] = jnp.zeros((4, 2048), BF)
+    ro[me.x, :12] = wo_i[...]
+    ro[me.x, 12:] = jnp.zeros((4, D), BF)
+    wdp[:70] = wd_i[...]
+    wdp[70:] = jnp.zeros((10, D), BF)
+    kv[:16] = jnp.zeros((16, BLK, 2 * KW), BF)
+
     pl.semaphore_wait(bar, N_CTX - 1 + len(others))
 
+    tiles = [60 if g == 7 else 35 * g // 4 for g in range(8)]
+
+    def panel(g, t):
+        col = pl.multiple_of(tiles[g] * 128 + lax.rem(t, 2) * 640, 128)
+        return wg.at[lax.div(t, 2), :, pl.ds(col, 640)]
+
+    def strip(t):
+        return wdp.at[:, pl.ds(pl.multiple_of(384 * t, 128), 384)]
+
+    def start(c, out):
+        c.start()
+        out.append(c)
+
     first = []
-    for k in (1, 2, 3):
-        t = me.step("x", k)
-        d = me.at(x=t)
-        for n, (src, dst) in enumerate(((wq, rq.at[me.x]), (wo, ro.at[me.x]))):
-            first.append(remote(src, dst, s1.at[k - 1, n], r1.at[k - 1, n], d))
+    xs = [(k, me.step("x", k), me.at(x=me.step("x", k))) for k in (1, 3, 2)]
+    for k, t, d in xs:
+        start(remote(rq.at[me.x], rq.at[me.x], s1.at[k - 1, 0], r1.at[k - 1, 0], d), first)
+    ez = ZGather(me, eext, oe, *ez_sems, BLK)
+    ez.first()
+    for k, t, d in xs:
+        start(remote(ro.at[me.x], ro.at[me.x], s1.at[k - 1, 1], r1.at[k - 1, 1], d), first)
+    for k, t, d in xs:
         for g in range(8):
-            tile = 60 if g == 7 else 35 * g // 4
-            col = pl.multiple_of(tile * 128 + lax.rem(t, 2) * 640, 128)
-            src = wg.at[lax.div(t, 2), :, pl.ds(col, 640)]
-            first.append(remote(src, rg.at[me.x, g], s1.at[k - 1, 2 + g], r1.at[k - 1, 2 + g], d))
-    for c in first:
-        c.start()
-    mine = [
-        pltpu.make_async_copy(wq, rq.at[me.x], ls.at[0]),
-        pltpu.make_async_copy(wo, ro.at[me.x], ls.at[1]),
-    ]
+            start(remote(panel(g, t), rg.at[me.x, g], s1.at[k - 1, 2 + g], r1.at[k - 1, 2 + g], d), first)
+        start(remote(strip(t), rd.at[me.x], s1.at[k - 1, 10], r1.at[k - 1, 10], d), first)
+    mine = []
     for g in range(8):
-        tile = 60 if g == 7 else 35 * g // 4
-        col = pl.multiple_of(tile * 128 + lax.rem(me.x, 2) * 640, 128)
-        mine.append(
-            pltpu.make_async_copy(wg.at[lax.div(me.x, 2), :, pl.ds(col, 640)], rg.at[me.x, g], ls.at[2 + g])
-        )
-    for c in mine:
-        c.start()
-    ez = ZGather(me, eext, oe, se, re_, ce, cre, BLK)
-    ez.first()
-    own_e = pltpu.make_async_copy(eext, oe.at[me.zlo, me.core, me.zhi], ls.at[10])
-    own_e.start()
-    own_i = pltpu.make_async_copy(idx, oi.at[me.dp, me.zhi], ls.at[11])
-    own_i.start()
-    ic = []
-    for n, d in enumerate(zpeers):
-        c = remote(idx, oi.at[me.dp, me.zhi], si.at[n], ri.at[n], d)
-        c.start()
-        ic.append(c)
-
-    for c in mine:
-        c.wait()
-    for k in (1, 2, 3):
-        f = me.step("x", 4 - k)
-        d = me.at(x=f)
-        for n, ref in enumerate((rq.at[f], ro.at[f])):
-            remote(ref, ref, s1.at[k - 1, n], r1.at[k - 1, n], d).wait_recv()
-        for g in range(8):
-            ref = rg.at[f, g]
-            remote(ref, ref, s1.at[k - 1, 2 + g], r1.at[k - 1, 2 + g], d).wait_recv()
+        start(pltpu.make_async_copy(panel(g, me.x), rg.at[me.x, g], ls.at[2 + g]), mine)
+    start(pltpu.make_async_copy(strip(me.x), rd.at[me.x], ls.at[1]), mine)
+    side = []
+    start(pltpu.make_async_copy(eext, oe.at[me.zlo, me.core, me.zhi], ls.at[10]), side)
+    start(pltpu.make_async_copy(idx, oi.at[me.dp, me.zhi], ls.at[11]), side)
+    for n, (dz, dc) in enumerate(ZK):
+        d = me.at(z=me.step("z", dz), core=lax.rem(me.core + dc, 2))
+        start(remote(idx, oi.at[me.dp, me.zhi], si.at[n], ri.at[n], d), first)
+
+    def from_x(n, ref_of):
+        for k in (1, 3, 2):
+            f = me.step("x", 4 - k)
+            ref = ref_of(f)
+            remote(ref, ref, s1.at[k - 1, n], r1.at[k - 1, n], me.at(x=f)).wait_recv()
+
     row, col = iota((48, 64), 0), iota((48, 64), 1)
     put = jnp.where(
         (lax.rem(col, 16) < 12) & (lax.div(col, 16) * 12 + lax.rem(col, 16) == row), 1.0, 0.0
     ).astype(BF)
+
+    from_x(0, lambda f: rq.at[f])
     cq[...] = mm(put, rq[...].reshape(64, 2048)).astype(BF)
+    lo, hi = pl.ds(0, 1024), pl.ds(1024, 1024)
+
+    def qy0(j, h):
+        return oq.at[me.zlo, me.core, j, me.zhi, :, lo if h is None else pl.ds(512 * h, 512)]
+
+    def qz0(j, h, core=me.core):
+        zl, zh = lax.rem(j, 2), lax.div(j, 2)
+        return oq.at[zl, core, :, zh, :, lo] if h is None else oq.at[zl, core, pl.ds(2 * h, 2), zh, :, lo]
+
+    def qz1(j, h):
+        cols = hi if h is None else pl.ds(1024 + 512 * h, 512)
+        return oq.at[lax.rem(j, 2), me.core, me.y, lax.div(j, 2), :, cols]
+
+    def qy1(j, h, core=me.core):
+        return oq.at[:, core, j, :, :, hi] if h is None else oq.at[h, core, j, :, :, hi]
+
+    qa = Ring(me, "y", cq.at[:, lo], qy0, ss.at[0], rs.at[0])
+    qb = Ring(me, "z", cq.at[:, hi], qz1, ss.at[1], rs.at[1])
+    qa.first()
+    qb.first()
+    oq[me.zlo, me.core, me.y, me.zhi] = cq[...]
+    from_x(1, lambda f: ro.at[f])
     co[...] = mm(put, ro[...].reshape(64, D)).astype(BF)
-
-    def vy0(j, h):
-        ref = oq.at[me.zlo, me.core, j, me.zhi]
-        return ref if h is None else ref.at[:, pl.ds(1024 * h, 1024)]
-
-    def vz0(j, h, core=me.core):
-        zl, zh = lax.rem(j, 2), lax.div(j, 2)
-        return oq.at[zl, core, :, zh] if h is None else oq.at[zl, core, pl.ds(2 * h, 2), zh]
-
-    def vz1(j, h):
-        ref = oo.at[lax.rem(j, 2), me.core, me.y, lax.div(j, 2)]
-        return ref if h is None else ref.at[:, pl.ds(768 * h, 768)]
-
-    def vy1(j, h, core=me.core):
-        return oo.at[:, core, j] if h is None else oo.at[h, core, j]
-
-    ra = Ring(me, "y", cq, vy0, ss.at[0], rs.at[0])
-    rb = Ring(me, "z", co, vz1, ss.at[1], rs.at[1])
-    ra.first()
-    rb.first()
-    own = [
-        pltpu.make_async_copy(cq, oq.at[me.zlo, me.core, me.y, me.zhi], ls.at[12]),
-        pltpu.make_async_copy(co, oo.at[me.zlo, me.core, me.y, me.zhi], ls.at[13]),
-    ]
-    for c in own:
-        c.start()
+    for n in range(8):
+        from_x(2 + n, lambda f: rg.at[f, n])
+    from_x(10, lambda f: rd.at[f])
+    for c in mine:
+        c.wait()
     for g in range(8):
         cg[g] = mm(put, rg[:, g].reshape(64, 640)).astype(BF)
-    own_g = pltpu.make_async_copy(
-        cg.at[me.slice], og.at[me.x, me.zlo, me.core, me.y, me.zhi], ls.at[14]
-    )
+    qa.second()
+    qb.second()
+
+    own_g = pltpu.make_async_copy(cg.at[me.slice], og.at[me.x, me.zlo, me.core, me.y, me.zhi], ls.at[14])
     own_g.start()
     zc = []
-    zk = [(dz, dc) for dz in range(4) for dc in range(2) if dz or dc]
-    for n, (dz, dc) in enumerate(zk):
+    for n, (dz, dc) in enumerate(ZK):
         z, core = me.step("z", dz), lax.rem(me.core + dc, 2)
         piece = 2 * (2 * lax.rem(z, 2) + core) + lax.div(z, 2)
-        c = remote(
-            cg.at[piece], og.at[me.x, me.zlo, me.core, me.y, me.zhi], s2.at[n], r2.at[n], me.at(z=z, core=core)
-        )
-        c.start()
-        zc.append(c)
-    zr = lax.div(me.y, 2)
-    slot = lax.rem(me.y, 2) * 8 + me.zhi * 4 + me.x
-
-    def down(k, wait):
-        t = lax.rem(m + k, N_CTX)
-
-        @pl.when(lax.rem(lax.div(t, 4), 2) == zr)
-        def _():
-            c = remote(wd, od.at[slot], sd.at[k], rd.at[slot], (me.dp, t))
-            if wait:
-                c.wait_send()
-            else:
-                c.start()
-
-    def down_send(k, carry):
-        down(k, False)
-        return carry
-
-    def down_sent(k, carry):
-        down(k, True)
-        return carry
-
-    lax.fori_loop(1, N_CTX, down_send, 0)
-
-    @pl.when(me.zhi == zr)
+        d = me.at(z=z, core=core)
+        start(remote(cg.at[piece], og.at[me.x, me.zlo, me.core, me.y, me.zhi], s2.at[n], r2.at[n], d), zc)
+    keeper = lax.div(me.y, 2) == me.zhi
+    rows4 = pl.ds(lax.rem(me.y, 2) * 8 + me.zhi * 4, 4)
+    across = me.at(z=me.step("z", 2))
+    d_local = pltpu.make_async_copy(rd, od.at[me.x, rows4], ls.at[15])
+    d_cross = remote(rd, od.at[me.x, rows4], sd.at[0], rdn.at[0], across)
+
+    @pl.when(keeper)
     def _():
-        c = pltpu.make_async_copy(wd, od.at[slot], ls.at[15])
-        c.start()
-        c.wait()
-
-    ra.second()
-    rb.second()
-    ez.second()
-    ra.last()
-    rb.last()
-    for c in own:
-        c.wait()
-    ra2 = Ring(me, "z", vz0(me.z, None), vz0, ss.at[2], rs.at[2])
-    rb2 = Ring(me, "y", vy1(me.y, None), vy1, ss.at[3], rs.at[3])
-    ra2.first()
-    rb2.first()
+        d_local.start()
+
+    @pl.when(jnp.logical_not(keeper))
+    def _():
+        d_cross.start()
+
+    qa.last()
+    qb.last()
+    qa2 = Ring(me, "z", qz0(me.z, None), qz0, ss.at[2], rs.at[2])
+    qb2 = Ring(me, "y", qy1(me.y, None), qy1, ss.at[3], rs.at[3])
+    qa2.first()
+    qb2.first()
     swaps = []
 
     def swap(view, j):
         n = len(swaps)
-        c = remote(view(j, None), view(j, None), sc.at[n], rc_.at[n], sib)
+        c = remote(view(j, None), view(j, None), sc.at[n], rc.at[n], sib)
         c.start()
         swaps.append((c, view, j))
 
-    swap(vz0, me.z)
-    swap(vy1, me.y)
+    def swapped(n):
+        c, view, j = swaps[n]
+        c.wait_send()
+        ref = view(j, None, 1 - me.core)
+        remote(ref, ref, sc.at[n], rc.at[n], sib).wait_recv()
+
+    swap(qz0, me.z)
+    swap(qy1, me.y)
+    ez.second()
+    def oy(j, h):
+        ref = oo.at[me.zlo, me.core, j, me.zhi]
+        return ref if h is None else ref.at[:, pl.ds(768 * h, 768)]
+
+    def oz(j, h, core=me.core):
+        zl, zh = lax.rem(j, 2), lax.div(j, 2)
+        return oo.at[zl, core, :, zh] if h is None else oo.at[zl, core, pl.ds(2 * h, 2), zh]
+
+    wa = Ring(me, "y", co, oy, ss.at[8], rs.at[8])
+    qa2.second()
+    qb2.second()
+    swap(qz0, qa2.l)
+    swap(qy1, qb2.l)
+    swap(qz0, qa2.r)
+    swap(qy1, qb2.r)
+    wa.first()
+    oo[me.zlo, me.core, me.y, me.zhi] = co[...]
 
     own_g.wait()
-    for n, (dz, dc) in enumerate(zk):
+    for n, (dz, dc) in enumerate(ZK):
         z, core = me.step("z", 4 - dz if dz else 0), lax.rem(me.core + dc, 2)
         ref = og.at[me.x, lax.rem(z, 2), core, me.y, lax.div(z, 2)]
         remote(ref, ref, s2.at[n], r2.at[n], me.at(z=z, core=core)).wait_recv()
@@ -439,341 +470,277 @@
     gb = Ring(me, "x", g1a(me.x, None), g1a, ss.at[5], rs.at[5])
     ga.first()
     gb.first()
-    ra2.second()
-    rb2.second()
-    swap(vz0, ra2.l)
-    swap(vy1, rb2.l)
-    swap(vz0, ra2.r)
-    swap(vy1, rb2.r)
+    qa2.last()
+    qb2.last()
+    swap(qz0, qa2.o)
+    swap(qy1, qb2.o)
+
+    rows4b = pl.ds(lax.rem(me.y, 2) * 8 + (1 - me.zhi) * 4, 4)
+    rows8 = pl.ds(lax.rem(me.y, 2) * 8, 8)
+    ys = [(k, me.step("y", k)) for k in (1, 3, 2)]
+
+    @pl.when(keeper)
+    def _():
+        d_local.wait()
+        ref = od.at[me.x, rows4b]
+        remote(rd, ref, sd.at[0], rdn.at[0], across).wait_recv()
+        for k, t in ys:
+            remote(od.at[me.x, rows8], od.at[me.x, rows8], sd.at[k], rdn.at[k], me.at(y=t)).start()
+
+    wa.second()
     ga.second()
     gb.second()
+    for n in range(8):
+        swapped(n)
+    keep_q = pltpu.make_async_copy(oq, oq_o, ls.at[12])
+    keep_q.start()
+
+    c, s = cos[...], sin[...]
+    n1v = n1[...]
+    for h in (12, 14, 0, 2, 4, 6, 8, 10):
+        pair = slice(h * HS, (h + 2) * HS)
+        j = mm(n1v, oq[:, :, :, :, :, pair].reshape(D, 2 * HS)) + ub[:, pair]
+        for i in range(2):
+            v = j[:, i * HS : (i + 1) * HS]
+            if h + i < HEADS + KV_HEADS:
+                v = turn(v, c, s)
+            v = v.astype(BF)
+            if h + i < HEADS:
+                q[:, (h + i) * HS : (h + i + 1) * HS] = v
+            else:
+                at = slice((h + i - HEADS) * HS, (h + i - HEADS + 1) * HS)
+                kv_own[0, :, at] = v[:BLK]
+                kv_own[1, :, at] = v[BLK:]
+        if h == 14:
+            def send(k, carry):
+                t = lax.rem(m + k, N_CTX)
+                for half in range(2):
+                    block = m if half == 0 else NBLK - 1 - m
+
+                    @pl.when(reads(t, block))
+                    def _():
+                        src, dst = kv_own.at[half], kv.at[16 + block]
+                        remote(src, dst, sk.at[half, k], rk.at[block], (me.dp, t)).start()
+
+                return carry
+
+            lax.fori_loop(1, N_CTX, send, 0)
+            kv[16 + m] = kv_own[0]
+            kv[16 + NBLK - 1 - m] = kv_own[1]
+
+    wa.last()
+    wb = Ring(me, "z", oz(me.z, None), oz, ss.at[9], rs.at[9])
+    wb.first()
+    swap(oz, me.z)
     ga.last()
     gb.last()
     ga2 = Ring(me, "x", g0b(me.x, None), g0b, ss.at[6], rs.at[6])
     gb2 = Ring(me, "y", g1b(me.y, None), g1b, ss.at[7], rs.at[7])
     ga2.first()
     gb2.first()
-    ra2.last()
-    rb2.last()
-    swap(vz0, ra2.o)
-    swap(vy1, rb2.o)
-    ez.last()
-    ga2.second()
-    gb2.second()
-    ga2.last()
-    gb2.last()
-
-    for r in (ra, rb, ra2, rb2, ga, gb, ga2, gb2):
-        r.sent()
-    for c in first:
-        c.wait_send()
-    for c in zc:
-        c.wait_send()
-    for n, (c, view, j) in enumerate(swaps):
-        c.wait_send()
-        ref = view(j, None, 1 - me.core)
-        remote(ref, ref, sc.at[n], rc_.at[n], sib).wait_recv()
-    ez.finish()
-    own_e.wait()
-    own_i.wait()
-    for n, (dz, dc) in enumerate(zk):
-        z, core = me.step("z", 4 - dz if dz else 0), lax.rem(me.core + dc, 2)
-        ic[n].wait_send()
-        ref = oi.at[2 * lax.rem(z, 2) + core, lax.div(z, 2)]
-        remote(ref, ref, si.at[n], ri.at[n], me.at(z=z, core=core)).wait_recv()
-    lax.fori_loop(1, N_CTX, down_sent, 0)
-
-    def down_got(n, carry):
-        src = (2 * me.zhi + lax.div(n, 8)) * 8 + lax.rem(n, 8)
-
-        @pl.when(src != m)
+
+    def arrived(block):
+        src = jnp.where(block < N_CTX, block, NBLK - 1 - block)
+        remote(kv_own.at[0], kv.at[16 + block], sk.at[0, 0], rk.at[block], (me.dp, src)).wait_recv()
+
+    def near0(j, carry):
+        block = m - (NWB - 1) + j
+
+        @pl.when(block >= 0)
         def _():
-            remote(wd, od.at[n], sd.at[0], rd.at[n], (me.dp, src)).wait_recv()
+            arrived(block)
 
         return carry
 
-    lax.fori_loop(0, 16, down_got, 0)
-
-
-def weights(idx, wq, wo, wg, wd, eext):
-    outs = (
-        sds((2, 2, 4, 2, 48, 2048), BF),
-        sds((2, 2, 4, 2, 48, D), BF),
-        sds((4, 2, 2, 4, 2, 48, 640), BF),
-        sds((16, 80, D), BF),
-        sds((2, 2, 2, ROWS, DX), BF),
-        sds((4, 2, 8, 128), jnp.int32),
-    )
-    scratch = [
-        pltpu.VMEM((4, 16, 2048), BF),
-        pltpu.VMEM((4, 16, D), BF),
-        pltpu.VMEM((4, 8, 16, 640), BF),
-        pltpu.VMEM((48, 2048), BF),
-        pltpu.VMEM((48, D), BF),
-        pltpu.VMEM((8, 48, 640), BF),
-        DMA((8, 4)),
-        DMA((8, 4)),
-        DMA((16,)),
-        DMA((3, 10)),
-        DMA((3, 10)),
-        DMA((7,)),
-        DMA((7,)),
-        DMA((8,)),
-        DMA((8,)),
-        DMA((N_CTX,)),
-        DMA((16,)),
-        DMA((4,)),
-        DMA((4,)),
-        DMA((4,)),
-        DMA((4,)),
-        DMA((7,)),
-        DMA((7,)),
-    ]
-    return pl.pallas_call(
-        weights_kernel,
-        out_shape=outs,
-        in_specs=[ANY] * 6,
-        out_specs=[ANY] * 6,
-        scratch_shapes=scratch,
-        compiler_params=pltpu.CompilerParams(collective_id=1, has_side_effects=True, vmem_limit_bytes=VMEM_LIMIT),
-    )(idx, wq, wo, wg, wd, eext)
-
-
-def turn(v, cos, sin):
-    return v * cos + pltpu.roll(v, 64, 1) * sin
-
-
-def turn_back(v, cos, sin):
-    return v * cos - pltpu.roll(v, 64, 1) * sin
-
-
-def qkv_kernel(n1, w, ub, cos, sin, q_o, kv_o):
-    c, s = cos[...], sin[...]
-    for h in range(HEADS + 2 * KV_HEADS):
-        cols = slice(h * HS, (h + 1) * HS)
-        if h % 2 == 0:
-            pair = slice(h * HS, (h + 2) * HS)
-            j = mm(n1[...], w[:, pair]) + ub[:, pair]
-        v = j[:, (h % 2) * HS : (h % 2 + 1) * HS]
-        if h < HEADS + KV_HEADS:
-            v = turn(v, c, s)
-        v = v.astype(BF)
-        if h < HEADS:
-            q_o[:, cols] = v
-        else:
-            at = slice((h - HEADS) * HS, (h - HEADS + 1) * HS)
-            kv_o[0, :, at] = v[:BLK]
-            kv_o[1, :, at] = v[BLK:]
-
-
-def qkv(n1, w, ub, cos, sin):
-    return pl.pallas_call(
-        qkv_kernel,
-        out_shape=(sds((ROWS, D), BF), sds((2, BLK, 2 * KW), BF)),
-        in_specs=[VM] * 5,
-        out_specs=[VM] * 2,
-        compiler_params=pltpu.CompilerParams(vmem_limit_bytes=VMEM_LIMIT),
-    )(n1, w, ub, cos, sin)
-
-
-def reads(t, block):
-    a, b = t - block, NBLK - 1 - t - block
-    return ((a >= 0) & (a < NWB)) | ((b >= 0) & (b < NWB))
-
-
-def halo_kernel(own, out, zero, ss, rs, ls):
-    me = Place()
-    m = me.ctx
-    bar = pltpu.get_barrier_semaphore()
-
-    def hello(t, carry):
-        @pl.when(t != m)
+    def near1(j, carry):
+        block = NBLK - 1 - m - (NWB - 1) + j
+
+        @pl.when(block > m)
         def _():
-            pl.semaphore_signal(bar, inc=1, device_id=(me.dp, t), device_id_type=MESH)
+            arrived(block)
 
         return carry
 
-    lax.fori_loop(0, N_CTX, hello, 0)
-    zero[...] = jnp.zeros_like(zero)
-    local = [
-        pltpu.make_async_copy(own.at[0], out.at[16 + m], ls.at[0]),
-        pltpu.make_async_copy(own.at[1], out.at[16 + NBLK - 1 - m], ls.at[1]),
-        pltpu.make_async_copy(zero, out.at[pl.ds(0, 16)], ls.at[2]),
-    ]
-    for c in local:
-        c.start()
-    pl.semaphore_wait(bar, N_CTX - 1)
-
-    def send(k, carry):
-        t = lax.rem(m + k, N_CTX)
-        for h in range(2):
-            block = m if h == 0 else NBLK - 1 - m
-
-            @pl.when(reads(t, block))
-            def _():
-                remote(own.at[h], out.at[16 + block], ss.at[h, k], rs.at[block], (me.dp, t)).start()
-
-        return carry
-
-    lax.fori_loop(1, N_CTX, send, 0)
-
-    def wait(k, carry):
-        t = lax.rem(m + k, N_CTX)
-        for h in range(2):
-            block = m if h == 0 else NBLK - 1 - m
-
-            @pl.when(reads(t, block))
-            def _():
-                remote(own.at[h], out.at[16 + block], ss.at[h, k], rs.at[block], (me.dp, t)).wait_send()
-
-            theirs = t if h == 0 else NBLK - 1 - t
-
-            @pl.when(reads(m, theirs))
-            def _():
-                remote(own.at[h], out.at[16 + theirs], ss.at[h, k], rs.at[theirs], (me.dp, t)).wait_recv()
-
-        return carry
-
-    lax.fori_loop(1, N_CTX, wait, 0)
-    for c in local:
-        c.wait()
-
-
-def halo(kv):
-    return pl.pallas_call(
-        halo_kernel,
-        out_shape=sds((16 + NBLK, BLK, 2 * KW), BF),
-        in_specs=[ANY],
-        out_specs=ANY,
-        scratch_shapes=[pltpu.VMEM((16, BLK, 2 * KW), BF), DMA((2, N_CTX)), DMA((NBLK,)), DMA((3,))],
-        compiler_params=pltpu.CompilerParams(collective_id=2, has_side_effects=True, vmem_limit_bytes=VMEM_LIMIT),
-    )(kv)
-
-
-def load_windows(kv, win, sem):
-    m = lax.axis_index("ctx")
-    copies = [
-        pltpu.make_async_copy(kv.at[pl.ds(m, NWB)], win.at[0], sem.at[0]),
-        pltpu.make_async_copy(kv.at[pl.ds(NBLK - 1 - m, NWB)], win.at[1], sem.at[1]),
-    ]
-    for c in copies:
-        c.start()
-    return copies
-
-
-def stack_heads(ref, h, a):
-    rows = slice(h * BLK, (h + 1) * BLK)
-    return jnp.concatenate(
-        [ref[rows, (a * GROUP + g) * HS : (a * GROUP + g + 1) * HS] for g in range(GROUP)], 0
-    )
-
-
-def attend_kernel(idx, low, q, kv, x, w_out, a_in, b_res, gain, a45, p_o, o_o, h_o, n2_o, win, sem):
-    m = lax.axis_index("ctx")
-    copies = load_windows(kv, win, sem)
+    wins = []
+    keep_p = []
     for h in range(2):
-        copies[h].wait()
+        lax.fori_loop(0, NWB - 1, near0 if h == 0 else near1, 0)
+        win = kv.at[pl.ds(m if h == 0 else NBLK - 1 - m, NWB)]
+        start(pltpu.make_async_copy(win, win_o.at[h], ls.at[16 + h]), wins)
         base = (m if h == 0 else NBLK - 1 - m) * BLK
         kpos = base - WIN + iota((BLK, KEYS), 1)
         qpos = base + iota((BLK, KEYS), 0)
         keep = (kpos <= qpos) & (kpos >= low[h * BLK : (h + 1) * BLK, :1])
         for a in range(KV_HEADS):
             qs = stack_heads(q, h, a)
-            k = win[h, :, :, a * HS : (a + 1) * HS].reshape(KEYS, HS)
-            v = win[h, :, :, KW + a * HS : KW + (a + 1) * HS].reshape(KEYS, HS)
-            sc = nt(qs, k) * SCALE
-            sc = jnp.where(keep[None], sc.reshape(GROUP, BLK, KEYS), -1e30)
-            e = jnp.exp(sc - jnp.max(sc, -1, keepdims=True))
-            p = (e / jnp.sum(e, -1, keepdims=True)).astype(BF).reshape(GROUP * BLK, KEYS)
-            p_o[2 * h + a] = p
-            o = mm(p, v).astype(BF)
+            k = win[:, :, a * HS : (a + 1) * HS].reshape(KEYS, HS)
+            v = win[:, :, KW + a * HS : KW + (a + 1) * HS].reshape(KEYS, HS)
+            sco = nt(qs, k) * SCALE
+            sco = jnp.where(keep[None], sco.reshape(GROUP, BLK, KEYS), -1e30)
+            e = jnp.exp(sco - jnp.max(sco, -1, keepdims=True))
+            pr = (e / jnp.sum(e, -1, keepdims=True)).astype(BF).reshape(GROUP * BLK, KEYS)
+            p[2 * h + a] = pr
+            o = mm(pr, v).astype(BF)
             for g in range(GROUP):
                 o_o[h * BLK : (h + 1) * BLK, (a * GROUP + g) * HS : (a * GROUP + g + 1) * HS] = o[
                     g * BLK : (g + 1) * BLK
                 ]
-    o = o_o[...]
-    u3 = nt(o, a_in[0, 3]).astype(BF)
-    hid = x[...].astype(F32) + mm(o, w_out[...]) + mm(u3, b_res[0, 0])
-    h_o[...] = hid
-    n2 = (hid * rms(hid) * gain[...].astype(F32)).astype(BF)
-    n2_o[:, :D] = n2
-    n2_o[:, D:] = nt(n2, a45[...]).astype(BF)
-
-
-def attend(idx, low, q, kv, x, w_out, a_in, b_res, gain, a45):
+        if h == 0:
+            wb.second()
+            swap(oz, wb.l)
+            swap(oz, wb.r)
+
+    start(pltpu.make_async_copy(p, p_o, ls.at[18]), keep_p)
+    wb.last()
+    swap(oz, wb.o)
+    def dx(j, h):
+        return od.at[j] if h is None else od.at[j, pl.ds(8 * h, 8)]
+
+    for k, t in ys:
+        f = me.step("y", 4 - k)
+
+        @pl.when(lax.div(f, 2) == me.zhi)
+        def _():
+            ref = od.at[me.x, pl.ds(lax.rem(f, 2) * 8, 8)]
+            remote(ref, ref, sd.at[k], rdn.at[k], me.at(y=f)).wait_recv()
+
+    da = Ring(me, "x", od.at[me.x], dx, ss.at[10], rs.at[10])
+    da.first()
+    for n in range(8, 12):
+        swapped(n)
+    keep_o = pltpu.make_async_copy(oo, oo_o, ls.at[13])
+    keep_o.start()
+
+    ob = o_o[...]
+    u3 = nt(ob, a3[...]).astype(BF)
+    hid = x[...].astype(F32) + mm(ob, oo[...].reshape(D, D)) + mm(u3, bo[...])
+    hid_o[...] = hid
+    nv = (hid * rms(hid) * gain[...].astype(F32)).astype(BF)
+    n2[:, :D] = nv
+    n2[:, D:] = nt(nv, a45[...]).astype(BF)
+    nz = ZGather(me, n2, xg, *nz_sems, BLK)
+    nz.first()
+    start(pltpu.make_async_copy(n2, xg.at[me.zlo, me.core, me.zhi], ls.at[19]), side)
+    ga2.second()
+    gb2.second()
+    da.second()
+    ez.last()
+    nz.second()
+    da.last()
+
+    piece = me.slice
+    off = FV * piece - 128 * window_tile(piece)
+    for r in range(5):
+        base = 256 * r - off
+        i0 = jnp.minimum(lax.div(jnp.maximum(base, 0), 70), 11)
+        rw, cl = iota((256, 400), 0) + base, iota((256, 400), 1)
+        i, k = i0 + lax.div(cl, 80), lax.rem(cl, 80)
+        pick70 = jnp.where((k < 70) & (i * 70 + k == rw), 1.0, 0.0).astype(BF)
+        for j in range(4):
+            src = od[j, pl.ds(i0, 5)].reshape(400, 384)
+            down[256 * r : 256 * (r + 1), 384 * j : 384 * (j + 1)] = mm(pick70, src).astype(BF)
+    keep_d = pltpu.make_async_copy(down, od_o, ls.at[20])
+    keep_d.start()
+    nz.last()
+    ga2.last()
+    gb2.last()
+
+    for r in (qa, qb, qa2, qb2, wa, wb, ga, gb, ga2, gb2, da):
+        r.sent()
+    for c in first + zc:
+        c.wait_send()
+
+    @pl.when(jnp.logical_not(keeper))
+    def _():
+        d_cross.wait_send()
+
+    @pl.when(keeper)
+    def _():
+        for k, t in ys:
+            remote(od.at[me.x, rows8], od.at[me.x, rows8], sd.at[k], rdn.at[k], me.at(y=t)).wait_send()
+
+    def sent(k, carry):
+        t = lax.rem(m + k, N_CTX)
+        for half in range(2):
+            block = m if half == 0 else NBLK - 1 - m
+
+            @pl.when(reads(t, block))
+            def _():
+                src, dst = kv_own.at[half], kv.at[16 + block]
+                remote(src, dst, sk.at[half, k], rk.at[block], (me.dp, t)).wait_send()
+
+        return carry
+
+    lax.fori_loop(1, N_CTX, sent, 0)
+    for n, (dz, dc) in enumerate(ZK):
+        z, core = me.step("z", 4 - dz if dz else 0), lax.rem(me.core + dc, 2)
+        ref = oi.at[2 * lax.rem(z, 2) + core, lax.div(z, 2)]
+        remote(ref, ref, si.at[n], ri.at[n], me.at(z=z, core=core)).wait_recv()
+    ez.finish()
+    nz.finish()
+    for c in side + wins + keep_p + [keep_q, keep_o, keep_d]:
+        c.wait()
+
+
+def front(idx, wq, wo, wg, wd, eext, n1, ub, cos, sin, low, x, gain, a45, a3, bo):
     outs = (
+        sds((2, 2, 4, 2, 48, 2048), BF),
+        sds((2, 2, 4, 2, 48, D), BF),
+        sds((4, 2, 2, 4, 2, 48, 640), BF),
+        sds((FW, D), BF),
+        sds((2, 2, 2, ROWS, DX), BF),
+        sds((4, 2, 8, 128), jnp.int32),
+        sds((2, NWB, BLK, 2 * KW), BF),
         sds((4, GROUP * BLK, KEYS), BF),
+        sds((2, 2, 2, ROWS, DX), BF),
+        sds((ROWS, D), BF),
         sds((ROWS, D), BF),
         sds((ROWS, D), F32),
         sds((ROWS, DX), BF),
     )
+    four = (DMA((4,)),) * 4
+    scratch = [
+        pltpu.VMEM((4, 16, 2048), BF),
+        pltpu.VMEM((4, 16, D), BF),
+        pltpu.VMEM((4, 8, 16, 640), BF),
+        pltpu.VMEM((80, D), BF),
+        pltpu.VMEM((4, 80, 384), BF),
+        pltpu.VMEM((48, 2048), BF),
+        pltpu.VMEM((48, D), BF),
+        pltpu.VMEM((8, 48, 640), BF),
+        pltpu.VMEM((2, 2, 4, 2, 48, 2048), BF),
+        pltpu.VMEM((2, 2, 4, 2, 48, D), BF),
+        pltpu.VMEM((4, 16, 80, 384), BF),
+        pltpu.VMEM((2, BLK, 2 * KW), BF),
+        pltpu.VMEM((16 + NBLK, BLK, 2 * KW), BF),
+        pltpu.VMEM((4, GROUP * BLK, KEYS), BF),
+        pltpu.VMEM((FW, D), BF),
+        DMA((11, 4)),
+        DMA((11, 4)),
+        DMA((21,)),
+        DMA((3, 11)),
+        DMA((3, 11)),
+        DMA((7,)),
+        DMA((7,)),
+        DMA((12,)),
+        DMA((12,)),
+        DMA((4,)),
+        DMA((4,)),
+        DMA((2, N_CTX)),
+        DMA((NBLK,)),
+        four,
+        DMA((7,)),
+        DMA((7,)),
+        four,
+    ]
     return pl.pallas_call(
-        attend_kernel,
+        front_kernel,
         out_shape=outs,
-        grid_spec=pltpu.PrefetchScalarGridSpec(
-            num_scalar_prefetch=1,
-            grid=(1,),
-            in_specs=[
-                whole(low.shape),
-                whole(q.shape),
-                ANY,
-                whole(x.shape),
-                whole(w_out.shape),
-                pick(a_in.shape),
-                pick(b_res.shape),
-                whole((1, D)),
-                whole(a45.shape),
-            ],
-            out_specs=[whole(o.shape) for o in outs],
-            scratch_shapes=[pltpu.VMEM((2, NWB, BLK, 2 * KW), BF), DMA((2,))],
-        ),
-        compiler_params=pltpu.CompilerParams(vmem_limit_bytes=VMEM_LIMIT),
-    )(idx, low, q, kv, x, w_out, a_in, b_res, gain, a45)
-
-
-def gather_kernel(own, out, ss, rs, cs, cr, ls):
-    me = Place()
-    greet(me.ring("z") + [me.sibling()])
-    c = pltpu.make_async_copy(own, out.at[me.zlo, me.core, me.zhi], ls.at[0])
-    c.start()
-    z = ZGather(me, own, out, ss, rs, cs, cr, BLK)
-    z.first()
-    z.second()
-    z.last()
-    z.finish()
-    c.wait()
-
-
-def gather(own):
-    return pl.pallas_call(
-        gather_kernel,
-        out_shape=sds((2, 2, 2, ROWS, DX), BF),
-        in_specs=[ANY],
-        out_specs=ANY,
-        scratch_shapes=[DMA((4,))] * 4 + [DMA((1,))],
-        compiler_params=pltpu.CompilerParams(collective_id=3, has_side_effects=True, vmem_limit_bytes=VMEM_LIMIT),
-    )(own)
-
-
-def compact_kernel(wd, out):
-    piece = 2 * lax.axis_index("dp") + lax.rem(lax.div(lax.axis_index("ctx"), 4), 2)
-    o = FV * piece - 128 * window_tile(piece)
-    for r in range(5):
-        row = iota((256, 1280), 0) + 256 * r - o
-        col = iota((256, 1280), 1)
-        i, k = lax.div(col, 80), lax.rem(col, 80)
-        put = jnp.where((k < 70) & (i * 70 + k == row), 1.0, 0.0).astype(BF)
-        out[256 * r : 256 * (r + 1)] = mm(put, wd[...].reshape(1280, D)).astype(BF)
-
-
-def compact(wd):
-    return pl.pallas_call(
-        compact_kernel,
-        out_shape=sds((FW, D), BF),
-        in_specs=[VM],
-        out_specs=VM,
-        compiler_params=pltpu.CompilerParams(vmem_limit_bytes=VMEM_LIMIT),
-    )(wd)
+        in_specs=[ANY, VM, VM, ANY, VM, ANY] + [VM] * 10,
+        out_specs=[ANY] * 9 + [VM] * 4,
+        scratch_shapes=scratch,
+        compiler_params=pltpu.CompilerParams(collective_id=1, has_side_effects=True, vmem_limit_bytes=VMEM_LIMIT),
+    )(idx, wq, wo, wg, wd, eext, n1, ub, cos, sin, low, x, gain, a45, a3, bo)
 
 
 FSTEPS = 4
@@ -929,10 +896,9 @@
 
 
 def back_kernel(
-    idx, gn2, e, hid, n2, q, o, p, kv, w_out, a_in, b_res, gain, a45,
-    gh_o, gq_o, win_o, g45_o, gbo_o, ga3_o, go, win, sem,
+    idx, gn2, e, hid, n2, q, o, p, win, w_out, a_in, b_res, gain, a45,
+    gh_o, gq_o, win_o, g45_o, gbo_o, ga3_o, go,
 ):
-    copies = load_windows(kv, win, sem)
     s = lax.axis_index("dp")
     gue = gn2[:, D:].astype(BF)
     gn = gn2[:, :D] + mm(gue, a45[...])
@@ -947,7 +913,6 @@
     ga3_o[...] = tn(gu3, ob)
     g45_o[...] = tn(gue, n2[:, :D])
     for h in range(2):
-        copies[h].wait()
         for a in range(KV_HEADS):
             qs, gs, os = stack_heads(q, h, a), stack_heads(go, h, a), stack_heads(o, h, a)
             k = win[h, :, :, a * HS : (a + 1) * HS].reshape(KEYS, HS)
@@ -964,7 +929,7 @@
             win_o[h, :, :, KW + a * HS : KW + (a + 1) * HS] = tn(pr, gs).astype(BF).reshape(NWB, BLK, HS)
 
 
-def back(idx, gn2, e, hid, n2, q, o, p, kv, w_out, a_in, b_res, gain, a45):
+def back(idx, gn2, e, hid, n2, q, o, p, win, w_out, a_in, b_res, gain, a45):
     outs = (
         sds((ROWS, D), F32),
         sds((ROWS, D), F32),
@@ -987,22 +952,18 @@
                 whole(q.shape),
                 whole(o.shape),
                 whole(p.shape),
-                ANY,
+                whole(win.shape),
                 whole(w_out.shape),
                 pick(a_in.shape),
                 pick(b_res.shape),
-                whole((1, D)),
+                whole((D,)),
                 whole(a45.shape),
             ],
             out_specs=[whole(x.shape) for x in outs],
-            scratch_shapes=[
-                pltpu.VMEM((ROWS, D), BF),
-                pltpu.VMEM((2, NWB, BLK, 2 * KW), BF),
-                DMA((2,)),
-            ],
+            scratch_shapes=[pltpu.VMEM((ROWS, D), BF)],
         ),
         compiler_params=pltpu.CompilerParams(vmem_limit_bytes=VMEM_LIMIT),
-    )(idx, gn2, e, hid, n2, q, o, p, kv, w_out, a_in, b_res, gain, a45)
+    )(idx, gn2, e, hid, n2, q, o, p, win, w_out, a_in, b_res, gain, a45)
 
 
 def return_kernel(win, out, got, ss, rs, ls):
@@ -1405,37 +1366,29 @@
     cos = jnp.concatenate([c, c], -1)
     sin = jnp.concatenate([-sn, sn], -1)
 
-    tok = jnp.transpose(tokens[0], (1, 0, 2)).reshape(ROWS, D)
-    cot = jnp.transpose(cotangent[0], (1, 0, 2)).reshape(ROWS, D)
-    gain1, gain2 = gain_attn[None], gain_mlp[None]
-    wq = jnp.pad(w_qkv, ((0, 4), (0, 0)))
-    wo = jnp.pad(w_out, ((0, 4), (0, 0)))
     wg = jnp.pad(jnp.transpose(w_gu, (1, 0, 2)), ((0, 0), (0, 4), (0, 0)))
-    wd = jnp.pad(w_down, ((0, 10), (0, 0)))
     idx_row = jnp.broadcast_to(adapter_index[:, None], (8, 128)).astype(jnp.int32)
 
-    x, n1, eext, ub, a45, bd = prepare(
-        adapter_index, tok, cot, adapt_in, adapt_out_qkv, adapt_out_res, gain1, b_qkv[None]
+    x, n1, eext, ub, a45, bd, a3, bo = prepare(
+        adapter_index, tokens[0], cotangent[0], adapt_in, adapt_out_qkv, adapt_out_res, gain_attn, b_qkv
     )
-    oq, oo, og, od, oe, oi = weights(idx_row, wq, wo, wg, wd, eext)
+    oq, oo, og, down, oe, oi, wins, p, xg, q, o, hid, n2 = front(
+        idx_row, w_qkv, w_out, wg, w_down, eext, n1, ub, cos, sin, low, x, gain_mlp, a45, a3, bo
+    )
     oq = oq.reshape(D, 2048)
     oo = oo.reshape(D, D)
     og = og.reshape(4, D, 640)
     idx4 = oi[:, 0, 0, 0]
-    q, kv = qkv(n1, oq, ub, cos, sin)
-    kv_all = halo(kv)
-    p, o, hid, n2 = attend(adapter_index, low, q, kv_all, x, oo, adapt_in, adapt_out_res, gain2, a45)
-    xg = gather(n2).reshape(8 * ROWS, DX)
-    down = compact(od)
+    xg = xg.reshape(8 * ROWS, DX)
     yp, gp, ft = feed(idx4, xg, oe.reshape(8 * ROWS, DX), og, down, adapt_in_ff, adapt_out_ff)
     gn2 = scatter(gp.reshape(2, 2, 2, ROWS, DX), 4)
     gh, gq, win, g45, gbo, ga3 = back(
-        adapter_index, gn2, eext, hid, n2, q, o, p, kv_all, oo, adapt_in, adapt_out_res, gain2, a45
+        adapter_index, gn2, eext, hid, n2, q, o, p, wins, oo, adapt_in, adapt_out_res, gain_mlp, a45
     )
     y = scatter(yp.reshape(2, 2, 2, ROWS, DX), 4)
     gkv = give_back(win)
     out, gt, lt = final(
-        adapter_index, gkv, gq, x, n1, gh, hid, y, eext, oq, adapt_in, adapt_out_qkv, bd, gain1, cos, sin, g45, gbo, ga3
+        adapter_index, gkv, gq, x, n1, gh, hid, y, eext, oq, adapt_in, adapt_out_qkv, bd, gain_attn, cos, sin, g45, gbo, ga3
     )
     tiles = total(lt, ft)
     grads = spread(idx4, tiles)

time: 511 us -> 436 us (0.85)
  Pallas kernels: 478 us -> 418 us
  local copies, waits for them, and re-layouts: 21 us -> 9.07 us
    pallas_call x6 -> x1, Pallas kernels: 232 us -> 172 us  [front(): pl.pallas_call(front_kernel, out_shape=outs, in_specs=[ANY, VM, VM, ANY,...]
where the time goes in v2:
time: 436 us; the launch traced here: 431 us
  Pallas kernels  418 us (96%)
  local copies, waits for them, and re-layouts  9.07 us (2%)
    pallas_call x1, Pallas kernels, front(): pl.pallas_call(front_kernel, out_shape=outs, in_specs=[ANY, VM, VM, ANY,...  172 us
    pallas_call x1, Pallas kernels, total(): pl.pallas_call(total_kernel, out_shape=sds((4, 4, 2, 2, 2, 12, R, 128), B...  65.7 us
    pallas_call x2, Pallas kernels, scatter(): pl.pallas_call(scatter_kernel, out_shape=sds((ROWS, DX), F32), in_specs=[...  57.1 us
    pallas_call x1, Pallas kernels, give_back(): pl.pallas_call(return_kernel, out_shape=sds((2, BLK, 2 * KW), F32), in_sp...  44 us
    pallas_call x1, Pallas kernels, feed(): pl.pallas_call(feed_kernel, out_shape=outs, grid_spec=pltpu.PrefetchScala...  39.1 us
    pallas_call x1, Pallas kernels, back(): pl.pallas_call(back_kernel, out_shape=outs, grid_spec=pltpu.PrefetchScala...  13.6 us
    pallas_call x1, Pallas kernels, spread(): pl.pallas_call(spread_kernel, out_shape=outs, grid_spec=pltpu.PrefetchSca...  11.6 us
    pallas_call x1, Pallas kernels, final(): pl.pallas_call(final_kernel, out_shape=outs, grid_spec=pltpu.PrefetchScal...  9.75 us

profile of v2, /device:TPU:1, one launch (start us, length us, event | category | flops | bytes accessed | tf_op | source)
XLA Modules:
  0.0 431.2 jit_solution(16494556302215809924)
XLA Ops:
  1.9 0.1 pad_add_fusion
  2.0 0.8 reduce-window.8
  2.8 0.1 iota_add_fusion
  2.9 0.1 add.42
  3.0 0.1 select_reduce_fusion
  3.1 0.6 broadcast_in_dim.21.idx
  3.7 0.7 broadcast_in_dim.23.low
  4.4 0.3 fusion
  4.7 0.8 pad_maximum_fusion
  5.5 1.1 copy.36
  6.5 0.9 pad.4.wg
  7.4 5.3 %shard_map.216 = (bf16[128,1536]{1,0:T(8,128)(2,1)}, bf16[128,1536]{1,0:T(8,128)(2,1)}, bf16[128,1664]{1,0:T(8,128)(2,1)}, f32[128,2048]{1,0:T(8,128)}, bf16[128...) custom-call(s32[1]{0:T(128)} %copy.39.idx, ...), custom_call_target="tpu_custom_call" | custom-call | tf_op jit(solution)/shard_map/pallas_call | solution.py:229
  12.7 171.6 %shard_map.217 = (bf16[2,2,4,2,48,2048]{5,4,3,2,1,0:T(8,128)(2,1)}, bf16[2,2,4,2,48,1536]{5,4,3,2,1,0:T(8,128)(2,1)}, bf16[4,2,2,4,2,48,640]{6,5,4,3,2,1,0:T(8,1...) custom-call(s32[8,128]{1,0:T(8,128)} %broadcast_in_dim.21.idx, ...), custom_call_target="tpu_custom_call" | custom-call | tf_op jit(solution)/shard_map/pallas_call | solution.py:736
  184.2 1.5 slice_reduce_fusion.idx
  185.7 39.1 %shard_map.218 = (bf16[1024,1664]{1,0:T(8,128)(2,1)}, bf16[1024,1664]{1,0:T(8,128)(2,1)}, bf16[128,16,128]{2,1,0:T(8,128)(2,1)}) custom-call(s32[4]{0:T(128)} %slice_reduce_fusion.idx, bf16[1024,1664]{1,0:T(8,128)(2,1)} %bitcast.38, bf16[1024,1664]{1,0:T(8,128)(2,1)} %bitcast.37, bf16[4,1536,640]{2,1,0:T(8,128)(2,1)} %bitcast.32, ...), custom_call_target="tpu_custom_call" | custom-call | tf_op jit(solution)/shard_map/pallas_call | solution.py:813
  224.8 27.0 %shard_map.219.gn2 = f32[128,1664]{1,0:T(8,128)} custom-call(bf16[2,2,2,128,1664]{4,3,2,1,0:T(8,128)(2,1)} %bitcast.36), custom_call_target="tpu_custom_call" | custom-call | tf_op jit(solution)/shard_map/pallas_call | solution.py:872
  251.8 13.6 %shard_map.220 = (f32[128,1536]{1,0:T(8,128)}, f32[128,1536]{1,0:T(8,128)}, bf16[2,17,64,512]{3,2,1,0:T(8,128)(2,1)}, f32[128,1536]{1,0:T(8,128)}, f32[16,1536]{1,0:T(8,128)}, /*index=5*/f32[16,1536]{1,0:T(8,128)}) custom-call(s32[1]{0:T(128)} %copy.39.idx, f32[128,1664]{1,0:T(8,128)} %shard_map.219.gn2, bf16[128,1664]{1,0:T(8,128)(2,1)} %get-tuple-element.45.eext.e, ...), custom_call_target="tpu_custom_call" | custom-call | tf_op jit(solution)/shard_map/pallas_call | solution.py:941
  265.4 44.0 %shard_map.221.gkv = f32[2,64,512]{2,1,0:T(8,128)} custom-call(bf16[2,17,64,512]{3,2,1,0:T(8,128)(2,1)} %get-tuple-element.65.win), custom_call_target="tpu_custom_call" | custom-call | tf_op jit(solution)/shard_map/pallas_call | solution.py:1048
  309.4 30.1 %shard_map.222.y = f32[128,1664]{1,0:T(8,128)} custom-call(bf16[2,2,2,128,1664]{4,3,2,1,0:T(8,128)(2,1)} %bitcast.35), custom_call_target="tpu_custom_call" | custom-call | tf_op jit(solution)/shard_map/pallas_call | solution.py:872
  339.5 9.8 %shard_map.223 = (bf16[128,1536]{1,0:T(8,128)(2,1)}, bf16[128,1536]{1,0:T(8,128)(2,1)}, bf16[128,16,128]{2,1,0:T(8,128)(2,1)}) custom-call(s32[1]{0:T(128)} %copy.39.idx, f32[2,64,512]{2,1,0:T(8,128)} %shard_map.221.gkv, f32[128,1536]{1,0:T(8,128)} %get-tuple-element.66.gq, bf16[128,1536]{1,0:T(8,128)(2,1)} %get-tuple-element.48.x, ...), custom_call_target="tpu_custom_call" | custom-call | tf_op jit(solution)/shard_map/pallas_call | solution.py:1110
  349.3 2.1 copy.38
  351.4 2.1 copy.37
  353.6 65.7 %shard_map.224.t = bf16[4,4,2,2,2,12,16,128]{7,6,5,4,3,2,1,0:T(8,128)(2,1)} custom-call(bf16[128,16,128]{2,1,0:T(8,128)(2,1)} %get-tuple-element.76.lt, bf16[128,16,128]{2,1,0:T(8,128)(2,1)} %get-tuple-element.77.ft), custom_call_target="tpu_custom_call" | custom-call | tf_op jit(solution)/shard_map/pallas_call | solution.py:1249
  419.3 11.6 %shard_map.225 = (f32[8,6,16,1536]{3,2,1,0:T(8,128)}, f32[8,16,8960]{2,1,0:T(8,128)}, f32[8,16,2048]{2,1,0:T(8,128)}, f32[8,2,16,1536]{3,2,1,0:T(8,128)}, f32[8,2,16,8960]{3,2,1,0:T(8,128)}) custom-call(s32[4]{0:T(128)} %slice_reduce_fusion.idx, bf16[4,4,2,2,2,12,16,128]{7,6,5,4,3,2,1,0:T(8,128)(2,1)} %shard_map.224.t), custom_call_target="tpu_custom_call" | custom-call | tf_op jit(solution)/shard_map/pallas_call | solution.py:1324
  (2 shorter events, 0.0 us)

commit v3 on v2

v3 whole, which is shorter than its diff:
```python
import functools

import jax
import jax.numpy as jnp
from jax import lax
from jax.experimental import pallas as pl
from jax.experimental.pallas import tpu as pltpu
from jax.sharding import PartitionSpec as P

D = 1536
HEADS = 12
KV_HEADS = 2
HS = 128
GROUP = HEADS // KV_HEADS
FF = 8960
R = 16
ADAPT = 8
BLK = 64
ROWS = 2 * BLK
N_CTX = 32
NBLK = 2 * N_CTX
WIN = 1024
NWB = WIN // BLK + 1
KEYS = NWB * BLK
EXT = 128
DX = D + EXT
FW = 1280
FV = FF // 8
QW = HEADS * HS
KW = KV_HEADS * HS
SCALE = HS**-0.5
EPS = 1e-6

MESH = pl.DeviceIdType.MESH
BF = jnp.bfloat16
F32 = jnp.float32
ANY = pl.BlockSpec(memory_space=pl.ANY)
VM = pl.BlockSpec(memory_space=pltpu.VMEM)
SM = pl.BlockSpec(memory_space=pltpu.SMEM)
DMA = pltpu.SemaphoreType.DMA
VMEM_LIMIT = 60 * 2**20


def sds(shape, dtype):
    return jax.ShapeDtypeStruct(shape, dtype)


def nt(a, b):
    return lax.dot_general(a, b, (((1,), (1,)), ((), ())), preferred_element_type=F32)


def tn(a, b):
    return lax.dot_general(a, b, (((0,), (0,)), ((), ())), preferred_element_type=F32)


def mm(a, b):
    return jnp.dot(a, b, preferred_element_type=F32)


def iota(shape, dim):
    return lax.broadcasted_iota(jnp.int32, shape, dim)


class Place:
    def __init__(self):
        dp, ctx = lax.axis_index("dp"), lax.axis_index("ctx")
        self.dp, self.ctx = dp, ctx
        self.zlo, self.core = lax.div(dp, 2), lax.rem(dp, 2)
        self.y, self.zhi, self.x = lax.div(ctx, 8), lax.rem(lax.div(ctx, 4), 2), lax.rem(ctx, 4)
        self.z = self.zhi * 2 + self.zlo
        self.slice = 2 * dp + self.zhi

    def at(self, x=None, y=None, z=None, core=None):
        x = self.x if x is None else x
        y = self.y if y is None else y
        z = self.z if z is None else z
        core = self.core if core is None else core
        return (lax.rem(z, 2) * 2 + core, y * 8 + lax.div(z, 2) * 4 + x)

    def step(self, axis, by):
        return lax.rem(getattr(self, axis) + by, 4)

    def ring(self, axis):
        return [self.at(**{axis: self.step(axis, k)}) for k in (1, 2, 3)]

    def sibling(self):
        return self.at(core=1 - self.core)


def window_tile(piece):
    return jnp.minimum(lax.div(35 * piece, 4), 60)


def remote(src, dst, send, recv, device):
    return pltpu.make_async_remote_copy(
        src_ref=src, dst_ref=dst, send_sem=send, recv_sem=recv, device_id=device, device_id_type=MESH
    )


def greet(peers):
    sem = pltpu.get_barrier_semaphore()
    for device in peers:
        pl.semaphore_signal(sem, inc=1, device_id=device, device_id_type=MESH)
    pl.semaphore_wait(sem, len(peers))


class Ring:
    def __init__(self, me, axis, own, view, send, recv):
        self.i = getattr(me, axis)
        self.r, self.o, self.l = (me.step(axis, k) for k in (1, 2, 3))
        self.right, self.left = me.at(**{axis: self.r}), me.at(**{axis: self.l})
        self.own, self.view, self.send, self.recv = own, view, send, recv

    def copy(self, k, src, dst, device):
        return remote(src, dst, self.send.at[k], self.recv.at[k], device)

    def first(self):
        place = self.view(self.i, None)
        self.out = [self.copy(0, self.own, place, self.right), self.copy(1, self.own, place, self.left)]
        for c in self.out:
            c.start()

    def second(self):
        v = self.view
        self.copy(0, v(self.l, None), v(self.l, None), self.right).wait_recv()
        c = self.copy(2, v(self.l, 0), v(self.l, 0), self.right)
        c.start()
        self.out.append(c)
        self.copy(1, v(self.r, None), v(self.r, None), self.left).wait_recv()
        c = self.copy(3, v(self.r, 1), v(self.r, 1), self.left)
        c.start()
        self.out.append(c)

    def last(self):
        v = self.view
        self.copy(2, v(self.o, 0), v(self.o, 0), self.right).wait_recv()
        self.copy(3, v(self.o, 1), v(self.o, 1), self.left).wait_recv()

    def sent(self):
        for c in self.out:
            c.wait_send()


class ZGather:
    def __init__(self, me, own, buf, send, recv, core_send, core_recv, half):
        self.me, self.own, self.buf = me, own, buf
        self.cs, self.cr = core_send, core_recv

        def view(j, h, core=me.core):
            ref = buf.at[lax.rem(j, 2), core, lax.div(j, 2)]
            return ref if h is None else ref.at[pl.ds(h * half, half)]

        self.view = view
        self.ring = Ring(me, "z", own, view, send, recv)
        self.out = []

    def swap(self, src, j):
        c = remote(src, self.view(j, None), self.cs.at[len(self.out)], self.cr.at[len(self.out)], self.me.sibling())
        c.start()
        self.out.append((c, j))

    def first(self):
        self.ring.first()
        self.swap(self.own, self.me.z)

    def second(self):
        self.ring.second()
        self.swap(self.view(self.ring.l, None), self.ring.l)
        self.swap(self.view(self.ring.r, None), self.ring.r)

    def last(self):
        self.ring.last()
        self.swap(self.view(self.ring.o, None), self.ring.o)

    def finish(self):
        self.ring.sent()
        for k, (c, j) in enumerate(self.out):
            c.wait_send()
            place = self.view(j, None, 1 - self.me.core)
            remote(place, place, self.cs.at[k], self.cr.at[k], self.me.sibling()).wait_recv()


def rms(z):
    return lax.rsqrt(jnp.mean(z * z, -1, keepdims=True) + EPS)


def prepare_kernel(idx, tok, cot, a_in, b_qkv_ad, b_res, gain, bias, x_o, n1_o, e_o, ub_o, a45_o, bd_o, a3_o, bo_o, a012_o, bqkv_o):
    s = lax.axis_index("dp")
    for h in range(2):
        rows = slice(h * BLK, (h + 1) * BLK)
        x_o[rows] = tok[:, h, :]
        e_o[rows, :D] = cot[:, h, :]
    x = x_o[...].astype(F32)
    n1 = (x * rms(x) * gain[...].astype(F32)).astype(BF)
    n1_o[...] = n1
    for m, (lo, hi) in enumerate(((0, QW), (QW, QW + KW), (QW + KW, QW + 2 * KW))):
        u = nt(n1, a_in[0, m]).astype(BF)
        ub_o[:, lo:hi] = mm(u, b_qkv_ad[0, :, lo:hi]) + bias[lo:hi].astype(F32)
    at = pl.multiple_of(s * R, R)
    a45_o[...] = jnp.zeros_like(a45_o)
    a45_o[pl.ds(at, R), :] = a_in[0, 4]
    a45_o[pl.ds(at + 64, R), :] = a_in[0, 5]
    bd_o[...] = jnp.zeros_like(bd_o)
    bd_o[pl.ds(at, R), :] = b_res[0, 1]
    a3_o[...] = a_in[0, 3]
    bo_o[...] = b_res[0, 0]
    a012_o[...] = a_in[0, :3]
    bqkv_o[...] = b_qkv_ad[0]
    e_o[:, D:] = nt(e_o[:, :D], bd_o[...]).astype(BF)


def pick(shape):
    return pl.BlockSpec((1,) + shape[1:], lambda i, idx: (idx[0],) + (0,) * (len(shape) - 1))


def whole(shape):
    return pl.BlockSpec(shape, lambda i, idx: (0,) * len(shape))


def prepare(idx, tok, cot, a_in, b_qkv_ad, b_res, gain, bias):
    outs = (
        sds((ROWS, D), BF),
        sds((ROWS, D), BF),
        sds((ROWS, DX), BF),
        sds((ROWS, 2048), F32),
        sds((EXT, D), BF),
        sds((EXT, D), BF),
        sds((R, D), BF),
        sds((R, D), BF),
        sds((3, R, D), BF),
        sds((R, 2048), BF),
    )
    return pl.pallas_call(
        prepare_kernel,
        out_shape=outs,
        grid_spec=pltpu.PrefetchScalarGridSpec(
            num_scalar_prefetch=1,
            grid=(1,),
            in_specs=[
                whole((BLK, 2, D)),
                whole((BLK, 2, D)),
                pick(a_in.shape),
                pick(b_qkv_ad.shape),
                pick(b_res.shape),
                whole((D,)),
                whole((2048,)),
            ],
            out_specs=[whole(o.shape) for o in outs],
        ),
        compiler_params=pltpu.CompilerParams(vmem_limit_bytes=VMEM_LIMIT),
    )(idx, tok, cot, a_in, b_qkv_ad, b_res, gain, bias)


def turn(v, cos, sin):
    return v * cos + pltpu.roll(v, 64, 1) * sin


def turn_back(v, cos, sin):
    return v * cos - pltpu.roll(v, 64, 1) * sin


def stack_heads(ref, h, a):
    rows = slice(h * BLK, (h + 1) * BLK)
    return jnp.concatenate(
        [ref[rows, (a * GROUP + g) * HS : (a * GROUP + g + 1) * HS] for g in range(GROUP)], 0
    )


def reads(t, block):
    a, b = t - block, NBLK - 1 - t - block
    return ((a >= 0) & (a < NWB)) | ((b >= 0) & (b < NWB))


ZK = [(dz, dc) for dz in range(4) for dc in range(2) if dz or dc]


def front_kernel(
    idx, wq_i, wo_i, wg, wd_i, eext, n1, ub, cos, sin, low, x, gain, a45, a3, bo,
    oq_o, oo_o, og, od_o, oe, oi, win_o, p_o, xg, q, o_o, hid_o, n2,
    rq, ro, rg, wdp, rd, cq, co, cg, oq, oo, od, kv_own, kv, p, down, pick70,
    ss, rs, ls, s1, r1, s2, r2, sc, rc, sd, rdn, sk, rk, ez_sems, si, ri, nz_sems,
):
    me = Place()
    sib = me.sibling()
    m = me.ctx
    bar = pltpu.get_barrier_semaphore()

    def hello(t, carry):
        @pl.when(t != m)
        def _():
            pl.semaphore_signal(bar, inc=1, device_id=(me.dp, t), device_id_type=MESH)

        return carry

    lax.fori_loop(0, N_CTX, hello, 0)
    others = [me.at(z=me.step("z", dz), core=lax.rem(me.core + dc, 2)) for dz, dc in ZK if dz % 2 or dc]
    for d in others:
        pl.semaphore_signal(bar, inc=1, device_id=d, device_id_type=MESH)

    rq[me.x, :12] = wq_i[...]
    rq[me.x, 12:] = jnp.zeros((4, 2048), BF)
    ro[me.x, :12] = wo_i[...]
    ro[me.x, 12:] = jnp.zeros((4, D), BF)
    wdp[:70] = wd_i[...]
    wdp[70:] = jnp.zeros((10, D), BF)
    kv[:16] = jnp.zeros((16, BLK, 2 * KW), BF)

    pl.semaphore_wait(bar, N_CTX - 1 + len(others))

    tiles = [60 if g == 7 else 35 * g // 4 for g in range(8)]

    def panel(g, t):
        col = pl.multiple_of(tiles[g] * 128 + lax.rem(t, 2) * 640, 128)
        return wg.at[lax.div(t, 2), :, pl.ds(col, 640)]

    def strip(t):
        return wdp.at[:, pl.ds(pl.multiple_of(384 * t, 128), 384)]

    def start(c, out):
        c.start()
        out.append(c)

    first = []
    xs = [(k, me.step("x", k), me.at(x=me.step("x", k))) for k in (1, 3, 2)]
    for k, t, d in xs:
        start(remote(rq.at[me.x], rq.at[me.x], s1.at[k - 1, 0], r1.at[k - 1, 0], d), first)
    for k, t, d in xs:
        start(remote(ro.at[me.x], ro.at[me.x], s1.at[k - 1, 1], r1.at[k - 1, 1], d), first)
    for k, t, d in xs:
        for g in range(8):
            start(remote(panel(g, t), rg.at[me.x, g], s1.at[k - 1, 2 + g], r1.at[k - 1, 2 + g], d), first)
        start(remote(strip(t), rd.at[me.x], s1.at[k - 1, 10], r1.at[k - 1, 10], d), first)
    mine = []
    for g in range(8):
        start(pltpu.make_async_copy(panel(g, me.x), rg.at[me.x, g], ls.at[2 + g]), mine)
    start(pltpu.make_async_copy(strip(me.x), rd.at[me.x], ls.at[1]), mine)
    side = []
    start(pltpu.make_async_copy(eext, oe.at[me.zlo, me.core, me.zhi], ls.at[10]), side)
    start(pltpu.make_async_copy(idx, oi.at[me.dp, me.zhi], ls.at[11]), side)
    for n, (dz, dc) in enumerate(ZK):
        d = me.at(z=me.step("z", dz), core=lax.rem(me.core + dc, 2))
        start(remote(idx, oi.at[me.dp, me.zhi], si.at[n], ri.at[n], d), first)

    def from_x(n, ref_of):
        for k in (1, 3, 2):
            f = me.step("x", 4 - k)
            ref = ref_of(f)
            remote(ref, ref, s1.at[k - 1, n], r1.at[k - 1, n], me.at(x=f)).wait_recv()

    row, col = iota((48, 64), 0), iota((48, 64), 1)
    put = jnp.where(
        (lax.rem(col, 16) < 12) & (lax.div(col, 16) * 12 + lax.rem(col, 16) == row), 1.0, 0.0
    ).astype(BF)

    from_x(0, lambda f: rq.at[f])
    cq[...] = mm(put, rq[...].reshape(64, 2048)).astype(BF)
    lo, hi = pl.ds(0, 1024), pl.ds(1024, 1024)

    def qy0(j, h):
        return oq.at[me.zlo, me.core, j, me.zhi, :, lo if h is None else pl.ds(512 * h, 512)]

    def qz0(j, h, core=me.core):
        zl, zh = lax.rem(j, 2), lax.div(j, 2)
        return oq.at[zl, core, :, zh, :, lo] if h is None else oq.at[zl, core, pl.ds(2 * h, 2), zh, :, lo]

    def qz1(j, h):
        cols = hi if h is None else pl.ds(1024 + 512 * h, 512)
        return oq.at[lax.rem(j, 2), me.core, me.y, lax.div(j, 2), :, cols]

    def qy1(j, h, core=me.core):
        return oq.at[:, core, j, :, :, hi] if h is None else oq.at[h, core, j, :, :, hi]

    qa = Ring(me, "y", cq.at[:, lo], qy0, ss.at[0], rs.at[0])
    qb = Ring(me, "z", cq.at[:, hi], qz1, ss.at[1], rs.at[1])
    qa.first()
    qb.first()
    oq[me.zlo, me.core, me.y, me.zhi] = cq[...]
    from_x(1, lambda f: ro.at[f])
    co[...] = mm(put, ro[...].reshape(64, D)).astype(BF)
    qa.second()
    qb.second()
    for n in range(8):
        from_x(2 + n, lambda f: rg.at[f, n])
    from_x(10, lambda f: rd.at[f])
    for c in mine:
        c.wait()
    for g in range(8):
        cg[g] = mm(put, rg[:, g].reshape(64, 640)).astype(BF)

    own_g = pltpu.make_async_copy(cg.at[me.slice], og.at[me.x, me.zlo, me.core, me.y, me.zhi], ls.at[14])
    own_g.start()
    zc = []
    for n, (dz, dc) in enumerate(ZK):
        z, core = me.step("z", dz), lax.rem(me.core + dc, 2)
        piece = 2 * (2 * lax.rem(z, 2) + core) + lax.div(z, 2)
        d = me.at(z=z, core=core)
        start(remote(cg.at[piece], og.at[me.x, me.zlo, me.core, me.y, me.zhi], s2.at[n], r2.at[n], d), zc)
    keeper = lax.div(me.y, 2) == me.zhi
    rows4 = pl.ds(lax.rem(me.y, 2) * 8 + me.zhi * 4, 4)
    across = me.at(z=me.step("z", 2))
    d_local = pltpu.make_async_copy(rd, od.at[me.x, rows4], ls.at[15])
    d_cross = remote(rd, od.at[me.x, rows4], sd.at[0], rdn.at[0], across)

    @pl.when(keeper)
    def _():
        d_local.start()

    @pl.when(jnp.logical_not(keeper))
    def _():
        d_cross.start()

    qa.last()
    qb.last()
    qa2 = Ring(me, "z", qz0(me.z, None), qz0, ss.at[2], rs.at[2])
    qb2 = Ring(me, "y", qy1(me.y, None), qy1, ss.at[3], rs.at[3])
    qa2.first()
    qb2.first()
    swaps = []

    def swap(view, j):
        n = len(swaps)
        c = remote(view(j, None), view(j, None), sc.at[n], rc.at[n], sib)
        c.start()
        swaps.append((c, view, j))

    def swapped(n):
        c, view, j = swaps[n]
        c.wait_send()
        ref = view(j, None, 1 - me.core)
        remote(ref, ref, sc.at[n], rc.at[n], sib).wait_recv()

    swap(qz0, me.z)
    swap(qy1, me.y)
    own_g.wait()
    for n, (dz, dc) in enumerate(ZK):
        z, core = me.step("z", 4 - dz if dz else 0), lax.rem(me.core + dc, 2)
        ref = og.at[me.x, lax.rem(z, 2), core, me.y, lax.div(z, 2)]
        remote(ref, ref, s2.at[n], r2.at[n], me.at(z=z, core=core)).wait_recv()

    def g0a(j, h):
        return og.at[me.x, 0, :, j] if h is None else og.at[me.x, 0, h, j]

    def g0b(j, h):
        return og.at[j, 0] if h is None else og.at[j, 0, h]

    def g1a(j, h):
        return og.at[j, 1, :, me.y] if h is None else og.at[j, 1, h, me.y]

    def g1b(j, h):
        return og.at[:, 1, :, j] if h is None else og.at[:, 1, h, j]

    ga = Ring(me, "y", g0a(me.y, None), g0a, ss.at[4], rs.at[4])
    gb = Ring(me, "x", g1a(me.x, None), g1a, ss.at[5], rs.at[5])
    ga.first()
    gb.first()
    def oy(j, h):
        ref = oo.at[me.zlo, me.core, j, me.zhi]
        return ref if h is None else ref.at[:, pl.ds(768 * h, 768)]

    def oz(j, h, core=me.core):
        zl, zh = lax.rem(j, 2), lax.div(j, 2)
        return oo.at[zl, core, :, zh] if h is None else oo.at[zl, core, pl.ds(2 * h, 2), zh]

    wa = Ring(me, "y", co, oy, ss.at[8], rs.at[8])
    qa2.second()
    qb2.second()
    swap(qz0, qa2.l)
    swap(qy1, qb2.l)
    swap(qz0, qa2.r)
    swap(qy1, qb2.r)
    oo[me.zlo, me.core, me.y, me.zhi] = co[...]

    ga.second()
    gb.second()
    wa.first()
    qa2.last()
    qb2.last()
    swap(qz0, qa2.o)
    swap(qy1, qb2.o)

    wa.second()
    rows4b = pl.ds(lax.rem(me.y, 2) * 8 + (1 - me.zhi) * 4, 4)
    rows8 = pl.ds(lax.rem(me.y, 2) * 8, 8)
    ys = [(k, me.step("y", k)) for k in (1, 3, 2)]

    @pl.when(keeper)
    def _():
        d_local.wait()
        ref = od.at[me.x, rows4b]
        remote(rd, ref, sd.at[0], rdn.at[0], across).wait_recv()
        for k, t in ys:
            remote(od.at[me.x, rows8], od.at[me.x, rows8], sd.at[k], rdn.at[k], me.at(y=t)).start()

    ga.last()
    gb.last()
    ga2 = Ring(me, "x", g0b(me.x, None), g0b, ss.at[6], rs.at[6])
    gb2 = Ring(me, "y", g1b(me.y, None), g1b, ss.at[7], rs.at[7])

    ga2.first()
    for n in range(8):
        swapped(n)
    keep_q = pltpu.make_async_copy(oq, oq_o, ls.at[12])
    keep_q.start()

    c, s = cos[...], sin[...]
    n1v = n1[...]
    for h in (12, 14, 0, 2, 4, 6, 8, 10):
        pair = slice(h * HS, (h + 2) * HS)
        j = mm(n1v, oq[:, :, :, :, :, pair].reshape(D, 2 * HS)) + ub[:, pair]
        for i in range(2):
            v = j[:, i * HS : (i + 1) * HS]
            if h + i < HEADS + KV_HEADS:
                v = turn(v, c, s)
            v = v.astype(BF)
            if h + i < HEADS:
                q[:, (h + i) * HS : (h + i + 1) * HS] = v
            else:
                at = slice((h + i - HEADS) * HS, (h + i - HEADS + 1) * HS)
                kv_own[0, :, at] = v[:BLK]
                kv_own[1, :, at] = v[BLK:]
        if h == 14:
            def send(k, carry):
                t = lax.rem(m + k, N_CTX)
                for half in range(2):
                    block = m if half == 0 else NBLK - 1 - m

                    @pl.when(reads(t, block))
                    def _():
                        src, dst = kv_own.at[half], kv.at[16 + block]
                        remote(src, dst, sk.at[half, k], rk.at[block], (me.dp, t)).start()

                return carry

            lax.fori_loop(1, N_CTX, send, 0)
            kv[16 + m] = kv_own[0]
            kv[16 + NBLK - 1 - m] = kv_own[1]

    gb2.first()
    wa.last()
    wb = Ring(me, "z", oz(me.z, None), oz, ss.at[9], rs.at[9])
    wb.first()
    swap(oz, me.z)
    ez = ZGather(me, eext, oe, *ez_sems, BLK)
    ez.first()
    def dx(j, h):
        return od.at[j] if h is None else od.at[j, pl.ds(8 * h, 8)]

    def arrived(block):
        src = jnp.where(block < N_CTX, block, NBLK - 1 - block)
        remote(kv_own.at[0], kv.at[16 + block], sk.at[0, 0], rk.at[block], (me.dp, src)).wait_recv()

    def near0(j, carry):
        block = m - (NWB - 1) + j

        @pl.when(block >= 0)
        def _():
            arrived(block)

        return carry

    def near1(j, carry):
        block = NBLK - 1 - m - (NWB - 1) + j

        @pl.when(block > m)
        def _():
            arrived(block)

        return carry

    wins = []
    keep_p = []
    for h in range(2):
        lax.fori_loop(0, NWB - 1, near0 if h == 0 else near1, 0)
        win = kv.at[pl.ds(m if h == 0 else NBLK - 1 - m, NWB)]
        start(pltpu.make_async_copy(win, win_o.at[h], ls.at[16 + h]), wins)
        base = (m if h == 0 else NBLK - 1 - m) * BLK
        kpos = base - WIN + iota((BLK, KEYS), 1)
        qpos = base + iota((BLK, KEYS), 0)
        keep = (kpos <= qpos) & (kpos >= low[h * BLK : (h + 1) * BLK, :1])
        for a in range(KV_HEADS):
            qs = stack_heads(q, h, a)
            k = win[:, :, a * HS : (a + 1) * HS].reshape(KEYS, HS)
            v = win[:, :, KW + a * HS : KW + (a + 1) * HS].reshape(KEYS, HS)
            sco = nt(qs, k) * SCALE
            sco = jnp.where(keep[None], sco.reshape(GROUP, BLK, KEYS), -1e30)
            e = jnp.exp(sco - jnp.max(sco, -1, keepdims=True))
            pr = (e / jnp.sum(e, -1, keepdims=True)).astype(BF).reshape(GROUP * BLK, KEYS)
            p[2 * h + a] = pr
            o = mm(pr, v).astype(BF)
            for g in range(GROUP):
                o_o[h * BLK : (h + 1) * BLK, (a * GROUP + g) * HS : (a * GROUP + g + 1) * HS] = o[
                    g * BLK : (g + 1) * BLK
                ]
        if h == 0:
            for k, t in ys:
                f = me.step("y", 4 - k)

                @pl.when(lax.div(f, 2) == me.zhi)
                def _():
                    ref = od.at[me.x, pl.ds(lax.rem(f, 2) * 8, 8)]
                    remote(ref, ref, sd.at[k], rdn.at[k], me.at(y=f)).wait_recv()

            da = Ring(me, "x", od.at[me.x], dx, ss.at[10], rs.at[10])
            da.first()
            wb.second()
            swap(oz, wb.l)
            swap(oz, wb.r)
            ez.second()
            ga2.second()

    start(pltpu.make_async_copy(p, p_o, ls.at[18]), keep_p)
    wb.last()
    swap(oz, wb.o)
    for n in range(8, 12):
        swapped(n)
    keep_o = pltpu.make_async_copy(oo, oo_o, ls.at[13])
    keep_o.start()

    ob = o_o[...]
    u3 = nt(ob, a3[...]).astype(BF)
    hid = x[...].astype(F32) + mm(ob, oo[...].reshape(D, D)) + mm(u3, bo[...])
    hid_o[...] = hid
    nv = (hid * rms(hid) * gain[...].astype(F32)).astype(BF)
    n2[:, :D] = nv
    n2[:, D:] = nt(nv, a45[...]).astype(BF)
    nz = ZGather(me, n2, xg, *nz_sems, BLK)
    nz.first()
    start(pltpu.make_async_copy(n2, xg.at[me.zlo, me.core, me.zhi], ls.at[19]), side)
    gb2.second()
    nz.second()
    da.second()
    off = FV * me.slice - 128 * window_tile(me.slice)

    def pack(r, strips, fresh):
        base = 256 * r - off
        i0 = jnp.minimum(lax.div(jnp.maximum(base, 0), 70), 11)
        if fresh:
            rw, cl = iota((256, 400), 0) + base, iota((256, 400), 1)
            i, k = i0 + lax.div(cl, 80), lax.rem(cl, 80)
            pick70[r] = jnp.where((k < 70) & (i * 70 + k == rw), 1.0, 0.0).astype(BF)
        for j in strips:
            src = od[j, pl.ds(i0, 5)].reshape(400, 384)
            at = pl.ds(pl.multiple_of(384 * j, 128), 384)
            down[256 * r : 256 * (r + 1), at] = mm(pick70[r], src).astype(BF)

    for r in range(5):
        pack(r, (da.i, da.l, da.r), True)
    nz.last()
    ez.last()
    da.last()
    for r in range(5):
        pack(r, (da.o,), False)
    keep_d = pltpu.make_async_copy(down, od_o, ls.at[20])
    keep_d.start()
    ga2.last()
    gb2.last()

    for r in (qa, qb, qa2, qb2, wa, wb, ga, gb, ga2, gb2, da):
        r.sent()
    for c in first + zc:
        c.wait_send()

    @pl.when(jnp.logical_not(keeper))
    def _():
        d_cross.wait_send()

    @pl.when(keeper)
    def _():
        for k, t in ys:
            remote(od.at[me.x, rows8], od.at[me.x, rows8], sd.at[k], rdn.at[k], me.at(y=t)).wait_send()

    def sent(k, carry):
        t = lax.rem(m + k, N_CTX)
        for half in range(2):
            block = m if half == 0 else NBLK - 1 - m

            @pl.when(reads(t, block))
            def _():
                src, dst = kv_own.at[half], kv.at[16 + block]
                remote(src, dst, sk.at[half, k], rk.at[block], (me.dp, t)).wait_send()

        return carry

    lax.fori_loop(1, N_CTX, sent, 0)
    for n, (dz, dc) in enumerate(ZK):
        z, core = me.step("z", 4 - dz if dz else 0), lax.rem(me.core + dc, 2)
        ref = oi.at[2 * lax.rem(z, 2) + core, lax.div(z, 2)]
        remote(ref, ref, si.at[n], ri.at[n], me.at(z=z, core=core)).wait_recv()
    ez.finish()
    nz.finish()
    for c in side + wins + keep_p + [keep_q, keep_o, keep_d]:
        c.wait()


def front(idx, wq, wo, wg, wd, eext, n1, ub, cos, sin, low, x, gain, a45, a3, bo):
    outs = (
        sds((2, 2, 4, 2, 48, 2048), BF),
        sds((2, 2, 4, 2, 48, D), BF),
        sds((4, 2, 2, 4, 2, 48, 640), BF),
        sds((FW, D), BF),
        sds((2, 2, 2, ROWS, DX), BF),
        sds((4, 2, 8, 128), jnp.int32),
        sds((2, NWB, BLK, 2 * KW), BF),
        sds((4, GROUP * BLK, KEYS), BF),
        sds((2, 2, 2, ROWS, DX), BF),
        sds((ROWS, D), BF),
        sds((ROWS, D), BF),
        sds((ROWS, D), F32),
        sds((ROWS, DX), BF),
    )
    four = (DMA((4,)),) * 4
    scratch = [
        pltpu.VMEM((4, 16, 2048), BF),
        pltpu.VMEM((4, 16, D), BF),
        pltpu.VMEM((4, 8, 16, 640), BF),
        pltpu.VMEM((80, D), BF),
        pltpu.VMEM((4, 80, 384), BF),
        pltpu.VMEM((48, 2048), BF),
        pltpu.VMEM((48, D), BF),
        pltpu.VMEM((8, 48, 640), BF),
        pltpu.VMEM((2, 2, 4, 2, 48, 2048), BF),
        pltpu.VMEM((2, 2, 4, 2, 48, D), BF),
        pltpu.VMEM((4, 16, 80, 384), BF),
        pltpu.VMEM((2, BLK, 2 * KW), BF),
        pltpu.VMEM((16 + NBLK, BLK, 2 * KW), BF),
        pltpu.VMEM((4, GROUP * BLK, KEYS), BF),
        pltpu.VMEM((FW, D), BF),
        pltpu.VMEM((5, 256, 400), BF),
        DMA((11, 4)),
        DMA((11, 4)),
        DMA((21,)),
        DMA((3, 11)),
        DMA((3, 11)),
        DMA((7,)),
        DMA((7,)),
        DMA((12,)),
        DMA((12,)),
        DMA((4,)),
        DMA((4,)),
        DMA((2, N_CTX)),
        DMA((NBLK,)),
        four,
        DMA((7,)),
        DMA((7,)),
        four,
    ]
    return pl.pallas_call(
        front_kernel,
        out_shape=outs,
        in_specs=[ANY, VM, VM, ANY, VM, ANY] + [VM] * 10,
        out_specs=[ANY] * 9 + [VM] * 4,
        scratch_shapes=scratch,
        compiler_params=pltpu.CompilerParams(collective_id=1, has_side_effects=True, vmem_limit_bytes=VMEM_LIMIT),
    )(idx, wq, wo, wg, wd, eext, n1, ub, cos, sin, low, x, gain, a45, a3, bo)


class Fan:
    def __init__(self, me, axis, view, send, recv):
        self.me, self.axis, self.view, self.send, self.recv = me, axis, view, send, recv
        self.i = getattr(me, axis)

    def copy(self, k, j, to):
        ref = self.view(j)
        return remote(ref, ref, self.send.at[k - 1], self.recv.at[k - 1], self.me.at(**{self.axis: to}))

    def first(self):
        self.out = []
        for k in (1, 3, 2):
            c = self.copy(k, self.i, self.me.step(self.axis, k))
            c.start()
            self.out.append(c)

    def last(self):
        for k in (1, 3, 2):
            f = self.me.step(self.axis, 4 - k)
            self.copy(k, f, f).wait_recv()

    def sent(self):
        for c in self.out:
            c.wait_send()


def norm_back(z, gain, grad):
    r = rms(z)
    t = gain * grad
    return r * t - z * (r * r * r) * jnp.mean(t * z, -1, keepdims=True)


def rear_kernel(
    xg, oe, og, wd_i, ad_all, b_all, e_i, hid_i, n2_i, q_i, o_i, p_i, win_i, wo_i, wq_i, x_i, n1_i,
    oi, a012, a3, a45, bqkv, bo, bd, gain1, gain2, cos, sin,
    out_o, gt_o, early, late,
    wgu, wdo, ad_in, b_in, ad, acc, xb, sib_out, sib_got, red, got2, ft,
    e, hid, n2, q, o, p, win, x, n1,
    gn2, ysum, gh, go, gq, gwin, got, gkv, gj, l1, l2, gf, gl1, gl2, red1, red2,
    wl, xl, ld, sb_s, sb_r, rz_s, rz_r, f_s, f_r, a_s, a_r, b_s, b_r, kv_s, kv_r, ls,
    ring_s, ring_r, fan_s, fan_r, core_s, core_r,
):
    me = Place()
    sib = me.sibling()
    m = me.ctx
    tile = window_tile(me.slice)
    off = FV * me.slice - 128 * tile
    bar = pltpu.get_barrier_semaphore()

    def hello(t, carry):
        @pl.when(t != m)
        def _():
            pl.semaphore_signal(bar, inc=1, device_id=(me.dp, t), device_id_type=MESH)

        return carry

    def load(src, dst, sem):
        c = pltpu.make_async_copy(src, dst, sem)
        c.start()
        return c

    cols = pl.ds(pl.multiple_of(tile * 128, 128), FW)
    wloads = [
        load(ad_all.at[:, :, cols], ad_in, wl.at[0]),
        load(b_all.at[:, :, :, cols], b_in, wl.at[1]),
    ]
    for k in range(4):
        wloads.append(load(og.at[k], wgu.at[pl.ds(0, D), pl.ds(640 * k, 640)], wl.at[2 + k]))
    wloads.append(load(wd_i, wdo.at[pl.ds(0, FW), pl.ds(0, D)], wl.at[6]))
    steps = [(1 - me.zlo, 1 - me.core), (1 - me.zlo, me.core), (me.zlo, 1 - me.core), (me.zlo, me.core)]

    def rows_in(n):
        zl, core = steps[n]
        return [load(src.at[zl, core], xb.at[n % 2, k], xl.at[n % 2, k]) for k, src in enumerate((xg, oe))]

    coming = [rows_in(0), rows_in(1)]
    lax.fori_loop(0, N_CTX, hello, 0)
    others = [me.at(z=me.step("z", 1)), me.at(z=me.step("z", 3)), sib]
    for d in others:
        pl.semaphore_signal(bar, inc=1, device_id=d, device_id_type=MESH)
    loads = [
        load(src, dst, ld.at[n])
        for n, (src, dst) in enumerate(
            (
                (e_i, e), (hid_i, hid), (n2_i, n2), (o_i, o), (q_i, q),
                (win_i, win), (p_i, p), (n1_i, n1), (x_i, x),
            )
        )
    ]
    for c in wloads[:2]:
        c.wait()
    row, col = iota((64, 128), 0), iota((64, 128), 1)
    choose = jnp.zeros((64, 128), F32)
    for k in range(4):
        hit = (lax.div(row, R) == k) & (lax.rem(row, R) == lax.rem(col, R)) & (lax.div(col, R) == oi[k, 0, :1, :1])
        choose += jnp.where(hit, 1.0, 0.0)
    choose = choose.astype(BF)
    fcol = iota((64, FW), 1)
    valid = (fcol >= off) & (fcol < off + FV)
    ad[:64] = jnp.where(valid, mm(choose, ad_in[...].reshape(128, FW)), 0.0).astype(BF)
    ad[64:] = jnp.zeros((64, FW), BF)
    eye = jnp.where(iota((EXT, EXT), 0) == iota((EXT, EXT), 1), 1.0, 0.0).astype(BF)
    wdo[:FW, D:] = tn(ad[...], eye).astype(BF)
    none = jnp.zeros((64, FW), BF)
    wgu[D : D + 64, :FW] = mm(choose, b_in[:, 0].reshape(128, FW)).astype(BF)
    wgu[D + 64 :, :FW] = none
    wgu[D : D + 64, FW:] = none
    wgu[D + 64 :, FW:] = mm(choose, b_in[:, 1].reshape(128, FW)).astype(BF)
    acc[...] = jnp.zeros_like(acc)
    for c in wloads[2:]:
        c.wait()
    pl.semaphore_wait(bar, N_CTX - 1 + len(others))
    sib_copies, z_copies = [], []

    def z_push(j, k, slot, z):
        c = remote(red.at[j, k], got2.at[slot, k], rz_s.at[j, k], rz_r.at[slot, k], me.at(z=z))
        c.start()
        z_copies.append(c)

    for n in range(4):
        for c in coming[n]:
            c.wait()
        xv = xb[n % 2, 0].reshape(2 * ROWS, DX)
        ev = xb[n % 2, 1].reshape(2 * ROWS, DX)
        both = mm(xv, wgu[...])
        gate, up = both[:, :FW], both[:, FW:]
        gm = nt(ev, wdo[:FW])
        sig = 1.0 / (1.0 + jnp.exp(-gate))
        sl = gate * sig
        act = (sl * up).astype(BF)
        gg = (gm * up * (sig * (1.0 + gate * (1.0 - sig)))).astype(BF)
        gu = (gm * sl).astype(BF)
        grads = jnp.concatenate([gg, gu], 1)
        acc[0] += tn(ev[:, D:], act)[:64]
        by_u = tn(xv[:, D:], grads)
        acc[1] += by_u[:64, :FW]
        acc[2] += by_u[64:, FW:]
        if n < 2:
            coming.append(rows_in(n + 2))
        for k in (1, 0):
            wide = nt(grads, wgu[...]) if k == 1 else mm(act, wdo[:FW])
            total = gn2 if k == 1 else ysum
            if n % 2 == 0:
                for zh in range(2):
                    rows = slice(zh * ROWS, (zh + 1) * ROWS)
                    sib_out[n // 2, k, zh] = wide[rows].astype(BF)
                c = remote(sib_out.at[n // 2, k], sib_got.at[n // 2, k], sb_s.at[n // 2, k], sb_r.at[n // 2, k], sib)
                c.start()
                sib_copies.append(c)
            else:
                theirs = sib_got.at[n // 2, k]
                remote(theirs, theirs, sb_s.at[n // 2, k], sb_r.at[n // 2, k], sib).wait_recv()
                if n == 1:
                    for zh in range(2):
                        rows = slice(zh * ROWS, (zh + 1) * ROWS)
                        red[zh, k] = (wide[rows] + theirs[zh].astype(F32)).astype(BF)
                        z_push(zh, k, me.zhi, 2 * zh + 1 - me.zlo)
                else:
                    mine = me.zhi == 1
                    far = jnp.where(mine, wide[:ROWS], wide[ROWS:])
                    near = jnp.where(mine, wide[ROWS:], wide[:ROWS])
                    red[2, k] = (far + theirs[1 - me.zhi].astype(F32)).astype(BF)
                    z_push(2, k, 2, me.step("z", 2))
                    total[...] = near + theirs[me.zhi].astype(F32)
    for k in range(3):
        v = jnp.where(valid, acc[k], 0.0).astype(BF)
        for i in range(4):
            for t in range(10):
                ft[i * 30 + k * 10 + t] = v[R * i : R * (i + 1), 128 * t : 128 * (t + 1)]
    for t in range(120, 128):
        ft[t] = jnp.zeros((R, 128), BF)
    xy = me.y * 4 + me.x

    def plane(k):
        return me.at(x=lax.rem(k, 4), y=lax.div(k, 4))

    def f_copy(t):
        return remote(ft.at[pl.ds(8 * t, 8)], gf.at[xy], f_s.at[t], f_r.at[xy], plane(t))

    def f_send(k, carry):
        f_copy(lax.rem(xy + k, 16)).start()
        return carry

    lax.fori_loop(1, 16, f_send, 0)
    gf[xy] = ft[pl.ds(8 * xy, 8)]
    wo_load = load(wo_i, wdo.at[:, pl.ds(0, D)], ld.at[9])
    wq_load = load(wq_i, wgu.at[pl.ds(0, D), pl.ds(0, 2048)], ld.at[10])

    def z_take(k, total):
        for slot in range(3):
            ref = got2.at[slot, k]
            remote(ref, ref, rz_s.at[slot, k], rz_r.at[slot, k], sib).wait_recv()
            total[...] += ref[...].astype(F32)

    z_take(1, gn2)
    for c in loads[:4] + [wo_load]:
        c.wait()

    def put(tiles, at, v):
        for t in range(v.shape[1] // 128):
            tiles[at + t] = v[:, 128 * t : 128 * (t + 1)].astype(BF)

    gue = gn2[:, D:].astype(BF)
    gn = gn2[:, :D] + mm(gue, a45[...])
    ghv = e[:, :D].astype(F32) + norm_back(hid[...], gain2[...].astype(F32), gn)
    gh[...] = ghv
    ghb = ghv.astype(BF)
    ob = o[...]
    gu3 = nt(ghb, bo[...]).astype(BF)
    go[...] = (nt(ghb, wdo[:, :D]) + mm(gu3, a3[...])).astype(BF)
    u3 = nt(ob, a3[...]).astype(BF)
    s = me.dp

    put(l1, 0, tn(gu3, ob))
    g45b = tn(gue, n2[:, :D]).astype(BF)
    pick_own = jnp.where((iota((R, EXT), 1) == iota((R, EXT), 0) + s * R), 1.0, 0.0).astype(BF)
    pick_up = jnp.where((iota((R, EXT), 1) == iota((R, EXT), 0) + s * R + 64), 1.0, 0.0).astype(BF)
    put(l1, 12, mm(pick_own, g45b))
    put(l1, 24, mm(pick_up, g45b))
    put(l1, 36, tn(u3, ghb))
    for t in range(48, 64):
        l1[t] = jnp.zeros((R, 128), BF)

    def l_copy(tiles, buf, ss, rs, t):
        return remote(tiles.at[pl.ds(2 * t, 2)], buf.at[m], ss.at[t], rs.at[m], (me.dp, t))

    def l_send(tiles, buf, ss, rs):
        def one(k, carry):
            l_copy(tiles, buf, ss, rs, lax.rem(m + k, N_CTX)).start()
            return carry

        lax.fori_loop(1, N_CTX, one, 0)
        buf[m] = tiles[pl.ds(2 * m, 2)]

    def l_sum(buf, ss, rs):
        def one(k, carry):
            t = lax.rem(m + k, N_CTX)
            remote(buf.at[t], buf.at[t], ss.at[t], rs.at[t], (me.dp, t)).wait_recv()
            return carry + buf[t].astype(F32)

        return lax.fori_loop(1, N_CTX, one, buf[m].astype(F32)).astype(BF)

    def l_sent(tiles, buf, ss, rs):
        def one(k, carry):
            l_copy(tiles, buf, ss, rs, lax.rem(m + k, N_CTX)).wait_send()
            return carry

        lax.fori_loop(1, N_CTX, one, 0)

    l_send(l1, gl1, a_s, a_r)

    def covers(t, w, owner, h):
        block = owner if h == 0 else NBLK - 1 - owner
        j = block - ((t if w == 0 else NBLK - 1 - t) - (NWB - 1))
        return j, (j >= 0) & (j < NWB)

    def kv_copy(w, h, t, j):
        return remote(gwin.at[w, j], got.at[h, w, j], kv_s.at[h, w, t], kv_r.at[h, w, j], (me.dp, t))

    for c in loads[4:7]:
        c.wait()
    for w in range(2):
        for a in range(KV_HEADS):
            qs, gv, ov = stack_heads(q, w, a), stack_heads(go, w, a), stack_heads(o, w, a)
            k = win[w, :, :, a * HS : (a + 1) * HS].reshape(KEYS, HS)
            v = win[w, :, :, KW + a * HS : KW + (a + 1) * HS].reshape(KEYS, HS)
            pr = p[2 * w + a]
            delta = jnp.sum(gv.astype(F32) * ov.astype(F32), -1, keepdims=True)
            ds = (pr.astype(F32) * (nt(gv, v) - delta)).astype(BF)
            gqv = mm(ds, k) * SCALE
            for g in range(GROUP):
                cols = slice((a * GROUP + g) * HS, (a * GROUP + g + 1) * HS)
                gq[w * BLK : (w + 1) * BLK, cols] = gqv[g * BLK : (g + 1) * BLK]
            gwin[w, :, :, a * HS : (a + 1) * HS] = (tn(ds, qs) * SCALE).astype(BF).reshape(NWB, BLK, HS)
            gwin[w, :, :, KW + a * HS : KW + (a + 1) * HS] = tn(pr, gv).astype(BF).reshape(NWB, BLK, HS)

        def kv_send(k, carry):
            t = lax.rem(m + k, N_CTX)
            for h in range(2):
                j, ok = covers(m, w, t, h)

                @pl.when(ok)
                def _():
                    kv_copy(w, h, t, j).start()

            return carry

        lax.fori_loop(1, N_CTX, kv_send, 0)
        for h in range(2):
            j, ok = covers(m, w, m, h)

            @pl.when(ok)
            def _():
                c = pltpu.make_async_copy(gwin.at[w, j], got.at[h, w, j], ls.at[2 * w + h])
                c.start()
                c.wait()


    def f_take(k, carry):
        t = lax.rem(xy + k, 16)
        remote(gf.at[t], gf.at[t], f_s.at[t], f_r.at[t], plane(t)).wait_recv()
        return carry + gf[t].astype(F32)

    red1[:8] = lax.fori_loop(1, 16, f_take, gf[xy].astype(F32)).astype(BF)
    red1[8:] = l_sum(gl1, a_s, a_r)

    def vz(j, h):
        ref = early.at[me.y, me.x, lax.rem(j, 2), me.core, lax.div(j, 2)]
        return ref if h is None else ref.at[pl.ds(5 * h, 5)]

    own_e = pltpu.make_async_copy(red1, vz(me.z, None), ls.at[5])
    own_e.start()
    rz = Ring(me, "z", red1, vz, ring_s.at[0], ring_r.at[0])
    rz.first()
    ta, tb = pl.ds(0, 5), pl.ds(5, 5)

    def x0(j, h):
        return early.at[me.y, j, :, me.core, :, ta] if h is None else early.at[me.y, j, h, me.core, :, ta]

    def y0(j, h):
        return early.at[j, :, :, me.core, :, ta] if h is None else early.at[j, pl.ds(2 * h, 2), :, me.core, :, ta]

    def y1(j, h):
        return early.at[j, me.x, :, me.core, :, tb] if h is None else early.at[j, me.x, h, me.core, :, tb]

    def x1(j, h):
        return early.at[:, j, :, me.core, :, tb] if h is None else early.at[pl.ds(2 * h, 2), j, :, me.core, :, tb]

    gkv[...] = jnp.zeros_like(gkv)

    def take(k, carry):
        t = lax.rem(m + N_CTX - k, N_CTX)
        for w in range(2):
            for h in range(2):
                j, ok = covers(t, w, m, h)

                @pl.when(ok & (k > 0))
                def _():
                    ref = got.at[h, w, j]
                    remote(ref, ref, kv_s.at[h, w, t], kv_r.at[h, w, j], (me.dp, t)).wait_recv()

                @pl.when(ok)
                def _():
                    gkv[h] += got[h, w, j].astype(F32)

        return carry

    lax.fori_loop(0, N_CTX, take, 0)
    rz.second()
    rz.last()
    own_e.wait()
    ra = Ring(me, "x", x0(me.x, None), x0, ring_s.at[1], ring_r.at[1])
    rb = Ring(me, "y", y1(me.y, None), y1, ring_s.at[2], ring_r.at[2])
    ra.first()
    rb.first()

    ra.second()
    rb.second()

    for c in loads[7:] + [wq_load]:
        c.wait()
    c, sn = cos[...], sin[...]
    for h in range(HEADS):
        cols = slice(h * HS, (h + 1) * HS)
        gj[:, cols] = turn_back(gq[:, cols], c, sn).astype(BF)
    for a in range(KV_HEADS):
        v = jnp.concatenate([gkv[0, :, a * HS : (a + 1) * HS], gkv[1, :, a * HS : (a + 1) * HS]], 0)
        gj[:, QW + a * HS : QW + (a + 1) * HS] = turn_back(v, c, sn).astype(BF)
    gj[:, QW + KW :] = jnp.concatenate([gkv[0, :, KW:], gkv[1, :, KW:]], 0).astype(BF)
    n1b = n1[...]
    more = jnp.zeros((ROWS, D), F32)
    for i, (lo, hi) in enumerate(((0, QW), (QW, QW + KW), (QW + KW, QW + 2 * KW))):
        am = a012[i]
        u = nt(n1b, am).astype(BF)
        gjm = gj[:, lo:hi]
        gum = nt(gjm, bqkv[:, lo:hi]).astype(BF)
        more += mm(gum, am)
        put(l2, 36 + lo // 128, tn(u, gjm))
        put(l2, 12 * i, tn(gum, n1b))
    z_take(0, ysum)
    ud = ysum[:, D:].astype(BF)
    y = hid[...] + ysum[:, :D] + mm(ud, bd[...])
    for h in range(2):
        out_o[:, h, :] = y[h * BLK : (h + 1) * BLK].astype(BF)
    put(l2, 52, mm(pick_own, tn(ud, e[:, :D]).astype(BF)))
    l_send(l2, gl2, b_s, b_r)
    ra.last()
    rb.last()
    rc = Ring(me, "y", y0(me.y, None), y0, ring_s.at[3], ring_r.at[3])
    rd = Ring(me, "x", x1(me.x, None), x1, ring_s.at[4], ring_r.at[4])
    rc.first()
    rd.first()
    gn = nt(gj[...], wgu[:D, :2048]) + more
    gt = gh[...] + norm_back(x[...].astype(F32), gain1[...].astype(F32), gn)
    for h in range(2):
        gt_o[:, h, :] = gt[h * BLK : (h + 1) * BLK].astype(BF)

    red2[...] = l_sum(gl2, b_s, b_r)

    def uz(j):
        return late.at[me.y, me.x, lax.rem(j, 2), me.core, lax.div(j, 2)]

    own_l = pltpu.make_async_copy(red2, uz(me.z), ls.at[6])
    own_l.start()
    own_l.wait()
    fz = Fan(me, "z", uz, fan_s.at[0], fan_r.at[0])
    fz.first()
    rc.second()
    rd.second()
    fz.last()

    def ux(j):
        return late.at[me.y, j, :, me.core]

    def uy(j):
        return late.at[j, :, :, me.core]

    fx = Fan(me, "x", ux, fan_s.at[1], fan_r.at[1])
    fx.first()
    rc.last()
    rd.last()
    swaps = []

    def swap(view, n):
        c = remote(view(me.core), view(me.core), core_s.at[n], core_r.at[n], sib)
        c.start()
        swaps.append((c, view, n))

    for k in range(4):
        swap(lambda core, k=k: early.at[k, :, :, core], k)
    fx.last()
    fy = Fan(me, "y", uy, fan_s.at[2], fan_r.at[2])
    fy.first()
    fy.last()
    for k in range(4):
        swap(lambda core, k=k: late.at[k, :, :, core], 4 + k)

    for c in sib_copies + z_copies:
        c.wait_send()
    for r in (rz, ra, rb, rc, rd, fz, fx, fy):
        r.sent()

    def f_sent(k, carry):
        f_copy(lax.rem(xy + k, 16)).wait_send()
        return carry

    lax.fori_loop(1, 16, f_sent, 0)
    l_sent(l1, gl1, a_s, a_r)
    l_sent(l2, gl2, b_s, b_r)

    def kv_sent(k, carry):
        t = lax.rem(m + k, N_CTX)
        for w in range(2):
            for h in range(2):
                j, ok = covers(m, w, t, h)

                @pl.when(ok)
                def _():
                    kv_copy(w, h, t, j).wait_send()

        return carry

    lax.fori_loop(1, N_CTX, kv_sent, 0)
    for c, view, n in swaps:
        c.wait_send()
        ref = view(1 - me.core)
        remote(ref, ref, core_s.at[n], core_r.at[n], sib).wait_recv()


def rear(xg, oe, og, wd, ad_all, b_all, e, hid, n2, q, o, p, win, wo, wq, x, n1, *small):
    outs = (
        sds((BLK, 2, D), BF),
        sds((BLK, 2, D), BF),
        sds((4, 4, 2, 2, 2, 10, R, 128), BF),
        sds((4, 4, 2, 2, 2, 2, R, 128), BF),
    )
    block = (ROWS, DX)
    scratch = [
        pltpu.VMEM((DX, 2 * FW), BF),
        pltpu.VMEM((D, DX), BF),
        pltpu.VMEM((ADAPT, R, FW), BF),
        pltpu.VMEM((ADAPT, 2, R, FW), BF),
        pltpu.VMEM((EXT, FW), BF),
        pltpu.VMEM((3, 64, FW), F32),
        pltpu.VMEM((2, 2, 2) + block, BF),
        pltpu.VMEM((2, 2, 2) + block, BF),
        pltpu.VMEM((2, 2, 2) + block, BF),
        pltpu.VMEM((3, 2) + block, BF),
        pltpu.VMEM((3, 2) + block, BF),
        pltpu.VMEM((128, R, 128), BF),
    ]
    scratch += [pltpu.VMEM(v.shape, v.dtype) for v in (e, hid, n2, q, o, p, win, x, n1)]
    scratch += [
        pltpu.VMEM(block, F32),
        pltpu.VMEM(block, F32),
        pltpu.VMEM((ROWS, D), F32),
        pltpu.VMEM((ROWS, D), BF),
        pltpu.VMEM((ROWS, D), F32),
        pltpu.VMEM((2, NWB, BLK, 2 * KW), BF),
        pltpu.VMEM((2, 2, NWB, BLK, 2 * KW), BF),
        pltpu.VMEM((2, BLK, 2 * KW), F32),
        pltpu.VMEM((ROWS, 2048), BF),
        pltpu.VMEM((64, R, 128), BF),
        pltpu.VMEM((64, R, 128), BF),
        pltpu.VMEM((16, 8, R, 128), BF),
        pltpu.VMEM((N_CTX, 2, R, 128), BF),
        pltpu.VMEM((N_CTX, 2, R, 128), BF),
        pltpu.VMEM((10, R, 128), BF),
        pltpu.VMEM((2, R, 128), BF),
        DMA((7,)),
        DMA((2, 2)),
        DMA((11,)),
        DMA((2, 2)),
        DMA((2, 2)),
        DMA((3, 2)),
        DMA((3, 2)),
        DMA((16,)),
        DMA((16,)),
        DMA((N_CTX,)),
        DMA((N_CTX,)),
        DMA((N_CTX,)),
        DMA((N_CTX,)),
        DMA((2, 2, N_CTX)),
        DMA((2, 2, NWB)),
        DMA((7,)),
        DMA((5, 4)),
        DMA((5, 4)),
        DMA((3, 3)),
        DMA((3, 3)),
        DMA((8,)),
        DMA((8,)),
    ]
    return pl.pallas_call(
        rear_kernel,
        out_shape=outs,
        in_specs=[ANY] * 17 + [VM] * len(small),
        out_specs=[VM, VM, ANY, ANY],
        scratch_shapes=scratch,
        compiler_params=pltpu.CompilerParams(collective_id=2, has_side_effects=True, vmem_limit_bytes=VMEM_LIMIT),
    )(xg, oe, og, wd, ad_all, b_all, e, hid, n2, q, o, p, win, wo, wq, x, n1, *small)


def spread_kernel(oi, early, late, ain_o, aff_o, bqkv_o, bres_o, bff_o):
    e = pl.program_id(0)
    for ref in (ain_o, aff_o, bqkv_o, bres_o, bff_o):
        ref[...] = jnp.zeros_like(ref)

    def local_tile(ref, at, s, n):
        k, j = n // 2, n % 2
        return ref[k // 8, k % 4, s // 2, s % 2, (k // 4) % 2, at + j].astype(F32)

    def ff_tile(piece, n):
        k, j = n // 8, n % 8
        return early[k // 4, k % 4, piece // 4, (piece // 2) % 2, piece % 2, j].astype(F32)

    for s in range(4):

        @pl.when(oi[s, 0, 0, 0] == e)
        def _():
            for c in range(12):
                cols = slice(128 * c, 128 * (c + 1))
                for m in range(3):
                    ain_o[0, m, :, cols] += local_tile(late, 0, s, 12 * m + c)
                    ain_o[0, 3 + m, :, cols] += local_tile(early, 8, s, 12 * m + c)
                bres_o[0, 0, :, cols] += local_tile(early, 8, s, 36 + c)
                bres_o[0, 1, :, cols] += local_tile(late, 0, s, 52 + c)
            for c in range(16):
                bqkv_o[0, :, 128 * c : 128 * (c + 1)] += local_tile(late, 0, s, 36 + c)
            for piece in range(8):
                tile = 60 if piece == 7 else 35 * piece // 4
                for k in range(3):
                    for c in range(10):
                        cols = slice(128 * (tile + c), 128 * (tile + c + 1))
                        v = ff_tile(piece, s * 30 + k * 10 + c)
                        if k == 0:
                            aff_o[0, :, cols] += v
                        else:
                            bff_o[0, k - 1, :, cols] += v


def spread(oi, early, late):
    outs = (
        sds((ADAPT, 6, R, D), F32),
        sds((ADAPT, R, FF), F32),
        sds((ADAPT, R, 2048), F32),
        sds((ADAPT, 2, R, D), F32),
        sds((ADAPT, 2, R, FF), F32),
    )

    def one(shape):
        return pl.BlockSpec((1,) + shape[1:], lambda i: (i,) + (0,) * (len(shape) - 1))

    return pl.pallas_call(
        spread_kernel,
        out_shape=outs,
        grid=(ADAPT,),
        in_specs=[
            SM,
            pl.BlockSpec(early.shape, lambda i: (0,) * 8),
            pl.BlockSpec(late.shape, lambda i: (0,) * 8),
        ],
        out_specs=[one(o.shape) for o in outs],
        compiler_params=pltpu.CompilerParams(vmem_limit_bytes=VMEM_LIMIT),
    )(oi, early, late)


def local(
    tokens,
    cotangent,
    w_qkv,
    b_qkv,
    w_out,
    w_gu,
    w_down,
    gain_attn,
    gain_mlp,
    adapt_in,
    adapt_in_ff,
    adapt_out_qkv,
    adapt_out_res,
    adapt_out_ff,
    doc_lengths,
    adapter_index,
    window,
):
    member = lax.axis_index("ctx")
    starts = jnp.stack([member * BLK, (NBLK - 1 - member) * BLK])
    pos = (starts[:, None] + jnp.arange(BLK, dtype=jnp.int32)[None]).reshape(ROWS)
    ends = jnp.cumsum(doc_lengths[0])
    begin = jnp.max(jnp.where(ends[None] <= pos[:, None], ends[None], 0), -1)
    low = jnp.maximum(begin, pos - window[0] + 1)
    low = jnp.broadcast_to(low[:, None], (ROWS, 128)).astype(jnp.int32)
    freq = 1000000.0 ** (-(2.0 * jnp.arange(HS // 2, dtype=F32)) / HS)
    ang = pos.astype(F32)[:, None] * freq[None]
    c, sn = jnp.cos(ang), jnp.sin(ang)
    cos = jnp.concatenate([c, c], -1)
    sin = jnp.concatenate([-sn, sn], -1)

    wg = jnp.pad(jnp.transpose(w_gu, (1, 0, 2)), ((0, 0), (0, 4), (0, 0)))
    idx_row = jnp.broadcast_to(adapter_index[:, None], (8, 128)).astype(jnp.int32)

    x, n1, eext, ub, a45, bd, a3, bo, a012, bqkv = prepare(
        adapter_index, tokens[0], cotangent[0], adapt_in, adapt_out_qkv, adapt_out_res, gain_attn, b_qkv
    )
    oq, oo, og, down, oe, oi, wins, p, xg, q, o, hid, n2 = front(
        idx_row, w_qkv, w_out, wg, w_down, eext, n1, ub, cos, sin, low, x, gain_mlp, a45, a3, bo
    )
    oq = oq.reshape(D, 2048)
    oo = oo.reshape(D, D)
    og = og.reshape(4, D, 640)
    out, gt, early, late = rear(
        xg, oe, og, down, adapt_in_ff, adapt_out_ff, eext, hid, n2, q, o, p, wins, oo, oq, x, n1,
        oi, a012, a3, a45, bqkv, bo, bd, gain_attn, gain_mlp, cos, sin,
    )
    return (out[None], gt[None]) + tuple(spread(oi, early, late))


def solution(mesh):
    return jax.shard_map(
        local,
        mesh=mesh,
        in_specs=(
            P("dp", "ctx", None, None),
            P("dp", "ctx", None, None),
            P(("dp", "ctx"), None),
            P(),
            P(("dp", "ctx"), None),
            P(("dp", "ctx"), None, None),
            P(("dp", "ctx"), None),
            P(),
            P(),
            P(),
            P(),
            P(),
            P(),
            P(),
            P("dp", None),
            P("dp"),
            P("dp"),
        ),
        out_specs=(P("dp", "ctx", None, None), P("dp", "ctx", None, None), P(), P(), P(), P(), P()),
        check_vma=False,
    )
```

time: 436 us -> 325 us (0.75)
  Pallas kernels: 418 us -> 312 us
    pallas_call x8 -> x2, Pallas kernels: 241 us -> 163 us  [the longest x1 151 us: rear(): pl.pallas_call(rear_kernel, out_shape=outs, in_specs=[ANY] * 17 + [VM] *...]
    pallas_call x1, Pallas kernels: 172 us -> 144 us  [front(): pl.pallas_call(front_kernel, out_shape=outs, in_specs=[ANY, VM, VM, ANY,...]
where the time goes in v3:
time: 325 us; the launch traced here: 321 us
  Pallas kernels  312 us (96%)
  local copies, waits for them, and re-layouts  4.82 us (1%)
    pallas_call x1, Pallas kernels, rear(): pl.pallas_call(rear_kernel, out_shape=outs, in_specs=[ANY] * 17 + [VM] *...  151 us
    pallas_call x1, Pallas kernels, front(): pl.pallas_call(front_kernel, out_shape=outs, in_specs=[ANY, VM, VM, ANY,...  144 us
    pallas_call x1, Pallas kernels, spread(): pl.pallas_call(spread_kernel, out_shape=outs, grid=(ADAPT,), in_specs=[SM...  11.1 us

profile of v3, /device:TPU:1, one launch (start us, length us, event | category | flops | bytes accessed | tf_op | source)
XLA Modules:
  0.0 321.2 jit_solution(16164254730837196493)
XLA Ops:
  1.9 0.1 pad_add_fusion
  2.0 0.8 reduce-window.8
  2.8 0.1 iota_add_fusion
  2.9 0.1 add.42
  3.0 0.1 select_reduce_fusion
  3.1 0.6 broadcast_in_dim.21.idx
  3.7 0.7 broadcast_in_dim.23.low
  4.4 0.3 fusion
  4.7 0.8 pad_maximum_fusion
  5.5 1.1 copy.27
  6.6 0.9 pad.4.wg
  7.4 5.5 %shard_map.216 = (bf16[128,1536]{1,0:T(8,128)(2,1)}, bf16[128,1536]{1,0:T(8,128)(2,1)}, bf16[128,1664]{1,0:T(8,128)(2,1)}, f32[128,2048]{1,0:T(8,128)}, bf16[128...) custom-call(s32[1]{0:T(128)} %copy.30.idx, ...), custom_call_target="tpu_custom_call" | custom-call | tf_op jit(solution)/shard_map/pallas_call | solution.py:233
  12.9 144.0 %shard_map.217 = (bf16[2,2,4,2,48,2048]{5,4,3,2,1,0:T(8,128)(2,1)}, bf16[2,2,4,2,48,1536]{5,4,3,2,1,0:T(8,128)(2,1)}, bf16[4,2,2,4,2,48,640]{6,5,4,3,2,1,0:T(8,1...) custom-call(s32[8,128]{1,0:T(8,128)} %broadcast_in_dim.21.idx, ...), custom_call_target="tpu_custom_call" | custom-call | tf_op jit(solution)/shard_map/pallas_call | solution.py:747
  156.9 151.5 %shard_map.218 = (bf16[64,2,1536]{2,1,0:T(2,128)(2,1)}, bf16[64,2,1536]{2,1,0:T(2,128)(2,1)}, bf16[4,4,2,2,2,10,16,128]{7,6,5,4,3,2,1,0:T(8,128)(2,1)}, bf16[4,4,2,2,2,2,16,128]{7,6,5,4,3,2,1,0:T(8,128)(2,1)}) custom-call(bf16[2,2,2,128,1664]{4,3,2,1,0:T(8,128)(2,1)} %get-tuple-element.46.xg, bf16[2,2,2,128,1664]{4,3,2,1,0:T(8,128)(2,1)} %get-tuple-element.47.oe, ...), custom_call_target="tpu_custom_call" | custom-call | tf_op jit(solution)/shard_map/pallas_call | solution.py:1289
  308.4 0.0 copy-start.1
  308.4 0.0 copy-start
  308.4 11.1 %shard_map.219 = (f32[8,6,16,1536]{3,2,1,0:T(8,128)}, f32[8,16,8960]{2,1,0:T(8,128)}, f32[8,16,2048]{2,1,0:T(8,128)}, f32[8,2,16,1536]{3,2,1,0:T(8,128)}, f32[8,2,16,8960]{3,2,1,0:T(8,128)}) custom-call(s32[4,2,8,128]{3,2,1,0:T(8,128)} %get-tuple-element.58.oi, bf16[4,4,2,2,2,10,16,128]{7,6,5,4,3,2,1,0:T(8,128)(2,1)} %get-tuple-element.64.early, ...), custom_call_target="tpu_custom_call" | custom-call | tf_op jit(solution)/shard_map/pallas_call | solution.py:1349
  319.6 0.0 copy-done.1
  319.6 0.7 copy.32
  320.3 0.0 copy-done
  320.3 0.7 copy.33
  (2 shorter events, 0.0 us)
Async XLA Ops:
  308.4 11.1 %copy-start.1 = (bf16[64,2,1536]{2,1,0:T(2,128)(2,1)S(1)}, bf16[64,2,1536]{2,1,0:T(2,128)(2,1)}, u32[]{:S(2)}) copy-start(bf16[64,2,1536]{2,1,0:T(2,128)(2,1)} %get-tuple-element.62) | copy-start | bytes 1179652
  308.4 11.9 %copy-start = (bf16[64,2,1536]{2,1,0:T(2,128)(2,1)S(1)}, bf16[64,2,1536]{2,1,0:T(2,128)(2,1)}, u32[]{:S(2)}) copy-start(bf16[64,2,1536]{2,1,0:T(2,128)(2,1)} %get-tuple-element.63) | copy-start | bytes 1179652

commit v4 on v3

--- a/solution.py
+++ b/solution.py
@@ -184,73 +184,6 @@
     return lax.rsqrt(jnp.mean(z * z, -1, keepdims=True) + EPS)
 
 
-def prepare_kernel(idx, tok, cot, a_in, b_qkv_ad, b_res, gain, bias, x_o, n1_o, e_o, ub_o, a45_o, bd_o, a3_o, bo_o, a012_o, bqkv_o):
-    s = lax.axis_index("dp")
-    for h in range(2):
-        rows = slice(h * BLK, (h + 1) * BLK)
-        x_o[rows] = tok[:, h, :]
-        e_o[rows, :D] = cot[:, h, :]
-    x = x_o[...].astype(F32)
-    n1 = (x * rms(x) * gain[...].astype(F32)).astype(BF)
-    n1_o[...] = n1
-    for m, (lo, hi) in enumerate(((0, QW), (QW, QW + KW), (QW + KW, QW + 2 * KW))):
-        u = nt(n1, a_in[0, m]).astype(BF)
-        ub_o[:, lo:hi] = mm(u, b_qkv_ad[0, :, lo:hi]) + bias[lo:hi].astype(F32)
-    at = pl.multiple_of(s * R, R)
-    a45_o[...] = jnp.zeros_like(a45_o)
-    a45_o[pl.ds(at, R), :] = a_in[0, 4]
-    a45_o[pl.ds(at + 64, R), :] = a_in[0, 5]
-    bd_o[...] = jnp.zeros_like(bd_o)
-    bd_o[pl.ds(at, R), :] = b_res[0, 1]
-    a3_o[...] = a_in[0, 3]
-    bo_o[...] = b_res[0, 0]
-    a012_o[...] = a_in[0, :3]
-    bqkv_o[...] = b_qkv_ad[0]
-    e_o[:, D:] = nt(e_o[:, :D], bd_o[...]).astype(BF)
-
-
-def pick(shape):
-    return pl.BlockSpec((1,) + shape[1:], lambda i, idx: (idx[0],) + (0,) * (len(shape) - 1))
-
-
-def whole(shape):
-    return pl.BlockSpec(shape, lambda i, idx: (0,) * len(shape))
-
-
-def prepare(idx, tok, cot, a_in, b_qkv_ad, b_res, gain, bias):
-    outs = (
-        sds((ROWS, D), BF),
-        sds((ROWS, D), BF),
-        sds((ROWS, DX), BF),
-        sds((ROWS, 2048), F32),
-        sds((EXT, D), BF),
-        sds((EXT, D), BF),
-        sds((R, D), BF),
-        sds((R, D), BF),
-        sds((3, R, D), BF),
-        sds((R, 2048), BF),
-    )
-    return pl.pallas_call(
-        prepare_kernel,
-        out_shape=outs,
-        grid_spec=pltpu.PrefetchScalarGridSpec(
-            num_scalar_prefetch=1,
-            grid=(1,),
-            in_specs=[
-                whole((BLK, 2, D)),
-                whole((BLK, 2, D)),
-                pick(a_in.shape),
-                pick(b_qkv_ad.shape),
-                pick(b_res.shape),
-                whole((D,)),
-                whole((2048,)),
-            ],
-            out_specs=[whole(o.shape) for o in outs],
-        ),
-        compiler_params=pltpu.CompilerParams(vmem_limit_bytes=VMEM_LIMIT),
-    )(idx, tok, cot, a_in, b_qkv_ad, b_res, gain, bias)
-
-
 def turn(v, cos, sin):
     return v * cos + pltpu.roll(v, 64, 1) * sin
 
@@ -275,9 +208,10 @@
 
 
 def front_kernel(
-    idx, wq_i, wo_i, wg, wd_i, eext, n1, ub, cos, sin, low, x, gain, a45, a3, bo,
+    idx_i, docs, span, wq_i, wo_i, wg_i, wd_i, tok, cot, ain_i, aqkv_i, ares_i, gain1, bias, cos, sin, gain,
     oq_o, oo_o, og, od_o, oe, oi, win_o, p_o, xg, q, o_o, hid_o, n2,
-    rq, ro, rg, wdp, rd, cq, co, cg, oq, oo, od, kv_own, kv, p, down, pick70,
+    x, n1, eext, a45, bd, a3, bo, a012, bqkv,
+    ub, idx, wg, ain, aqkv, ares, rq, ro, rg, wdp, rd, cq, co, cg, oq, oo, od, kv_own, kv, p, down, pick70,
     ss, rs, ls, s1, r1, s2, r2, sc, rc, sd, rdn, sk, rk, ez_sems, si, ri, nz_sems,
 ):
     me = Place()
@@ -297,13 +231,17 @@
     for d in others:
         pl.semaphore_signal(bar, inc=1, device_id=d, device_id_type=MESH)
 
+    adapters = []
+    for n, (src, dst) in enumerate(((ain_i, ain), (aqkv_i, aqkv), (ares_i, ares))):
+        adapters.append(pltpu.make_async_copy(src, dst, ls.at[21 + n]))
+        adapters[-1].start()
     rq[me.x, :12] = wq_i[...]
     rq[me.x, 12:] = jnp.zeros((4, 2048), BF)
     ro[me.x, :12] = wo_i[...]
     ro[me.x, 12:] = jnp.zeros((4, D), BF)
     wdp[:70] = wd_i[...]
     wdp[70:] = jnp.zeros((10, D), BF)
-    kv[:16] = jnp.zeros((16, BLK, 2 * KW), BF)
+    idx[...] = jnp.full((8, 128), idx_i[0], jnp.int32)
 
     pl.semaphore_wait(bar, N_CTX - 1 + len(others))
 
@@ -326,6 +264,9 @@
         start(remote(rq.at[me.x], rq.at[me.x], s1.at[k - 1, 0], r1.at[k - 1, 0], d), first)
     for k, t, d in xs:
         start(remote(ro.at[me.x], ro.at[me.x], s1.at[k - 1, 1], r1.at[k - 1, 1], d), first)
+    for k in range(2):
+        wg[k, :12] = wg_i[:, k, :]
+        wg[k, 12:] = jnp.zeros((4, FF), BF)
     for k, t, d in xs:
         for g in range(8):
             start(remote(panel(g, t), rg.at[me.x, g], s1.at[k - 1, 2 + g], r1.at[k - 1, 2 + g], d), first)
@@ -335,7 +276,6 @@
         start(pltpu.make_async_copy(panel(g, me.x), rg.at[me.x, g], ls.at[2 + g]), mine)
     start(pltpu.make_async_copy(strip(me.x), rd.at[me.x], ls.at[1]), mine)
     side = []
-    start(pltpu.make_async_copy(eext, oe.at[me.zlo, me.core, me.zhi], ls.at[10]), side)
     start(pltpu.make_async_copy(idx, oi.at[me.dp, me.zhi], ls.at[11]), side)
     for n, (dz, dc) in enumerate(ZK):
         d = me.at(z=me.step("z", dz), core=lax.rem(me.core + dc, 2))
@@ -352,6 +292,37 @@
         (lax.rem(col, 16) < 12) & (lax.div(col, 16) * 12 + lax.rem(col, 16) == row), 1.0, 0.0
     ).astype(BF)
 
+    kv[:16] = jnp.zeros((16, BLK, 2 * KW), BF)
+    for h in range(2):
+        rows = slice(h * BLK, (h + 1) * BLK)
+        x[rows] = tok[:, h, :]
+        eext[rows, :D] = cot[:, h, :]
+    xf = x[...].astype(F32)
+    n1[...] = (xf * rms(xf) * gain1[...].astype(F32)).astype(BF)
+    row, col = iota((R, 128), 0), iota((R, 128), 1)
+    choose = jnp.where((lax.div(col, R) == idx_i[0]) & (lax.rem(col, R) == row), 1.0, 0.0).astype(BF)
+
+    def chosen(ref):
+        return mm(choose, ref.reshape(ADAPT * R, ref.shape[-1])).astype(BF)
+
+    for c in adapters:
+        c.wait()
+    for k in range(3):
+        a012[k] = chosen(ain[:, k])
+    a3[...] = chosen(ain[:, 3])
+    at = pl.multiple_of(me.dp * R, R)
+    a45[...] = jnp.zeros_like(a45)
+    a45[pl.ds(at, R), :] = chosen(ain[:, 4])
+    a45[pl.ds(at + 64, R), :] = chosen(ain[:, 5])
+    bqkv[...] = chosen(aqkv[...])
+    bo[...] = chosen(ares[:, 0])
+    bd[...] = jnp.zeros_like(bd)
+    bd[pl.ds(at, R), :] = chosen(ares[:, 1])
+    for k, (c0, c1) in enumerate(((0, QW), (QW, QW + KW), (QW + KW, QW + 2 * KW))):
+        u = nt(n1[...], a012[k]).astype(BF)
+        ub[:, c0:c1] = mm(u, bqkv[:, c0:c1]) + bias[c0:c1].astype(F32)
+    eext[:, D:] = nt(eext[:, :D], bd[...]).astype(BF)
+    start(pltpu.make_async_copy(eext, oe.at[me.zlo, me.core, me.zhi], ls.at[10]), side)
     from_x(0, lambda f: rq.at[f])
     cq[...] = mm(put, rq[...].reshape(64, 2048)).astype(BF)
     lo, hi = pl.ds(0, 1024), pl.ds(1024, 1024)
@@ -576,7 +547,13 @@
         base = (m if h == 0 else NBLK - 1 - m) * BLK
         kpos = base - WIN + iota((BLK, KEYS), 1)
         qpos = base + iota((BLK, KEYS), 0)
-        keep = (kpos <= qpos) & (kpos >= low[h * BLK : (h + 1) * BLK, :1])
+        pos = base + iota((BLK, 1), 0)
+        begin, end = jnp.zeros((BLK, 1), jnp.int32), 0
+        for i in range(8):
+            end = end + docs[0, i]
+            begin = jnp.where(end <= pos, end, begin)
+        low = jnp.maximum(begin, pos - span[0] + 1)
+        keep = (kpos <= qpos) & (kpos >= low)
         for a in range(KV_HEADS):
             qs = stack_heads(q, h, a)
             k = win[:, :, a * HS : (a + 1) * HS].reshape(KEYS, HS)
@@ -692,7 +669,7 @@
         c.wait()
 
 
-def front(idx, wq, wo, wg, wd, eext, n1, ub, cos, sin, low, x, gain, a45, a3, bo):
+def front(*args):
     outs = (
         sds((2, 2, 4, 2, 48, 2048), BF),
         sds((2, 2, 4, 2, 48, D), BF),
@@ -707,9 +684,24 @@
         sds((ROWS, D), BF),
         sds((ROWS, D), F32),
         sds((ROWS, DX), BF),
+        sds((ROWS, D), BF),
+        sds((ROWS, D), BF),
+        sds((ROWS, DX), BF),
+        sds((EXT, D), BF),
+        sds((EXT, D), BF),
+        sds((R, D), BF),
+        sds((R, D), BF),
+        sds((3, R, D), BF),
+        sds((R, 2048), BF),
     )
     four = (DMA((4,)),) * 4
     scratch = [
+        pltpu.VMEM((ROWS, 2048), F32),
+        pltpu.VMEM((8, 128), jnp.int32),
+        pltpu.VMEM((2, 16, FF), BF),
+        pltpu.VMEM((ADAPT, 6, R, D), BF),
+        pltpu.VMEM((ADAPT, R, 2048), BF),
+        pltpu.VMEM((ADAPT, 2, R, D), BF),
         pltpu.VMEM((4, 16, 2048), BF),
         pltpu.VMEM((4, 16, D), BF),
         pltpu.VMEM((4, 8, 16, 640), BF),
@@ -728,7 +720,7 @@
         pltpu.VMEM((5, 256, 400), BF),
         DMA((11, 4)),
         DMA((11, 4)),
-        DMA((21,)),
+        DMA((24,)),
         DMA((3, 11)),
         DMA((3, 11)),
         DMA((7,)),
@@ -747,11 +739,11 @@
     return pl.pallas_call(
         front_kernel,
         out_shape=outs,
-        in_specs=[ANY, VM, VM, ANY, VM, ANY] + [VM] * 10,
-        out_specs=[ANY] * 9 + [VM] * 4,
+        in_specs=[SM] * 3 + [VM] * 6 + [ANY] * 3 + [VM] * 5,
+        out_specs=[ANY] * 9 + [VM] * 13,
         scratch_shapes=scratch,
         compiler_params=pltpu.CompilerParams(collective_id=1, has_side_effects=True, vmem_limit_bytes=VMEM_LIMIT),
-    )(idx, wq, wo, wg, wd, eext, n1, ub, cos, sin, low, x, gain, a45, a3, bo)
+    )(*args)
 
 
 class Fan:
@@ -863,9 +855,8 @@
     wgu[D : D + 64, FW:] = none
     wgu[D + 64 :, FW:] = mm(choose, b_in[:, 1].reshape(128, FW)).astype(BF)
     acc[...] = jnp.zeros_like(acc)
-    for c in wloads[2:]:
+    for c in wloads[2:6]:
         c.wait()
-    pl.semaphore_wait(bar, N_CTX - 1 + len(others))
     sib_copies, z_copies = [], []
 
     def z_push(j, k, slot, z):
@@ -880,6 +871,8 @@
         ev = xb[n % 2, 1].reshape(2 * ROWS, DX)
         both = mm(xv, wgu[...])
         gate, up = both[:, :FW], both[:, FW:]
+        if n == 0:
+            wloads[6].wait()
         gm = nt(ev, wdo[:FW])
         sig = 1.0 / (1.0 + jnp.exp(-gate))
         sl = gate * sig
@@ -893,6 +886,8 @@
         acc[2] += by_u[64:, FW:]
         if n < 2:
             coming.append(rows_in(n + 2))
+        if n == 0:
+            pl.semaphore_wait(bar, N_CTX - 1 + len(others))
         for k in (1, 0):
             wide = nt(grads, wgu[...]) if k == 1 else mm(act, wdo[:FW])
             total = gn2 if k == 1 else ysum
@@ -1008,14 +1003,15 @@
     def covers(t, w, owner, h):
         block = owner if h == 0 else NBLK - 1 - owner
         j = block - ((t if w == 0 else NBLK - 1 - t) - (NWB - 1))
-        return j, (j >= 0) & (j < NWB)
+        ok = (j >= 0) & (j < NWB)
+        return j, ok if w == 0 else ok & (block > t)
 
     def kv_copy(w, h, t, j):
         return remote(gwin.at[w, j], got.at[h, w, j], kv_s.at[h, w, t], kv_r.at[h, w, j], (me.dp, t))
 
     for c in loads[4:7]:
         c.wait()
-    for w in range(2):
+    for w in (1, 0):
         for a in range(KV_HEADS):
             qs, gv, ov = stack_heads(q, w, a), stack_heads(go, w, a), stack_heads(o, w, a)
             k = win[w, :, :, a * HS : (a + 1) * HS].reshape(KEYS, HS)
@@ -1030,6 +1026,18 @@
             gwin[w, :, :, a * HS : (a + 1) * HS] = (tn(ds, qs) * SCALE).astype(BF).reshape(NWB, BLK, HS)
             gwin[w, :, :, KW + a * HS : KW + (a + 1) * HS] = tn(pr, gv).astype(BF).reshape(NWB, BLK, HS)
 
+        if w == 0:
+            def both_windows(j, carry):
+                j1 = j + 2 * m - (NBLK - 1)
+
+                @pl.when(j1 >= 0)
+                def _():
+                    gwin[0, j] = (gwin[0, j].astype(F32) + gwin[1, j1].astype(F32)).astype(BF)
+
+                return carry
+
+            lax.fori_loop(0, NWB, both_windows, 0)
+
         def kv_send(k, carry):
             t = lax.rem(m + k, N_CTX)
             for h in range(2):
@@ -1102,16 +1110,6 @@
         return carry
 
     lax.fori_loop(0, N_CTX, take, 0)
-    rz.second()
-    rz.last()
-    own_e.wait()
-    ra = Ring(me, "x", x0(me.x, None), x0, ring_s.at[1], ring_r.at[1])
-    rb = Ring(me, "y", y1(me.y, None), y1, ring_s.at[2], ring_r.at[2])
-    ra.first()
-    rb.first()
-
-    ra.second()
-    rb.second()
 
     for c in loads[7:] + [wq_load]:
         c.wait()
@@ -1140,86 +1138,112 @@
         out_o[:, h, :] = y[h * BLK : (h + 1) * BLK].astype(BF)
     put(l2, 52, mm(pick_own, tn(ud, e[:, :D]).astype(BF)))
     l_send(l2, gl2, b_s, b_r)
+    rz.second()
+    rz.last()
+    own_e.wait()
+    ra = Ring(me, "x", x0(me.x, None), x0, ring_s.at[1], ring_r.at[1])
+    rb = Ring(me, "y", y1(me.y, None), y1, ring_s.at[2], ring_r.at[2])
+    ra.first()
+    rb.first()
+
+    gn = nt(gj[...], wgu[:D, :2048]) + more
+    gt = gh[...] + norm_back(x[...].astype(F32), gain1[...].astype(F32), gn)
+    for h in range(2):
+        gt_o[:, h, :] = gt[h * BLK : (h + 1) * BLK].astype(BF)
+
+    ra.second()
+    rb.second()
+    red2[...] = l_sum(gl2, b_s, b_r)
+
+    def uz(j):
+        return late.at[me.y, me.x, lax.rem(j, 2), me.core, lax.div(j, 2)]
+
+    own_l = pltpu.make_async_copy(red2, uz(me.z), ls.at[6])
+    own_l.start()
+    own_l.wait()
+    def f_sent(k, carry):
+        f_copy(lax.rem(xy + k, 16)).wait_send()
+        return carry
+
+    def kv_sent(k, carry):
+        t = lax.rem(m + k, N_CTX)
+        for w in range(2):
+            for h in range(2):
+                j, ok = covers(m, w, t, h)
+
+                @pl.when(ok)
+                def _():
+                    kv_copy(w, h, t, j).wait_send()
+
+        return carry
+
+    fz = Fan(me, "z", uz, fan_s.at[0], fan_r.at[0])
+    fz.first()
     ra.last()
     rb.last()
     rc = Ring(me, "y", y0(me.y, None), y0, ring_s.at[3], ring_r.at[3])
     rd = Ring(me, "x", x1(me.x, None), x1, ring_s.at[4], ring_r.at[4])
     rc.first()
     rd.first()
-    gn = nt(gj[...], wgu[:D, :2048]) + more
-    gt = gh[...] + norm_back(x[...].astype(F32), gain1[...].astype(F32), gn)
-    for h in range(2):
-        gt_o[:, h, :] = gt[h * BLK : (h + 1) * BLK].astype(BF)
-
-    red2[...] = l_sum(gl2, b_s, b_r)
-
-    def uz(j):
-        return late.at[me.y, me.x, lax.rem(j, 2), me.core, lax.div(j, 2)]
-
-    own_l = pltpu.make_async_copy(red2, uz(me.z), ls.at[6])
-    own_l.start()
-    own_l.wait()
-    fz = Fan(me, "z", uz, fan_s.at[0], fan_r.at[0])
-    fz.first()
+    swaps = []
+
+    def swap(view, j):
+        n = len(swaps)
+        c = remote(view(j, me.core), view(j, me.core), core_s.at[n], core_r.at[n], sib)
+        c.start()
+        swaps.append((c, view, j))
+
+    def ey(j, core):
+        return early.at[j, :, :, core, :, ta]
+
+    def ex(j, core):
+        return early.at[:, j, :, core, :, tb]
+
+    def late_all(j, core):
+        return late.at[j, :, :, core]
+
+    swap(ey, me.y)
+    swap(ex, me.x)
+    l_sent(l1, gl1, a_s, a_r)
+    lax.fori_loop(1, 16, f_sent, 0)
+    fz.last()
+    t0, t1 = pl.ds(0, 1), pl.ds(1, 1)
+    fx = Fan(me, "x", lambda j: late.at[me.y, j, :, me.core, :, t0], fan_s.at[1], fan_r.at[1])
+    fy = Fan(me, "y", lambda j: late.at[j, me.x, :, me.core, :, t1], fan_s.at[2], fan_r.at[2])
+    fx.first()
+    fy.first()
+    lax.fori_loop(1, N_CTX, kv_sent, 0)
     rc.second()
     rd.second()
-    fz.last()
-
-    def ux(j):
-        return late.at[me.y, j, :, me.core]
-
-    def uy(j):
-        return late.at[j, :, :, me.core]
-
-    fx = Fan(me, "x", ux, fan_s.at[1], fan_r.at[1])
-    fx.first()
+    swap(ey, rc.l)
+    swap(ex, rd.l)
+    swap(ey, rc.r)
+    swap(ex, rd.r)
+    fx.last()
+    fy.last()
+    fy2 = Fan(me, "y", lambda j: late.at[j, :, :, me.core, :, t0], fan_s.at[3], fan_r.at[3])
+    fx2 = Fan(me, "x", lambda j: late.at[:, j, :, me.core, :, t1], fan_s.at[4], fan_r.at[4])
+    fy2.first()
+    fx2.first()
+    l_sent(l2, gl2, b_s, b_r)
     rc.last()
     rd.last()
-    swaps = []
-
-    def swap(view, n):
-        c = remote(view(me.core), view(me.core), core_s.at[n], core_r.at[n], sib)
-        c.start()
-        swaps.append((c, view, n))
-
+    swap(ey, rc.o)
+    swap(ex, rd.o)
+    fy2.last()
+    fx2.last()
     for k in range(4):
-        swap(lambda core, k=k: early.at[k, :, :, core], k)
-    fx.last()
-    fy = Fan(me, "y", uy, fan_s.at[2], fan_r.at[2])
-    fy.first()
-    fy.last()
-    for k in range(4):
-        swap(lambda core, k=k: late.at[k, :, :, core], 4 + k)
+        swap(late_all, k)
 
     for c in sib_copies + z_copies:
         c.wait_send()
-    for r in (rz, ra, rb, rc, rd, fz, fx, fy):
+    for r in (rz, ra, rb, rc, rd, fz, fx, fy, fx2, fy2):
         r.sent()
 
-    def f_sent(k, carry):
-        f_copy(lax.rem(xy + k, 16)).wait_send()
-        return carry
-
-    lax.fori_loop(1, 16, f_sent, 0)
-    l_sent(l1, gl1, a_s, a_r)
-    l_sent(l2, gl2, b_s, b_r)
-
-    def kv_sent(k, carry):
-        t = lax.rem(m + k, N_CTX)
-        for w in range(2):
-            for h in range(2):
-                j, ok = covers(m, w, t, h)
-
-                @pl.when(ok)
-                def _():
-                    kv_copy(w, h, t, j).wait_send()
-
-        return carry
-
-    lax.fori_loop(1, N_CTX, kv_sent, 0)
-    for c, view, n in swaps:
+
+    for n, (c, view, j) in enumerate(swaps):
         c.wait_send()
-        ref = view(1 - me.core)
+        ref = view(j, 1 - me.core)
         remote(ref, ref, core_s.at[n], core_r.at[n], sib).wait_recv()
 
 
@@ -1281,10 +1305,10 @@
         DMA((7,)),
         DMA((5, 4)),
         DMA((5, 4)),
-        DMA((3, 3)),
-        DMA((3, 3)),
-        DMA((8,)),
-        DMA((8,)),
+        DMA((5, 3)),
+        DMA((5, 3)),
+        DMA((12,)),
+        DMA((12,)),
     ]
     return pl.pallas_call(
         rear_kernel,
@@ -1382,24 +1406,18 @@
     member = lax.axis_index("ctx")
     starts = jnp.stack([member * BLK, (NBLK - 1 - member) * BLK])
     pos = (starts[:, None] + jnp.arange(BLK, dtype=jnp.int32)[None]).reshape(ROWS)
-    ends = jnp.cumsum(doc_lengths[0])
-    begin = jnp.max(jnp.where(ends[None] <= pos[:, None], ends[None], 0), -1)
-    low = jnp.maximum(begin, pos - window[0] + 1)
-    low = jnp.broadcast_to(low[:, None], (ROWS, 128)).astype(jnp.int32)
     freq = 1000000.0 ** (-(2.0 * jnp.arange(HS // 2, dtype=F32)) / HS)
     ang = pos.astype(F32)[:, None] * freq[None]
     c, sn = jnp.cos(ang), jnp.sin(ang)
     cos = jnp.concatenate([c, c], -1)
     sin = jnp.concatenate([-sn, sn], -1)
 
-    wg = jnp.pad(jnp.transpose(w_gu, (1, 0, 2)), ((0, 0), (0, 4), (0, 0)))
-    idx_row = jnp.broadcast_to(adapter_index[:, None], (8, 128)).astype(jnp.int32)
-
-    x, n1, eext, ub, a45, bd, a3, bo, a012, bqkv = prepare(
-        adapter_index, tokens[0], cotangent[0], adapt_in, adapt_out_qkv, adapt_out_res, gain_attn, b_qkv
-    )
-    oq, oo, og, down, oe, oi, wins, p, xg, q, o, hid, n2 = front(
-        idx_row, w_qkv, w_out, wg, w_down, eext, n1, ub, cos, sin, low, x, gain_mlp, a45, a3, bo
+    (
+        oq, oo, og, down, oe, oi, wins, p, xg, q, o, hid, n2,
+        x, n1, eext, a45, bd, a3, bo, a012, bqkv,
+    ) = front(
+        adapter_index, doc_lengths, window, w_qkv, w_out, w_gu, w_down, tokens[0], cotangent[0],
+        adapt_in, adapt_out_qkv, adapt_out_res, gain_attn, b_qkv, cos, sin, gain_mlp,
     )
     oq = oq.reshape(D, 2048)
     oo = oo.reshape(D, D)

time: 325 us -> 310 us (0.954)
  Pallas kernels: 312 us -> 300 us
    pallas_call x1, Pallas kernels: 151 us -> 144 us  [rear(): pl.pallas_call(rear_kernel, out_shape=outs, in_specs=[ANY] * 17 + [VM] *...]
    pallas_call x2 -> x1, Pallas kernels: 150 us -> 145 us  [front(): pl.pallas_call(front_kernel, out_shape=outs, in_specs=[SM] * 3 + [VM] * 6...]
where the time goes in v4:
time: 310 us; the launch traced here: 305 us
  Pallas kernels  300 us (97%)
    pallas_call x1, Pallas kernels, front(): pl.pallas_call(front_kernel, out_shape=outs, in_specs=[SM] * 3 + [VM] * 6...  145 us
    pallas_call x1, Pallas kernels, rear(): pl.pallas_call(rear_kernel, out_shape=outs, in_specs=[ANY] * 17 + [VM] *...  144 us
    pallas_call x1, Pallas kernels, spread(): pl.pallas_call(spread_kernel, out_shape=outs, grid=(ADAPT,), in_specs=[SM...  11.1 us

profile of v4, /device:TPU:1, one launch (start us, length us, event | category | flops | bytes accessed | tf_op | source)
XLA Modules:
  0.0 304.8 jit_solution(17467234998048188712)
XLA Ops:
  1.9 0.1 pad_add_fusion
  2.0 0.1 add_convert_fusion
  2.1 0.1 convert_element_type.11
  2.2 0.3 fusion
  2.5 0.8 pad_maximum_fusion
  3.3 145.2 %shard_map.216 = (bf16[2,2,4,2,48,2048]{5,4,3,2,1,0:T(8,128)(2,1)}, bf16[2,2,4,2,48,1536]{5,4,3,2,1,0:T(8,128)(2,1)}, bf16[4,2,2,4,2,48,640]{6,5,4,3,2,1,0:T(8,1...) custom-call(s32[1]{0:T(128)S(6)} %copy.26.idx_i, ...), custom_call_target="tpu_custom_call" | custom-call | tf_op jit(solution)/shard_map/pallas_call | solution.py:739
  148.5 143.5 %shard_map.217 = (bf16[64,2,1536]{2,1,0:T(2,128)(2,1)}, bf16[64,2,1536]{2,1,0:T(2,128)(2,1)}, bf16[4,4,2,2,2,10,16,128]{7,6,5,4,3,2,1,0:T(8,128)(2,1)}, bf16[4,4,2,2,2,2,16,128]{7,6,5,4,3,2,1,0:T(8,128)(2,1)}) custom-call(bf16[2,2,2,128,1664]{4,3,2,1,0:T(8,128)(2,1)} %get-tuple-element.38.xg, bf16[2,2,2,128,1664]{4,3,2,1,0:T(8,128)(2,1)} %get-tuple-element.39.oe, ...), custom_call_target="tpu_custom_call" | custom-call | tf_op jit(solution)/shard_map/pallas_call | solution.py:1313
  292.0 0.0 copy-start.1
  292.0 0.0 copy-start
  292.1 11.1 %shard_map.218 = (f32[8,6,16,1536]{3,2,1,0:T(8,128)}, f32[8,16,8960]{2,1,0:T(8,128)}, f32[8,16,2048]{2,1,0:T(8,128)}, f32[8,2,16,1536]{3,2,1,0:T(8,128)}, f32[8,2,16,8960]{3,2,1,0:T(8,128)}) custom-call(s32[4,2,8,128]{3,2,1,0:T(8,128)} %get-tuple-element.53.oi, bf16[4,4,2,2,2,10,16,128]{7,6,5,4,3,2,1,0:T(8,128)(2,1)} %get-tuple-element.62.early, ...), custom_call_target="tpu_custom_call" | custom-call | tf_op jit(solution)/shard_map/pallas_call | solution.py:1373
  303.1 0.0 copy-done.1
  303.1 0.7 copy.28
  303.9 0.0 copy-done
  303.9 0.7 copy.29
  (1 shorter events, 0.0 us)
Async XLA Ops:
  292.0 11.1 %copy-start.1 = (bf16[64,2,1536]{2,1,0:T(2,128)(2,1)S(1)}, bf16[64,2,1536]{2,1,0:T(2,128)(2,1)}, u32[]{:S(2)}) copy-start(bf16[64,2,1536]{2,1,0:T(2,128)(2,1)} %get-tuple-element.60) | copy-start | bytes 1179652
  292.0 11.8 %copy-start = (bf16[64,2,1536]{2,1,0:T(2,128)(2,1)S(1)}, bf16[64,2,1536]{2,1,0:T(2,128)(2,1)}, u32[]{:S(2)}) copy-start(bf16[64,2,1536]{2,1,0:T(2,128)(2,1)} %get-tuple-element.61) | copy-start | bytes 1179652

commit v5 on v4

--- a/solution.py
+++ b/solution.py
@@ -209,8 +209,9 @@
 
 def front_kernel(
     idx_i, docs, span, wq_i, wo_i, wg_i, wd_i, tok, cot, ain_i, aqkv_i, ares_i, gain1, bias, cos, sin, gain,
-    oq_o, oo_o, og, od_o, oe, oi, win_o, p_o, xg, q, o_o, hid_o, n2,
-    x, n1, eext, a45, bd, a3, bo, a012, bqkv,
+    oq_o, oo_o, og, od_o, oe, oi, win_o, p_o, xg, q_h, o_h, hid_h, n2_h,
+    x_h, n1_h, e_h, a45_h, bd_h, a3_h, bo_h, a012_h, bqkv_h,
+    q, o_o, hid_o, n2, x, n1, eext, a45, bd, a3, bo, a012, bqkv, keep_s,
     ub, idx, wg, ain, aqkv, ares, rq, ro, rg, wdp, rd, cq, co, cg, oq, oo, od, kv_own, kv, p, down, pick70,
     ss, rs, ls, s1, r1, s2, r2, sc, rc, sd, rdn, sk, rk, ez_sems, si, ri, nz_sems,
 ):
@@ -262,8 +263,6 @@
     xs = [(k, me.step("x", k), me.at(x=me.step("x", k))) for k in (1, 3, 2)]
     for k, t, d in xs:
         start(remote(rq.at[me.x], rq.at[me.x], s1.at[k - 1, 0], r1.at[k - 1, 0], d), first)
-    for k, t, d in xs:
-        start(remote(ro.at[me.x], ro.at[me.x], s1.at[k - 1, 1], r1.at[k - 1, 1], d), first)
     for k in range(2):
         wg[k, :12] = wg_i[:, k, :]
         wg[k, 12:] = jnp.zeros((4, FF), BF)
@@ -271,6 +270,8 @@
         for g in range(8):
             start(remote(panel(g, t), rg.at[me.x, g], s1.at[k - 1, 2 + g], r1.at[k - 1, 2 + g], d), first)
         start(remote(strip(t), rd.at[me.x], s1.at[k - 1, 10], r1.at[k - 1, 10], d), first)
+    for k, t, d in xs:
+        start(remote(ro.at[me.x], ro.at[me.x], s1.at[k - 1, 1], r1.at[k - 1, 1], d), first)
     mine = []
     for g in range(8):
         start(pltpu.make_async_copy(panel(g, me.x), rg.at[me.x, g], ls.at[2 + g]), mine)
@@ -323,6 +324,15 @@
         ub[:, c0:c1] = mm(u, bqkv[:, c0:c1]) + bias[c0:c1].astype(F32)
     eext[:, D:] = nt(eext[:, :D], bd[...]).astype(BF)
     start(pltpu.make_async_copy(eext, oe.at[me.zlo, me.core, me.zhi], ls.at[10]), side)
+    kept = []
+
+    def keep_all(*pairs):
+        for ref, place in pairs:
+            start(pltpu.make_async_copy(ref, place, keep_s.at[len(kept)]), kept)
+
+    keep_all(
+        (x, x_h), (n1, n1_h), (eext, e_h), (a45, a45_h), (bd, bd_h), (a3, a3_h), (bo, bo_h), (a012, a012_h), (bqkv, bqkv_h)
+    )
     from_x(0, lambda f: rq.at[f])
     cq[...] = mm(put, rq[...].reshape(64, 2048)).astype(BF)
     lo, hi = pl.ds(0, 1024), pl.ds(1024, 1024)
@@ -346,8 +356,6 @@
     qa.first()
     qb.first()
     oq[me.zlo, me.core, me.y, me.zhi] = cq[...]
-    from_x(1, lambda f: ro.at[f])
-    co[...] = mm(put, ro[...].reshape(64, D)).astype(BF)
     qa.second()
     qb.second()
     for n in range(8):
@@ -402,6 +410,8 @@
 
     swap(qz0, me.z)
     swap(qy1, me.y)
+    from_x(1, lambda f: ro.at[f])
+    co[...] = mm(put, ro[...].reshape(64, D)).astype(BF)
     own_g.wait()
     for n, (dz, dc) in enumerate(ZK):
         z, core = me.step("z", 4 - dz if dz else 0), lax.rem(me.core + dc, 2)
@@ -444,6 +454,12 @@
     ga.second()
     gb.second()
     wa.first()
+    ga.last()
+    gb.last()
+    ga2 = Ring(me, "x", g0b(me.x, None), g0b, ss.at[6], rs.at[6])
+    gb2 = Ring(me, "y", g1b(me.y, None), g1b, ss.at[7], rs.at[7])
+
+    ga2.first()
     qa2.last()
     qb2.last()
     swap(qz0, qa2.o)
@@ -462,12 +478,6 @@
         for k, t in ys:
             remote(od.at[me.x, rows8], od.at[me.x, rows8], sd.at[k], rdn.at[k], me.at(y=t)).start()
 
-    ga.last()
-    gb.last()
-    ga2 = Ring(me, "x", g0b(me.x, None), g0b, ss.at[6], rs.at[6])
-    gb2 = Ring(me, "y", g1b(me.y, None), g1b, ss.at[7], rs.at[7])
-
-    ga2.first()
     for n in range(8):
         swapped(n)
     keep_q = pltpu.make_async_copy(oq, oq_o, ls.at[12])
@@ -582,10 +592,10 @@
             wb.second()
             swap(oz, wb.l)
             swap(oz, wb.r)
-            ez.second()
             ga2.second()
 
     start(pltpu.make_async_copy(p, p_o, ls.at[18]), keep_p)
+    ez.second()
     wb.last()
     swap(oz, wb.o)
     for n in range(8, 12):
@@ -602,6 +612,7 @@
     n2[:, D:] = nt(nv, a45[...]).astype(BF)
     nz = ZGather(me, n2, xg, *nz_sems, BLK)
     nz.first()
+    keep_all((q, q_h), (o_o, o_h), (hid_o, hid_h), (n2, n2_h))
     start(pltpu.make_async_copy(n2, xg.at[me.zlo, me.core, me.zhi], ls.at[19]), side)
     gb2.second()
     nz.second()
@@ -665,7 +676,7 @@
         remote(ref, ref, si.at[n], ri.at[n], me.at(z=z, core=core)).wait_recv()
     ez.finish()
     nz.finish()
-    for c in side + wins + keep_p + [keep_q, keep_o, keep_d]:
+    for c in side + wins + keep_p + kept + [keep_q, keep_o, keep_d]:
         c.wait()
 
 
@@ -695,7 +706,8 @@
         sds((R, 2048), BF),
     )
     four = (DMA((4,)),) * 4
-    scratch = [
+    scratch = [pltpu.VMEM(v.shape, v.dtype) for v in outs[9:]] + [
+        DMA((13,)),
         pltpu.VMEM((ROWS, 2048), F32),
         pltpu.VMEM((8, 128), jnp.int32),
         pltpu.VMEM((2, 16, FF), BF),
@@ -740,7 +752,7 @@
         front_kernel,
         out_shape=outs,
         in_specs=[SM] * 3 + [VM] * 6 + [ANY] * 3 + [VM] * 5,
-        out_specs=[ANY] * 9 + [VM] * 13,
+        out_specs=[ANY] * 22,
         scratch_shapes=scratch,
         compiler_params=pltpu.CompilerParams(collective_id=1, has_side_effects=True, vmem_limit_bytes=VMEM_LIMIT),
     )(*args)
@@ -780,8 +792,9 @@
 
 def rear_kernel(
     xg, oe, og, wd_i, ad_all, b_all, e_i, hid_i, n2_i, q_i, o_i, p_i, win_i, wo_i, wq_i, x_i, n1_i,
-    oi, a012, a3, a45, bqkv, bo, bd, gain1, gain2, cos, sin,
-    out_o, gt_o, early, late,
+    a012_i, a3_i, a45_i, bqkv_i, bo_i, bd_i, cos_i, sin_i, oi, gain1, gain2,
+    out_h, gt_h, early, late,
+    a012, a3, a45, bqkv, bo, bd, cos, sin, out_o, gt_o, ld2,
     wgu, wdo, ad_in, b_in, ad, acc, xb, sib_out, sib_got, red, got2, ft,
     e, hid, n2, q, o, p, win, x, n1,
     gn2, ysum, gh, go, gq, gwin, got, gkv, gj, l1, l2, gf, gl1, gl2, red1, red2,
@@ -832,6 +845,14 @@
             (
                 (e_i, e), (hid_i, hid), (n2_i, n2), (o_i, o), (q_i, q),
                 (win_i, win), (p_i, p), (n1_i, n1), (x_i, x),
+            )
+        )
+    ]
+    small = [
+        load(src, dst, ld2.at[n])
+        for n, (src, dst) in enumerate(
+            (
+                (a45_i, a45), (bo_i, bo), (a3_i, a3), (a012_i, a012), (bqkv_i, bqkv), (bd_i, bd), (cos_i, cos), (sin_i, sin),
             )
         )
     ]
@@ -944,7 +965,7 @@
             total[...] += ref[...].astype(F32)
 
     z_take(1, gn2)
-    for c in loads[:4] + [wo_load]:
+    for c in loads[:4] + small + [wo_load]:
         c.wait()
 
     def put(tiles, at, v):
@@ -1109,7 +1130,16 @@
 
         return carry
 
-    lax.fori_loop(0, N_CTX, take, 0)
+    lax.fori_loop(0, 20, take, 0)
+    rz.second()
+    rz.last()
+    own_e.wait()
+    ra = Ring(me, "x", x0(me.x, None), x0, ring_s.at[1], ring_r.at[1])
+    rb = Ring(me, "y", y1(me.y, None), y1, ring_s.at[2], ring_r.at[2])
+    ra.first()
+    rb.first()
+
+    lax.fori_loop(20, N_CTX, take, 0)
 
     for c in loads[7:] + [wq_load]:
         c.wait()
@@ -1136,20 +1166,14 @@
     y = hid[...] + ysum[:, :D] + mm(ud, bd[...])
     for h in range(2):
         out_o[:, h, :] = y[h * BLK : (h + 1) * BLK].astype(BF)
+    out_load = load(out_o, out_h, ld2.at[8])
     put(l2, 52, mm(pick_own, tn(ud, e[:, :D]).astype(BF)))
     l_send(l2, gl2, b_s, b_r)
-    rz.second()
-    rz.last()
-    own_e.wait()
-    ra = Ring(me, "x", x0(me.x, None), x0, ring_s.at[1], ring_r.at[1])
-    rb = Ring(me, "y", y1(me.y, None), y1, ring_s.at[2], ring_r.at[2])
-    ra.first()
-    rb.first()
-
     gn = nt(gj[...], wgu[:D, :2048]) + more
     gt = gh[...] + norm_back(x[...].astype(F32), gain1[...].astype(F32), gn)
     for h in range(2):
         gt_o[:, h, :] = gt[h * BLK : (h + 1) * BLK].astype(BF)
+    gt_load = load(gt_o, gt_h, ld2.at[9])
 
     ra.second()
     rb.second()
@@ -1181,29 +1205,6 @@
     fz.first()
     ra.last()
     rb.last()
-    rc = Ring(me, "y", y0(me.y, None), y0, ring_s.at[3], ring_r.at[3])
-    rd = Ring(me, "x", x1(me.x, None), x1, ring_s.at[4], ring_r.at[4])
-    rc.first()
-    rd.first()
-    swaps = []
-
-    def swap(view, j):
-        n = len(swaps)
-        c = remote(view(j, me.core), view(j, me.core), core_s.at[n], core_r.at[n], sib)
-        c.start()
-        swaps.append((c, view, j))
-
-    def ey(j, core):
-        return early.at[j, :, :, core, :, ta]
-
-    def ex(j, core):
-        return early.at[:, j, :, core, :, tb]
-
-    def late_all(j, core):
-        return late.at[j, :, :, core]
-
-    swap(ey, me.y)
-    swap(ex, me.x)
     l_sent(l1, gl1, a_s, a_r)
     lax.fori_loop(1, 16, f_sent, 0)
     fz.last()
@@ -1212,19 +1213,42 @@
     fy = Fan(me, "y", lambda j: late.at[j, me.x, :, me.core, :, t1], fan_s.at[2], fan_r.at[2])
     fx.first()
     fy.first()
+    rc = Ring(me, "y", y0(me.y, None), y0, ring_s.at[3], ring_r.at[3])
+    rd = Ring(me, "x", x1(me.x, None), x1, ring_s.at[4], ring_r.at[4])
+    rc.first()
+    rd.first()
+    swaps = []
+
+    def swap(view, j):
+        n = len(swaps)
+        c = remote(view(j, me.core), view(j, me.core), core_s.at[n], core_r.at[n], sib)
+        c.start()
+        swaps.append((c, view, j))
+
+    def ey(j, core):
+        return early.at[j, :, :, core, :, ta]
+
+    def ex(j, core):
+        return early.at[:, j, :, core, :, tb]
+
+    def late_all(j, core):
+        return late.at[j, :, :, core]
+
+    swap(ey, me.y)
+    swap(ex, me.x)
     lax.fori_loop(1, N_CTX, kv_sent, 0)
+    fx.last()
+    fy.last()
+    fy2 = Fan(me, "y", lambda j: late.at[j, :, :, me.core, :, t0], fan_s.at[3], fan_r.at[3])
+    fx2 = Fan(me, "x", lambda j: late.at[:, j, :, me.core, :, t1], fan_s.at[4], fan_r.at[4])
+    fy2.first()
+    fx2.first()
     rc.second()
     rd.second()
     swap(ey, rc.l)
     swap(ex, rd.l)
     swap(ey, rc.r)
     swap(ex, rd.r)
-    fx.last()
-    fy.last()
-    fy2 = Fan(me, "y", lambda j: late.at[j, :, :, me.core, :, t0], fan_s.at[3], fan_r.at[3])
-    fx2 = Fan(me, "x", lambda j: late.at[:, j, :, me.core, :, t1], fan_s.at[4], fan_r.at[4])
-    fy2.first()
-    fx2.first()
     l_sent(l2, gl2, b_s, b_r)
     rc.last()
     rd.last()
@@ -1237,6 +1261,8 @@
 
     for c in sib_copies + z_copies:
         c.wait_send()
+    out_load.wait()
+    gt_load.wait()
     for r in (rz, ra, rb, rc, rd, fz, fx, fy, fx2, fy2):
         r.sent()
 
@@ -1255,7 +1281,10 @@
         sds((4, 4, 2, 2, 2, 2, R, 128), BF),
     )
     block = (ROWS, DX)
-    scratch = [
+    scratch = [pltpu.VMEM(v.shape, v.dtype) for v in small[:8]] + [
+        pltpu.VMEM((BLK, 2, D), BF),
+        pltpu.VMEM((BLK, 2, D), BF),
+        DMA((10,)),
         pltpu.VMEM((DX, 2 * FW), BF),
         pltpu.VMEM((D, DX), BF),
         pltpu.VMEM((ADAPT, R, FW), BF),
@@ -1313,8 +1342,8 @@
     return pl.pallas_call(
         rear_kernel,
         out_shape=outs,
-        in_specs=[ANY] * 17 + [VM] * len(small),
-        out_specs=[VM, VM, ANY, ANY],
+        in_specs=[ANY] * 25 + [VM] * 3,
+        out_specs=[ANY] * 4,
         scratch_shapes=scratch,
         compiler_params=pltpu.CompilerParams(collective_id=2, has_side_effects=True, vmem_limit_bytes=VMEM_LIMIT),
     )(xg, oe, og, wd, ad_all, b_all, e, hid, n2, q, o, p, win, wo, wq, x, n1, *small)
@@ -1424,7 +1453,7 @@
     og = og.reshape(4, D, 640)
     out, gt, early, late = rear(
         xg, oe, og, down, adapt_in_ff, adapt_out_ff, eext, hid, n2, q, o, p, wins, oo, oq, x, n1,
-        oi, a012, a3, a45, bqkv, bo, bd, gain_attn, gain_mlp, cos, sin,
+        a012, a3, a45, bqkv, bo, bd, cos, sin, oi, gain_attn, gain_mlp,
     )
     return (out[None], gt[None]) + tuple(spread(oi, early, late))
 

time: 310 us -> 305 us (0.984)
  Pallas kernels: 300 us -> 295 us
where the time goes in v5:
time: 305 us; the launch traced here: 300 us
  Pallas kernels  295 us (97%)
    pallas_call x1, Pallas kernels, front(): pl.pallas_call(front_kernel, out_shape=outs, in_specs=[SM] * 3 + [VM] * 6...  143 us
    pallas_call x1, Pallas kernels, rear(): pl.pallas_call(rear_kernel, out_shape=outs, in_specs=[ANY] * 25 + [VM] *...  141 us
    pallas_call x1, Pallas kernels, spread(): pl.pallas_call(spread_kernel, out_shape=outs, grid=(ADAPT,), in_specs=[SM...  11.3 us

profile of v5, /device:TPU:1, one launch (start us, length us, event | category | flops | bytes accessed | tf_op | source)
XLA Modules:
  0.0 300.4 jit_solution(10585220995854080219)
XLA Ops:
  1.9 0.1 pad_add_fusion
  2.0 0.1 add_convert_fusion
  2.1 0.1 convert_element_type.11
  2.2 0.3 fusion
  2.5 0.8 pad_maximum_fusion
  3.3 142.8 %shard_map.216 = (bf16[2,2,4,2,48,2048]{5,4,3,2,1,0:T(8,128)(2,1)}, bf16[2,2,4,2,48,1536]{5,4,3,2,1,0:T(8,128)(2,1)}, bf16[4,2,2,4,2,48,640]{6,5,4,3,2,1,0:T(8,1...) custom-call(s32[1]{0:T(128)S(6)} %copy.26.idx_i, ...), custom_call_target="tpu_custom_call" | custom-call | tf_op jit(solution)/shard_map/pallas_call | solution.py:751
  146.1 141.3 %shard_map.217 = (bf16[64,2,1536]{2,1,0:T(2,128)(2,1)}, bf16[64,2,1536]{2,1,0:T(2,128)(2,1)}, bf16[4,4,2,2,2,10,16,128]{7,6,5,4,3,2,1,0:T(8,128)(2,1)}, bf16[4,4,2,2,2,2,16,128]{7,6,5,4,3,2,1,0:T(8,128)(2,1)}) custom-call(bf16[2,2,2,128,1664]{4,3,2,1,0:T(8,128)(2,1)} %get-tuple-element.38.xg, bf16[2,2,2,128,1664]{4,3,2,1,0:T(8,128)(2,1)} %get-tuple-element.39.oe, ...), custom_call_target="tpu_custom_call" | custom-call | tf_op jit(solution)/shard_map/pallas_call | solution.py:1342
  287.3 0.0 copy-start.1
  287.3 0.0 copy-start
  287.4 11.3 %shard_map.218 = (f32[8,6,16,1536]{3,2,1,0:T(8,128)}, f32[8,16,8960]{2,1,0:T(8,128)}, f32[8,16,2048]{2,1,0:T(8,128)}, f32[8,2,16,1536]{3,2,1,0:T(8,128)}, f32[8,2,16,8960]{3,2,1,0:T(8,128)}) custom-call(s32[4,2,8,128]{3,2,1,0:T(8,128)} %get-tuple-element.59.oi, bf16[4,4,2,2,2,10,16,128]{7,6,5,4,3,2,1,0:T(8,128)(2,1)} %get-tuple-element.62.early, ...), custom_call_target="tpu_custom_call" | custom-call | tf_op jit(solution)/shard_map/pallas_call | solution.py:1402
  298.7 0.0 copy-done.1
  298.7 0.7 copy.28
  299.4 0.0 copy-done
  299.4 0.7 copy.29
  (1 shorter events, 0.0 us)
Async XLA Ops:
  287.3 11.4 %copy-start.1 = (bf16[64,2,1536]{2,1,0:T(2,128)(2,1)S(1)}, bf16[64,2,1536]{2,1,0:T(2,128)(2,1)}, u32[]{:S(2)}) copy-start(bf16[64,2,1536]{2,1,0:T(2,128)(2,1)} %get-tuple-element.60) | copy-start | bytes 1179652
  287.3 12.1 %copy-start = (bf16[64,2,1536]{2,1,0:T(2,128)(2,1)S(1)}, bf16[64,2,1536]{2,1,0:T(2,128)(2,1)}, u32[]{:S(2)}) copy-start(bf16[64,2,1536]{2,1,0:T(2,128)(2,1)} %get-tuple-element.61) | copy-start | bytes 1179652

commit v6 on v5

--- a/solution.py
+++ b/solution.py
@@ -1349,8 +1349,17 @@
     )(xg, oe, og, wd, ad_all, b_all, e, hid, n2, q, o, p, win, wo, wq, x, n1, *small)
 
 
-def spread_kernel(oi, early, late, ain_o, aff_o, bqkv_o, bres_o, bff_o):
-    e = pl.program_id(0)
+def spread_kernel(oi, early_i, late_i, ain_o, aff_o, bqkv_o, bres_o, bff_o, early, late, loaded, sem):
+    step = pl.program_id(0)
+    e = lax.rem(step + 1, ADAPT)
+    copies = [pltpu.make_async_copy(early_i, early, sem.at[0]), pltpu.make_async_copy(late_i, late, sem.at[1])]
+
+    @pl.when(step == 0)
+    def _():
+        loaded[0] = 0
+        for c in copies:
+            c.start()
+
     for ref in (ain_o, aff_o, bqkv_o, bres_o, bff_o):
         ref[...] = jnp.zeros_like(ref)
 
@@ -1361,6 +1370,16 @@
     def ff_tile(piece, n):
         k, j = n // 8, n % 8
         return early[k // 4, k % 4, piece // 4, (piece // 2) % 2, piece % 2, j].astype(F32)
+
+    used = step == ADAPT - 1
+    for s in range(4):
+        used = used | (oi[s, 0, 0, 0] == e)
+
+    @pl.when(used & (loaded[0] == 0))
+    def _():
+        loaded[0] = 1
+        for c in copies:
+            c.wait()
 
     for s in range(4):
 
@@ -1397,18 +1416,20 @@
     )
 
     def one(shape):
-        return pl.BlockSpec((1,) + shape[1:], lambda i: (i,) + (0,) * (len(shape) - 1))
+        return pl.BlockSpec((1,) + shape[1:], lambda i: (lax.rem(i + 1, ADAPT),) + (0,) * (len(shape) - 1))
 
     return pl.pallas_call(
         spread_kernel,
         out_shape=outs,
         grid=(ADAPT,),
-        in_specs=[
-            SM,
-            pl.BlockSpec(early.shape, lambda i: (0,) * 8),
-            pl.BlockSpec(late.shape, lambda i: (0,) * 8),
+        in_specs=[SM, ANY, ANY],
+        out_specs=[one(o.shape) for o in outs],
+        scratch_shapes=[
+            pltpu.VMEM(early.shape, BF),
+            pltpu.VMEM(late.shape, BF),
+            pltpu.SMEM((1,), jnp.int32),
+            DMA((2,)),
         ],
-        out_specs=[one(o.shape) for o in outs],
         compiler_params=pltpu.CompilerParams(vmem_limit_bytes=VMEM_LIMIT),
     )(oi, early, late)
 

time: 305 us -> 306 us (level)
  no operation moved by 1% of the time
where the time goes in v6:
time: 306 us; the launch traced here: 301 us
  Pallas kernels  296 us (97%)
    pallas_call x1, Pallas kernels, front(): pl.pallas_call(front_kernel, out_shape=outs, in_specs=[SM] * 3 + [VM] * 6...  143 us
    pallas_call x1, Pallas kernels, rear(): pl.pallas_call(rear_kernel, out_shape=outs, in_specs=[ANY] * 25 + [VM] *...  141 us
    pallas_call x1, Pallas kernels, spread(): pl.pallas_call(spread_kernel, out_shape=outs, grid=(ADAPT,), in_specs=[SM...  12.2 us

profile of v6, /device:TPU:1, one launch (start us, length us, event | category | flops | bytes accessed | tf_op | source)
XLA Modules:
  0.0 301.3 jit_solution(1559268594485713218)
XLA Ops:
  1.9 0.1 pad_add_fusion
  2.0 0.1 add_convert_fusion
  2.1 0.1 convert_element_type.11
  2.2 0.3 fusion
  2.5 0.8 pad_maximum_fusion
  3.3 142.8 %shard_map.216 = (bf16[2,2,4,2,48,2048]{5,4,3,2,1,0:T(8,128)(2,1)}, bf16[2,2,4,2,48,1536]{5,4,3,2,1,0:T(8,128)(2,1)}, bf16[4,2,2,4,2,48,640]{6,5,4,3,2,1,0:T(8,1...) custom-call(s32[1]{0:T(128)S(6)} %copy.26.idx_i, ...), custom_call_target="tpu_custom_call" | custom-call | tf_op jit(solution)/shard_map/pallas_call | solution.py:751
  146.1 141.3 %shard_map.217 = (bf16[64,2,1536]{2,1,0:T(2,128)(2,1)}, bf16[64,2,1536]{2,1,0:T(2,128)(2,1)}, bf16[4,4,2,2,2,10,16,128]{7,6,5,4,3,2,1,0:T(8,128)(2,1)}, bf16[4,4,2,2,2,2,16,128]{7,6,5,4,3,2,1,0:T(8,128)(2,1)}) custom-call(bf16[2,2,2,128,1664]{4,3,2,1,0:T(8,128)(2,1)} %get-tuple-element.38.xg, bf16[2,2,2,128,1664]{4,3,2,1,0:T(8,128)(2,1)} %get-tuple-element.39.oe, ...), custom_call_target="tpu_custom_call" | custom-call | tf_op jit(solution)/shard_map/pallas_call | solution.py:1342
  287.3 0.0 copy-start.1
  287.3 0.0 copy-start
  287.4 12.2 %shard_map.218 = (f32[8,6,16,1536]{3,2,1,0:T(8,128)}, f32[8,16,8960]{2,1,0:T(8,128)}, f32[8,16,2048]{2,1,0:T(8,128)}, f32[8,2,16,1536]{3,2,1,0:T(8,128)}, f32[8,2,16,8960]{3,2,1,0:T(8,128)}) custom-call(s32[4,2,8,128]{3,2,1,0:T(8,128)} %get-tuple-element.59.oi, bf16[4,4,2,2,2,10,16,128]{7,6,5,4,3,2,1,0:T(8,128)(2,1)} %get-tuple-element.62.early_i, ...), custom_call_target="tpu_custom_call" | custom-call | tf_op jit(solution)/shard_map/pallas_call | solution.py:1421
  299.6 0.0 copy-done.1
  299.6 0.7 copy.28
  300.3 0.0 copy-done
  300.3 0.7 copy.29
  (1 shorter events, 0.0 us)
Async XLA Ops:
  287.3 12.3 %copy-start.1 = (bf16[64,2,1536]{2,1,0:T(2,128)(2,1)S(1)}, bf16[64,2,1536]{2,1,0:T(2,128)(2,1)}, u32[]{:S(2)}) copy-start(bf16[64,2,1536]{2,1,0:T(2,128)(2,1)} %get-tuple-element.60) | copy-start | bytes 1179652
  287.3 13.0 %copy-start = (bf16[64,2,1536]{2,1,0:T(2,128)(2,1)S(1)}, bf16[64,2,1536]{2,1,0:T(2,128)(2,1)}, u32[]{:S(2)}) copy-start(bf16[64,2,1536]{2,1,0:T(2,128)(2,1)} %get-tuple-element.61) | copy-start | bytes 1179652
